TPU v7x, 32 devices: a whole 2x2x4 slice. The times are simulated.
32 devices in a mesh: ingest: 16 (over z, y, x), span: 2 (over core).
Axes of the slice: x: 2, y: 2, z: 4, core: 2. Of those that a mesh axis runs over, the one named last changes fastest.
Arguments:
- embeddings: bfloat16 [16384, 768], P(('ingest', 'span')), may hold values from -100 to 100
- cluster_id: int32 [16384], P(('ingest', 'span')), may hold values from 0 to 15, as said below
- rank: int32 [16384], P(('ingest', 'span')), may hold values from 0 to 16383, each once
Outputs:
- max_cosine: float32 [16384], P(('ingest', 'span'))
Inputs may be any that keep to these rules, and one draw needn't show every extreme that they name: `cluster_id`: the 512 embeddings of each device name one cluster at most 64 times, and some cluster exactly 64 times. `rank`: every value once.
All inputs are finite; a program needn't handle non-finite values.
Results may differ from a plain program's by a relative error of at most 0.00054.
Values may be sent and summed in bfloat16 or wider, within the bound.
No kernel may reach another device: no remote copies, remote signals or barrier semaphores. Data moves between devices by JAX's collectives and lax.ppermute only.
A program may use at most 64 MiB of HBM per device.

v0:
```python
import jax
import jax.numpy as jnp
from jax import lax
from jax.sharding import PartitionSpec as P

beyond_rank = 2**30


def normalize(embeddings):
    widened = embeddings.astype(jnp.float32)
    return (widened * lax.rsqrt(jnp.sum(widened * widened, axis=1, keepdims=True) + 1e-06)).astype(
        jnp.bfloat16
    )


def tile_maxima(queries, query_rank, candidates, candidate_rank):
    scores = jnp.einsum("qd,kd->qk", queries, candidates, preferred_element_type=jnp.float32)
    earlier = candidate_rank[None, :] < query_rank[:, None]
    return jnp.max(jnp.where(earlier, scores, -1.0), axis=1)


def blocked_rows(queries, query_rank, candidates, candidate_rank):
    total = queries.shape[0]
    height = min(512, total)
    grouped = queries.reshape(total // height, height, queries.shape[1])
    rank_groups = query_rank.reshape(total // height, height)
    maxima = lax.map(
        lambda grouping: tile_maxima(grouping[0], grouping[1], candidates, candidate_rank),
        (grouped, rank_groups),
    )
    return maxima.reshape(total)


def body(embeddings, cluster_id, rank):
    nodes = lax.axis_size("ingest")
    rows = embeddings.shape[0]
    width = embeddings.shape[1]
    capacity = 2 * rows // nodes
    slots = nodes * capacity
    normed = normalize(embeddings)
    owner_table = (cluster_id[:, None] == jnp.arange(nodes, dtype=jnp.int32)[None, :]).astype(
        jnp.int32
    )
    before = jnp.cumsum(owner_table, axis=0) - owner_table
    position = jnp.sum(before * owner_table, axis=1)
    target = cluster_id * capacity + position
    outgoing = (
        jnp.zeros((slots, width), jnp.bfloat16)
        .at[target]
        .set(normed)
        .reshape(nodes, capacity, width)
    )
    outgoing_rank = (
        jnp.full((slots,), beyond_rank, jnp.int32).at[target].set(rank).reshape(nodes, capacity)
    )
    arrived, arrived_rank = (
        lax.all_to_all(outgoing, "ingest", split_axis=0, concat_axis=0, tiled=True),
        lax.all_to_all(outgoing_rank, "ingest", split_axis=0, concat_axis=0, tiled=True),
    )
    arrived = arrived.reshape(slots, width)
    arrived_rank = arrived_rank.reshape(slots)
    highest = jnp.maximum(
        jnp.full((slots,), -1.0, jnp.float32),
        blocked_rows(
            arrived,
            arrived_rank,
            lax.all_gather(arrived, "span", axis=0, tiled=True),
            lax.all_gather(arrived_rank, "span", axis=0, tiled=True),
        ),
    )
    returned = lax.all_to_all(
        highest.reshape(nodes, capacity), "ingest", split_axis=0, concat_axis=0, tiled=True
    )
    return returned.reshape(slots)[target]


def solution(mesh):
    in_specs = (P(("ingest", "span"), None), P(("ingest", "span")), P(("ingest", "span")))
    out_specs = P(("ingest", "span"))
    return jax.shard_map(body, mesh=mesh, in_specs=in_specs, out_specs=out_specs, check_vma=False)
```

profile of v0, /device:TPU:0, one launch (start us, length us, event | category | flops | bytes accessed | tf_op | source)
XLA Modules:
  0.0 109.3 jit_solution(4533937896206467782)
XLA Ops:
  6.5 0.7 fusion.12
  7.2 1.1 %reduce-window.6 = s32[16,4,128]{2,0,1:T(8,128)S(1)} reduce-window(s32[16,4,128]{2,0,1:T(8,128)S(1)} %fusion.12, s32[]{:T(128)} %constant.8.clone.1), window={size=1x1x128 pad=0_0x0_0x127_0}, to_apply=%region_0.0 | reduce-window | flops 1040384 | bytes 65540 | tf_op jit(solution)/shard_map/reduce-window
  8.4 0.2 slice_reduce_fusion
  8.6 0.8 fusion.11
  9.4 0.7 compare_select_fusion
  10.1 1.4 %fusion.3 = f32[512]{0:T(512)S(1)} fusion(bf16[512,768]{1,0:T(8,128)(2,1)} %param.5), kind=kLoop, calls=%fused_computation.10 | loop fusion | flops 1179136 | bytes 788480 | tf_op jit(solution)/shard_map/reduce_sum | solution.py:11
  11.5 3.7 %scatter_custom_fusion.1 = bf16[1024,768]{1,0:T(8,128)(2,1)S(1)} fusion(s32[512]{0:T(512)S(1)} %compare_select_fusion, bf16[512,768]{1,0:T(8,128)(2,1)} %param.5, f32[512]{0:T(512)S(1)} %add_rsqrt_fusion, bf16[]{:T(256)} %constant.9.clone.1), kind=kCustom, calls=%fused_computation.12 | custom fusion | flops 1179648 | bytes 2361346 | tf_op jit(solution)/shard_map/scatter | solution.py:50
  15.1 45.8 %all_to_all.20 = bf16[16,64,768]{2,1,0:T(8,128)(2,1)} all-to-all(bf16[16,64,768]{2,1,0:T(8,128)(2,1)S(1)} %bitcast.40), channel_id=1, replica_groups=mesh['ingest'=16,'span'=2] {'ingest'}, dimensions={0} | all-to-all | bytes 3145728 | tf_op jit(solution)/shard_map/all_to_all | solution.py:57
  61.0 2.7 %scatter_custom_fusion = s32[1024]{0:T(1024)S(1)} fusion(s32[512]{0:T(512)S(1)} %compare_select_fusion, s32[512]{0:T(512)} %param.7, s32[]{:T(128)} %constant.24.clone.1), kind=kCustom, calls=%fused_computation.28 | custom fusion | bytes 4608 | tf_op jit(solution)/shard_map/scatter | solution.py:54
  63.7 0.7 all_to_all.13
  64.4 3.9 %all-to-all-start = ((s32[16,1,64]{2,1,0:T(1,128)}), s32[16,1,64]{2,1,0:T(1,128)S(1)}, u32[]{:S(2)}, u32[]{:S(2)}) async-start(s32[16,1,64]{2,1,0:T(1,128)} %all_to_all.13), calls=%async_computation | async-start | bytes 16384 | tf_op jit(solution)/shard_map/all_to_all | solution.py:58
  68.3 7.3 %all-to-all-done = s32[16,1,64]{2,1,0:T(1,128)S(1)} async-done(((s32[16,1,64]{2,1,0:T(1,128)}), s32[16,1,64]{2,1,0:T(1,128)S(1)}, u32[]{:S(2)}, u32[]{:S(2)}) %all-to-all-start) | async-done | bytes 4128 | tf_op jit(solution)/shard_map/all_to_all | solution.py:58
  75.6 0.5 broadcast.58
  76.1 0.6 reduce.10
  76.8 1.8 %all_gather.6 = s32[2048]{0:T(1024)S(1)} all-gather(s32[1024]{0:T(1024)S(1)} %reshape.62), channel_id=1, replica_groups=mesh['ingest'=16,'span'=2] {'span'}, dimensions={0}, use_global_device_ids=true | all-gather | bytes 12288 | tf_op jit(solution)/shard_map/all_gather | solution.py:68
  78.6 7.8 %while.10 = (s32[]{:T(128)}, f32[2,512]{1,0:T(2,128)S(1)}, s32[2048]{0:T(1024)S(1)}, s32[2,512]{1,0:T(2,128)S(1)}, bf16[2,512,768]{2,1,0:T(8,128)(2,1)S(1)}, /*i...) while((s32[]{:T(128)}, f32[2,512]{1,0:T(2,128)S(1)}, s32[2048]{0:T(1024)S(1)}, s32[2,512]{1,0:T(2,128)S(1)}, ...), condition=%wide.region_8.9_spmd, body=%wide.region_6.8_spmd.sunk | while | flops 1613757952 | bytes 3952745 | solution.py:27
  78.6 3.8 %select_reduce_fusion.2 = f32[512]{0:T(512)S(1)} fusion(bf16[2048,768]{1,0:T(8,128)(2,1)} %get-tuple-element.108, s32[2048]{0:T(1024)S(1)} %get-tuple-element.105, s32[512]{0:T(512)S(1)} %bitcast.43, bf16[2,512,768]{2,1,0:T(8,128)(2,1)S(1)} %get-tuple-element.107, s32[]{:T(128)S(6)} %copy.11), kind=kOutput, calls=%fused_computation.3.clone.1 | convolution fusion | flops 1613757952 | bytes 3944452 | tf_op jit(solution)/shard_map/while/body/eval_jaxpr/qd,kd->qk/dot_general | solution.py:17
  82.5 3.8 %select_reduce_fusion.2 = f32[512]{0:T(512)S(1)} fusion(bf16[2048,768]{1,0:T(8,128)(2,1)} %get-tuple-element.108, s32[2048]{0:T(1024)S(1)} %get-tuple-element.105, s32[512]{0:T(512)S(1)} %bitcast.43, bf16[2,512,768]{2,1,0:T(8,128)(2,1)S(1)} %get-tuple-element.107, s32[]{:T(128)S(6)} %copy.11), kind=kOutput, calls=%fused_computation.3.clone.1 | convolution fusion | flops 1613757952 | bytes 3944452 | tf_op jit(solution)/shard_map/while/body/eval_jaxpr/qd,kd->qk/dot_general | solution.py:17
  86.4 0.7 max_broadcast_in_dim.15
  87.1 3.5 %all-to-all-start.2 = ((f32[16,1,64]{2,1,0:T(1,128)}), f32[16,1,64]{2,1,0:T(1,128)S(1)}, u32[]{:S(2)}, u32[]{:S(2)}) async-start(f32[16,1,64]{2,1,0:T(1,128)} %max_broadcast_in_dim.15), calls=%async_computation.2 | async-start | bytes 16384 | tf_op jit(solution)/shard_map/all_to_all | solution.py:71
  90.6 7.2 %all-to-all-done.2 = f32[16,1,64]{2,1,0:T(1,128)S(1)} async-done(((f32[16,1,64]{2,1,0:T(1,128)}), f32[16,1,64]{2,1,0:T(1,128)S(1)}, u32[]{:S(2)}, u32[]{:S(2)}) %all-to-all-start.2) | async-done | bytes 4128 | tf_op jit(solution)/shard_map/all_to_all | solution.py:71
  97.8 0.5 broadcast.59
  98.3 0.7 reduce.11
  99.1 3.4 %gather_fusion = f32[512]{0:T(512)} fusion(f32[1024]{0:T(1024)S(1)} %reshape.65, s32[1024]{0:T(1024)S(1)} %pad_clamp_fusion), kind=kCustom, calls=%fused_computation | custom fusion | bytes 6144 | tf_op jit(solution)/shard_map/gather | solution.py:74
  (18 shorter events, 0.4 us)
Async XLA Ops:
  6.5 72.0 %all-gather.2.cloned.1.call-start = ((), (), s32[]{:S(2)}) async-start(), calls=%async_computation.3 | async-start | bytes 4718592 | tf_op jit(solution)/shard_map/all_gather | solution.py:67
  61.0 17.6 %copy-start = (bf16[16,64,768]{2,1,0:T(8,128)(2,1)S(1)}, bf16[16,64,768]{2,1,0:T(8,128)(2,1)}, u32[]{:S(2)}) copy-start(bf16[16,64,768]{2,1,0:T(8,128)(2,1)} %all_to_all.20) | copy-start | bytes 4718596
  64.4 11.2 %all-to-all-start = ((s32[16,1,64]{2,1,0:T(1,128)}), s32[16,1,64]{2,1,0:T(1,128)S(1)}, u32[]{:S(2)}, u32[]{:S(2)}) async-start(s32[16,1,64]{2,1,0:T(1,128)} %all_to_all.13), calls=%async_computation | async-start | bytes 16384 | tf_op jit(solution)/shard_map/all_to_all | solution.py:58
  87.1 10.7 %all-to-all-start.2 = ((f32[16,1,64]{2,1,0:T(1,128)}), f32[16,1,64]{2,1,0:T(1,128)S(1)}, u32[]{:S(2)}, u32[]{:S(2)}) async-start(f32[16,1,64]{2,1,0:T(1,128)} %max_broadcast_in_dim.15), calls=%async_computation.2 | async-start | bytes 16384 | tf_op jit(solution)/shard_map/all_to_all | solution.py:71
Sparse Core Ops, SparseCore 0:
  61.1 10.3 all-gather.1
where the time goes:
time: 110 us; the launch traced here: 109 us
  blocking collectives  47.6 us (43%)
  waiting for transfers between devices  14.5 us (13%)
  between operations  13.5 us (12%)
  other arithmetic  9.62 us (9%)
  local copies, waits for them, and re-layouts  9.03 us (8%)
  matrix products  7.64 us (7%)
  starting transfers between devices  7.39 us (7%)
    all_to_all x1, blocking collectives, body(): lax.all_to_all(outgoing, 'ingest', split_axis=0, concat_axis=0, tiled=True)  45.8 us
    dot_general x2, matrix products, tile_maxima(): jnp.einsum('qd,kd->qk', queries, candidates, preferred_element_type=jnp.f...  7.64 us
    all_to_all x1, waiting for transfers between devices, body(): lax.all_to_all(outgoing_rank, 'ingest', split_axis=0, concat_axis=0, tile...  7.26 us
    all_to_all x1, waiting for transfers between devices, body(): lax.all_to_all(highest.reshape(nodes, capacity), 'ingest', split_axis=0,...  7.22 us
    all_to_all x1, starting transfers between devices, body(): lax.all_to_all(outgoing_rank, 'ingest', split_axis=0, concat_axis=0, tile...  3.89 us
    scatter x1, other arithmetic, body(): outgoing = jnp.zeros((slots, width), jnp.bfloat16).at[target].set(normed)...  3.67 us
    all_to_all x1, starting transfers between devices, body(): lax.all_to_all(highest.reshape(nodes, capacity), 'ingest', split_axis=0,...  3.49 us
    gather x1, local copies, waits for them, and re-layouts, body(): return returned.reshape(slots)[target]  3.41 us
  transfers between devices with their start and end apart: 3, of which 2 were waited for; matrix products, arithmetic and copies ran while one was open for 4% of the time, Pallas kernels for 0%

commit v1 on v0

v1 whole, which is shorter than its diff:
```python
import functools

import jax
import jax.numpy as jnp
from jax import lax
from jax.experimental import pallas as pl
from jax.experimental.pallas import tpu as pltpu
from jax.sharding import PartitionSpec as P

LANES = 128
EXTRA = 8
NEVER = 2.0**24
TILE = 512
PARAMS = pltpu.CompilerParams(vmem_limit_bytes=40 * 2**20)
VMEM = pl.BlockSpec(memory_space=pltpu.VMEM)
SMEM = pl.BlockSpec(memory_space=pltpu.SMEM)
ANY = pl.BlockSpec(memory_space=pl.ANY)


LIGHT = pl.CostEstimate(flops=1, bytes_accessed=1, transcendentals=0)


def membership(cid, nodes, rows):
    return lax.broadcasted_iota(jnp.int32, (nodes, rows), 0) == cid


def partners(nodes):
    half = nodes // 2
    far = [half, nodes - 1, *range(half + half // 2, nodes - 1), *range(half + 1, half + half // 2)]
    near = [1, *range(half // 2, half), *range(2, half // 2)]
    sequence = [far[0]]
    for pair in zip(near, far[1:]):
        sequence.extend(pair)
    flips = [0] * nodes
    for g, flip in zip([*range(half + 3, nodes), *range(half, half + 3), *range(1, half)], sequence):
        flips[g] = flip
    return flips


def place_kernel(me_ref, cid_ref, rank_ref, pos_ref, target_ref, digits_ref, *, flips, capacity):
    nodes = len(flips)
    rows = cid_ref.shape[1]
    flip = cid_ref[...] ^ me_ref[0]
    slot = jnp.zeros_like(flip)
    for g, value in enumerate(flips):
        slot = jnp.where(flip == value, g, slot)
    chunks = [slice(i, i + LANES) for i in range(0, rows, LANES)]
    members = [membership(slot[:, at], nodes, LANES) for at in chunks]
    ahead = lax.broadcasted_iota(jnp.int32, (LANES, LANES), 0) < lax.broadcasted_iota(
        jnp.int32, (LANES, LANES), 1
    )
    ones = [member.astype(jnp.float32) for member in members]
    within = jnp.dot(
        jnp.concatenate(ones, axis=0).astype(jnp.bfloat16),
        ahead.astype(jnp.float32).astype(jnp.bfloat16),
        preferred_element_type=jnp.float32,
    )
    before = jnp.zeros((nodes, 1), jnp.float32)
    for i, at in enumerate(chunks):
        counts = within[i * nodes : (i + 1) * nodes, :] + before
        pos = jnp.sum(jnp.where(members[i], counts, 0.0), axis=0, keepdims=True).astype(jnp.int32)
        pos_ref[:, at] = pos
        target_ref[:, at] = slot[:, at] * capacity + pos
        before = before + jnp.sum(ones[i], axis=1, keepdims=True)
        shown = rank_ref[:, at] + 1
        digit = lax.broadcasted_iota(jnp.int32, (LANES, LANES), 0)
        digits = jnp.where(
            digit == 0,
            shown & 127,
            jnp.where(digit == 1, (shown >> 7) & 127, jnp.where(digit == 2, (shown >> 14) & 127, 0)),
        ).astype(jnp.float32)
        digits_ref[at, :] = jnp.transpose(digits).astype(jnp.bfloat16)


def pack_kernel(x_ref, target_ref, digits_ref, *out_refs, capacity):
    nodes = len(out_refs)
    rows, width = x_ref.shape
    pieces = width // LANES
    slots = nodes * capacity
    place = lax.broadcasted_iota(jnp.int32, (slots, rows), 0) == target_ref[...]
    place = place.astype(jnp.float32).astype(jnp.bfloat16)
    widened = x_ref[...].astype(jnp.float32)
    squares = jnp.sum(widened * widened, axis=1, keepdims=True)
    normed = (widened * lax.rsqrt(squares + 1e-06)).astype(jnp.bfloat16)
    whole = jnp.concatenate([normed, digits_ref[...]], axis=1)
    moved = jnp.dot(place, whole, preferred_element_type=jnp.float32)
    for first in range(0, slots, LANES):
        lines = jnp.transpose(moved[first : first + LANES, width:])[0:EXTRA, :].astype(jnp.bfloat16)
        for g in range(first // capacity, (first + LANES) // capacity):
            at = g * capacity
            for p in range(pieces):
                out_refs[g][p * capacity : (p + 1) * capacity, :] = moved[
                    at : at + capacity, p * LANES : (p + 1) * LANES
                ].astype(jnp.bfloat16)
            out_refs[g][pieces * capacity :, :] = jnp.zeros((EXTRA, LANES), jnp.bfloat16)
            out_refs[g][pieces * capacity :, 0:capacity] = lines[:, at - first : at - first + capacity]


def assemble_kernel(*refs, messages, capacity, pieces):
    sources, (rows_ref, line_ref) = refs[:messages], refs[-2:]
    if len(sources[0].shape) == 3:
        sources = [sources[0].at[i] for i in range(sources[0].shape[0])]
    for i, source in enumerate(sources):
        for p in range(pieces):
            rows_ref[i * capacity : (i + 1) * capacity, p * LANES : (p + 1) * LANES] = source[
                p * capacity : (p + 1) * capacity, :
            ]
        tile = source[pieces * capacity :, :].astype(jnp.float32)
        square = jnp.concatenate([tile, jnp.zeros((LANES - EXTRA, LANES), jnp.float32)], axis=0)
        rows_ref[i * capacity : (i + 1) * capacity, pieces * LANES :] = jnp.transpose(square)[
            0:capacity, :
        ].astype(jnp.bfloat16)
        line = tile[0:1, :] + 128.0 * tile[1:2, :] + 16384.0 * tile[2:3, :]
        line_ref[0:1, i * capacity : (i + 1) * capacity] = line[:, 0:capacity]


def assemble(messages, count, after, held, width):
    pieces = width // LANES
    capacity = (messages[0].shape[-2] - EXTRA) // pieces
    rows = count * capacity
    ahead = len(messages) + len(after)
    return pl.pallas_call(
        functools.partial(assemble_kernel, messages=len(messages), capacity=capacity, pieces=pieces),
        out_shape=[jax.ShapeDtypeStruct(h.shape, h.dtype) for h in held]
        + [
            jax.ShapeDtypeStruct((rows, width + LANES), jnp.bfloat16),
            jax.ShapeDtypeStruct((8, rows), jnp.float32),
        ],
        in_specs=[VMEM] * len(messages) + [ANY] * (len(after) + len(held)),
        out_specs=[ANY] * len(held) + [VMEM, VMEM],
        input_output_aliases={ahead + i: i for i in range(len(held))},
        compiler_params=PARAMS,
        cost_estimate=LIGHT,
    )(*messages, *after, *held)


def match_kernel(*refs, width, queries, candidates, pairs, mirrored, carried):
    q_refs, refs = refs[:queries], refs[queries:]
    line_refs, refs = refs[:queries], refs[queries:]
    k_refs, refs = refs[:candidates], refs[candidates:]
    carry_refs, out_refs = dict(zip(carried, refs)), refs[len(carried) :]
    best = {}
    for q in range(queries):
        rows = q_refs[q].shape[0]
        best[q] = carry_refs[q][0:1, :] if q in carry_refs else jnp.full((1, rows), -1.0, jnp.float32)
    for k in range(candidates):
        for first in range(0, k_refs[k].shape[0], TILE):
            at = slice(first, min(first + TILE, k_refs[k].shape[0]))
            tile = k_refs[k][at, width:].astype(jnp.float32)
            theirs = tile[:, 0:1] + 128.0 * tile[:, 1:2] + 16384.0 * tile[:, 2:3]
            other = jnp.where(theirs > 0.0, theirs, NEVER)
            for q in range(queries):
                if (q, k) not in pairs:
                    continue
                scores = lax.dot_general(
                    k_refs[k][at, 0:width],
                    q_refs[q][:, 0:width],
                    (((1,), (1,)), ((), ())),
                    preferred_element_type=jnp.float32,
                )
                kept = jnp.where(other < line_refs[q][0:1, :], scores, -1.0)
                best[q] = jnp.maximum(best[q], jnp.max(kept, axis=0, keepdims=True))
                if (q, k) in mirrored:
                    asked = mirrored[q, k]
                    line = line_refs[q][0:1, :]
                    line = jnp.where(line > 0.0, line, NEVER)
                    kept = jnp.where(line < theirs, scores, -1.0)
                    folded = kept[:, 0:LANES]
                    for lane in range(LANES, kept.shape[1], LANES):
                        folded = jnp.maximum(folded, kept[:, lane : lane + LANES])
                    found = jnp.max(jnp.transpose(folded), axis=0, keepdims=True)
                    best[asked] = jnp.maximum(best[asked], found)
    for q in range(queries):
        out_refs[q][0:1, :] = best[q]


def match(groups, candidates, pairs, carry, width, mirrored=None):
    carried = tuple(sorted(carry))
    operands = [
        *[rows for rows, _ in groups],
        *[line for _, line in groups],
        *candidates,
        *[carry[q] for q in carried],
    ]
    return pl.pallas_call(
        functools.partial(
            match_kernel,
            width=width,
            queries=len(groups),
            candidates=len(candidates),
            pairs=frozenset(pairs),
            mirrored=mirrored or {},
            carried=carried,
        ),
        out_shape=[jax.ShapeDtypeStruct(line.shape, jnp.float32) for _, line in groups],
        in_specs=[VMEM] * len(operands),
        out_specs=[VMEM] * len(groups),
        compiler_params=PARAMS,
        cost_estimate=LIGHT,
    )(*operands)


def address_kernel(me_ref, *refs, flips, capacity):
    *lines, out_ref = refs
    out_ref[...] = jnp.zeros(out_ref.shape, jnp.float32)
    blocks = [(line, i) for line in lines for i in range(line.shape[1] // capacity)]
    for flip, (line, i) in zip(flips, blocks):
        out_ref[(out_ref.shape[0] - 1) - (me_ref[0] ^ flip), 0:1, 0:capacity] = line[0:1, i * capacity : (i + 1) * capacity]


def unpack_kernel(back_ref, cid_ref, pos_ref, out_ref):
    nodes = back_ref.shape[0]
    lines = jnp.concatenate([back_ref[g] for g in range(nodes)], axis=0)
    for first in range(0, cid_ref.shape[1], LANES):
        at = slice(first, first + LANES)
        index = jnp.broadcast_to(pos_ref[:, at], (nodes, LANES))
        found = jnp.take_along_axis(lines, index, axis=1, mode="promise_in_bounds")
        member = membership((nodes - 1) - cid_ref[:, at], nodes, LANES)
        out_ref[:, at] = jnp.sum(jnp.where(member, found, 0.0), axis=0, keepdims=True)


def body(embeddings, cluster_id, rank):
    nodes = lax.axis_size("ingest")
    rows, width = embeddings.shape
    capacity = 2 * rows // nodes
    height = capacity * (width // LANES) + EXTRA
    cid = cluster_id.reshape(1, rows)
    half = nodes // 2
    me = lax.axis_index("ingest").astype(jnp.int32).reshape(1)
    flips = partners(nodes)
    pos, target, digits = pl.pallas_call(
        functools.partial(place_kernel, flips=flips, capacity=capacity),
        out_shape=(
            jax.ShapeDtypeStruct((1, rows), jnp.int32),
            jax.ShapeDtypeStruct((1, rows), jnp.int32),
            jax.ShapeDtypeStruct((rows, LANES), jnp.bfloat16),
        ),
        in_specs=[SMEM] + [VMEM] * 2,
        out_specs=[VMEM] * 3,
        compiler_params=PARAMS,
        cost_estimate=pl.CostEstimate(flops=2**28, bytes_accessed=2**12, transcendentals=0),
    )(me, cid, rank.reshape(1, rows))
    messages = pl.pallas_call(
        functools.partial(pack_kernel, capacity=capacity),
        out_shape=[jax.ShapeDtypeStruct((height, LANES), jnp.bfloat16)] * nodes,
        in_specs=[VMEM] * 3,
        out_specs=[VMEM] * nodes,
        compiler_params=PARAMS,
        cost_estimate=pl.CostEstimate(
            flops=2 * nodes * capacity * rows * (width + LANES), bytes_accessed=2**12, transcendentals=0
        ),
    )(embeddings, target, digits)
    messages = list(messages)
    for g in range(1, nodes):
        messages[g] = lax.ppermute(messages[g], "ingest", [(i, i ^ flips[g]) for i in range(nodes)])

    def across(rows):
        return lax.ppermute(rows, "span", [(0, 1), (1, 0)])

    b, b_line = assemble(messages[half:], half, [], [], width)
    (best_b,) = match([(b, b_line)], [b], [(0, 0)], {}, width)
    a, a_line = assemble(messages[:half], half, [best_b], [], width)
    groups = [(a, a_line), (b, b_line)]
    best_a, best_b = match(
        groups, [b, a], [(0, 1), (0, 0)], {1: best_b}, width, mirrored={(0, 0): 1}
    )
    for other in (across(b), across(a)):
        best_a, best_b = match(groups, [other], [(0, 0), (1, 0)], {0: best_a, 1: best_b}, width)
    highest = pl.pallas_call(
        functools.partial(address_kernel, flips=flips, capacity=capacity),
        out_shape=jax.ShapeDtypeStruct((nodes, 1, LANES), jnp.float32),
        in_specs=[SMEM] + [VMEM] * 2,
        out_specs=VMEM,
        compiler_params=PARAMS,
    )(me, best_a, best_b)
    back = lax.all_to_all(
        highest,
        "ingest",
        split_axis=0,
        concat_axis=0,
        tiled=True,
        axis_index_groups=[list(range(nodes))[::-1]],
    )
    result = pl.pallas_call(
        unpack_kernel,
        out_shape=jax.ShapeDtypeStruct((1, rows), jnp.float32),
        in_specs=[VMEM] * 3,
        out_specs=VMEM,
        compiler_params=PARAMS,
    )(back, cid, pos)
    return result.reshape(rows)


def solution(mesh):
    in_specs = (P(("ingest", "span"), None), P(("ingest", "span")), P(("ingest", "span")))
    out_specs = P(("ingest", "span"))
    return jax.shard_map(body, mesh=mesh, in_specs=in_specs, out_specs=out_specs, check_vma=False)
```

time: 110 us -> 58.3 us (0.53)
  blocking collectives: 47.6 us -> 9.6 us
  starting transfers between devices: 7.39 us -> 30.7 us
  between operations: 13.5 us -> 0.07 us
  other arithmetic: 9.62 us -> 0 us
  local copies, waits for them, and re-layouts: 9.03 us -> 1 us
  matrix products: 7.64 us -> 0 us
  Pallas kernels: 0 us -> 6.6 us
  waiting for transfers between devices: 14.5 us -> 10.1 us
    all_to_all x1, blocking collectives: 45.8 us -> 9.6 us  [body(): lax.all_to_all(highest, 'ingest', split_axis=0, concat_axis=0, tiled=True...]
    ppermute x0 -> x17, starting transfers between devices: none -> 30.7 us  [the longest x15 30.6 us: body(): lax.ppermute(messages[g], 'ingest', [(i, i ^ flips[g]) for i in range(nod...]
    all_to_all x2 -> x0, waiting for transfers between devices: 14.5 us -> none  [the longest x1 7.26 us: body(): lax.all_to_all(outgoing_rank, 'ingest', split_axis=0, concat_axis=0, tile...]
    ppermute x0 -> x17, waiting for transfers between devices: none -> 10.1 us  [the longest x15 9.79 us: body(): lax.ppermute(messages[g], 'ingest', [(i, i ^ flips[g]) for i in range(nod...]
    dot_general x2 -> x0, matrix products: 7.64 us -> none  [tile_maxima(): jnp.einsum('qd,kd->qk', queries, candidates, preferred_element_type=jnp.f...]
    all_to_all x2 -> x0, starting transfers between devices: 7.39 us -> none  [the longest x1 3.89 us: body(): lax.all_to_all(outgoing_rank, 'ingest', split_axis=0, concat_axis=0, tile...]
    pallas_call x0 -> x10, Pallas kernels: none -> 6.6 us  [the longest x4 3.74 us: match(): pl.pallas_call(functools.partial(match_kernel, width=width, queries=len(g...]
    scatter x1 -> x0, other arithmetic: 3.67 us -> none  [body(): outgoing = jnp.zeros((slots, width), jnp.bfloat16).at[target].set(normed)...]
  transfers between devices with their start and end apart: 3 -> 17, of which waited for: 2 -> 6; matrix products, arithmetic and copies ran while one was open for 4% -> 0% of each run, Pallas kernels for 0% -> 5%
where the time goes in v1:
time: 58.3 us; the launch traced here: 58.1 us
  starting transfers between devices  30.7 us (53%)
  waiting for transfers between devices  10.1 us (17%)
  blocking collectives  9.6 us (16%)
  Pallas kernels  6.6 us (11%)
  local copies, waits for them, and re-layouts  1 us (2%)
    ppermute x15, starting transfers between devices, body(): lax.ppermute(messages[g], 'ingest', [(i, i ^ flips[g]) for i in range(nod...  30.6 us
    ppermute x15, waiting for transfers between devices, body(): lax.ppermute(messages[g], 'ingest', [(i, i ^ flips[g]) for i in range(nod...  9.79 us
    all_to_all x1, blocking collectives, body(): lax.all_to_all(highest, 'ingest', split_axis=0, concat_axis=0, tiled=True...  9.6 us
    pallas_call x4, Pallas kernels, match(): pl.pallas_call(functools.partial(match_kernel, width=width, queries=len(g...  3.74 us
    pallas_call x1, Pallas kernels, body(): pl.pallas_call(functools.partial(pack_kernel, capacity=capacity), out_sha...  1.51 us
  transfers between devices with their start and end apart: 17, of which 6 were waited for; matrix products, arithmetic and copies ran while one was open for 0% of the time, Pallas kernels for 5%

profile of v1, /device:TPU:0, one launch (start us, length us, event | category | flops | bytes accessed | tf_op | source)
XLA Modules:
  0.0 58.1 jit_solution(1418307757941538723)
XLA Ops:
  0.0 0.7 %copy-done.2 = s32[512]{0:T(512)S(1)} copy-done((s32[512]{0:T(512)S(1)}, s32[512]{0:T(512)}, u32[]{:S(2)}) %copy-start.2) | copy-done | bytes 2072
  1.2 1.5 %shard_map.38 = (bf16[392,128]{1,0:T(8,128)(2,1)S(1)}, bf16[392,128]{1,0:T(8,128)(2,1)S(1)}, bf16[392,128]{1,0:T(8,128)(2,1)S(1)}, bf16[392,128]{1,0:T(8,128)(2,...) custom-call(bf16[512,768]{1,0:T(8,128)(2,1)S(1)} %copy-done.1, ...), custom_call_target="tpu_custom_call" | custom-call | flops 939524096 | bytes 4096 | tf_op jit(solution)/shard_map/pallas_call | solution.py:243
  2.7 4.0 %collective-permute-start.10 = (bf16[392,128]{1,0:T(8,128)(2,1)S(1)}, bf16[392,128]{1,0:T(8,128)(2,1)S(1)}, u32[]{:S(2)}, u32[]{:S(2)}) collective-permute-start(bf16[392,128]{1,0:T(8,128)(2,1)S(1)} %get-tuple-element.47), channel_id=1, source_target_pairs={{0,16},{2,18},{4,20},{6,22},{8,24},{10,26},{12,28},{14,30},{16,0},... | collective-permute-start | bytes 301064 | tf_op jit(solution)/shard_map/ppermute | solution.py:255
  6.7 1.5 %collective-permute-start.11 = (bf16[392,128]{1,0:T(8,128)(2,1)S(1)}, bf16[392,128]{1,0:T(8,128)(2,1)S(1)}, u32[]{:S(2)}, u32[]{:S(2)}) collective-permute-start(bf16[392,128]{1,0:T(8,128)(2,1)S(1)} %get-tuple-element.48), channel_id=1, source_target_pairs={{0,2},{2,0},{4,6},{6,4},{8,10},{10,8},{12,14},{14,12},{16,18},{18,... | collective-permute-start | bytes 301064 | tf_op jit(solution)/shard_map/ppermute | solution.py:255
  8.2 2.3 %collective-permute-start.12 = (bf16[392,128]{1,0:T(8,128)(2,1)S(1)}, bf16[392,128]{1,0:T(8,128)(2,1)S(1)}, u32[]{:S(2)}, u32[]{:S(2)}) collective-permute-start(bf16[392,128]{1,0:T(8,128)(2,1)S(1)} %get-tuple-element.49), channel_id=1, source_target_pairs={{0,30},{2,28},{4,26},{6,24},{8,22},{10,20},{12,18},{14,16},{16,14}... | collective-permute-start | bytes 301064 | tf_op jit(solution)/shard_map/ppermute | solution.py:255
  10.5 3.1 %collective-permute-start.14 = (bf16[392,128]{1,0:T(8,128)(2,1)S(1)}, bf16[392,128]{1,0:T(8,128)(2,1)S(1)}, u32[]{:S(2)}, u32[]{:S(2)}) collective-permute-start(bf16[392,128]{1,0:T(8,128)(2,1)S(1)} %get-tuple-element.51), channel_id=1, source_target_pairs={{0,24},{2,26},{4,28},{6,30},{8,16},{10,18},{12,20},{14,22},{16,8},... | collective-permute-start | bytes 301064 | tf_op jit(solution)/shard_map/ppermute | solution.py:255
  13.6 1.4 %collective-permute-start.7 = (bf16[392,128]{1,0:T(8,128)(2,1)S(1)}, bf16[392,128]{1,0:T(8,128)(2,1)S(1)}, u32[]{:S(2)}, u32[]{:S(2)}) collective-permute-start(bf16[392,128]{1,0:T(8,128)(2,1)S(1)} %get-tuple-element.44), channel_id=1, source_target_pairs={{0,10},{2,8},{4,14},{6,12},{8,2},{10,0},{12,6},{14,4},{16,26},{18,... | collective-permute-start | bytes 301064 | tf_op jit(solution)/shard_map/ppermute | solution.py:255
  15.0 4.2 %collective-permute-start.8 = (bf16[392,128]{1,0:T(8,128)(2,1)S(1)}, bf16[392,128]{1,0:T(8,128)(2,1)S(1)}, u32[]{:S(2)}, u32[]{:S(2)}) collective-permute-start(bf16[392,128]{1,0:T(8,128)(2,1)S(1)} %get-tuple-element.45), channel_id=1, source_target_pairs={{0,26},{2,24},{4,30},{6,28},{8,18},{10,16},{12,22},{14,20},{16,10}... | collective-permute-start | bytes 301064 | tf_op jit(solution)/shard_map/ppermute | solution.py:255
  19.2 2.4 %collective-permute-start.9 = (bf16[392,128]{1,0:T(8,128)(2,1)S(1)}, bf16[392,128]{1,0:T(8,128)(2,1)S(1)}, u32[]{:S(2)}, u32[]{:S(2)}) collective-permute-start(bf16[392,128]{1,0:T(8,128)(2,1)S(1)} %get-tuple-element.46), channel_id=1, source_target_pairs={{0,12},{2,14},{4,8},{6,10},{8,4},{10,6},{12,0},{14,2},{16,28},{18,... | collective-permute-start | bytes 301064 | tf_op jit(solution)/shard_map/ppermute | solution.py:255
  21.6 4.5 %collective-permute-start = (bf16[392,128]{1,0:T(8,128)(2,1)S(1)}, bf16[392,128]{1,0:T(8,128)(2,1)S(1)}, u32[]{:S(2)}, u32[]{:S(2)}) collective-permute-start(bf16[392,128]{1,0:T(8,128)(2,1)S(1)} %get-tuple-element.37), channel_id=1, source_target_pairs={{0,28},{2,30},{4,24},{6,26},{8,20},{10,22},{12,16},{14,18},{16,12}... | collective-permute-start | bytes 301064 | tf_op jit(solution)/shard_map/ppermute | solution.py:255
  26.1 1.7 %collective-permute-start.2 = (bf16[392,128]{1,0:T(8,128)(2,1)S(1)}, bf16[392,128]{1,0:T(8,128)(2,1)S(1)}, u32[]{:S(2)}, u32[]{:S(2)}) collective-permute-start(bf16[392,128]{1,0:T(8,128)(2,1)S(1)} %get-tuple-element.39), channel_id=1, source_target_pairs={{0,18},{2,16},{4,22},{6,20},{8,26},{10,24},{12,30},{14,28},{16,2},... | collective-permute-start | bytes 301064 | tf_op jit(solution)/shard_map/ppermute | solution.py:255
  27.8 1.3 %collective-permute-start.3 = (bf16[392,128]{1,0:T(8,128)(2,1)S(1)}, bf16[392,128]{1,0:T(8,128)(2,1)S(1)}, u32[]{:S(2)}, u32[]{:S(2)}) collective-permute-start(bf16[392,128]{1,0:T(8,128)(2,1)S(1)} %get-tuple-element.40), channel_id=1, source_target_pairs={{0,4},{2,6},{4,0},{6,2},{8,12},{10,14},{12,8},{14,10},{16,20},{18,... | collective-permute-start | bytes 301064 | tf_op jit(solution)/shard_map/ppermute | solution.py:255
  29.1 1.9 %collective-permute-start.4 = (bf16[392,128]{1,0:T(8,128)(2,1)S(1)}, bf16[392,128]{1,0:T(8,128)(2,1)S(1)}, u32[]{:S(2)}, u32[]{:S(2)}) collective-permute-start(bf16[392,128]{1,0:T(8,128)(2,1)S(1)} %get-tuple-element.41), channel_id=1, source_target_pairs={{0,20},{2,22},{4,16},{6,18},{8,28},{10,30},{12,24},{14,26},{16,4},... | collective-permute-start | bytes 301064 | tf_op jit(solution)/shard_map/ppermute | solution.py:255
  31.1 0.6 %collective-permute-done.refs_1_ = bf16[392,128]{1,0:T(8,128)(2,1)S(1)} collective-permute-done((bf16[392,128]{1,0:T(8,128)(2,1)S(1)}, bf16[392,128]{1,0:T(8,128)(2,1)S(1)}, u32[]{:S(2)}, u32[]{:S(2)}) %collective-permute-start) | collective-permute-done | bytes 100384 | tf_op jit(solution)/shard_map/ppermute | solution.py:255
  31.8 2.6 %collective-permute-done.1.refs_2_ = bf16[392,128]{1,0:T(8,128)(2,1)S(1)} collective-permute-done((bf16[392,128]{1,0:T(8,128)(2,1)S(1)}, bf16[392,128]{1,0:T(8,128)(2,1)S(1)}, u32[]{:S(2)}, u32[]{:S(2)}) %collective-permute-start.1) | collective-permute-done | bytes 100384 | tf_op jit(solution)/shard_map/ppermute | solution.py:255
  34.5 2.1 %collective-permute-start.6 = (bf16[392,128]{1,0:T(8,128)(2,1)S(1)}, bf16[392,128]{1,0:T(8,128)(2,1)S(1)}, u32[]{:S(2)}, u32[]{:S(2)}) collective-permute-start(bf16[392,128]{1,0:T(8,128)(2,1)S(1)} %get-tuple-element.43), channel_id=1, source_target_pairs={{0,22},{2,20},{4,18},{6,16},{8,30},{10,28},{12,26},{14,24},{16,6},... | collective-permute-start | bytes 301064 | tf_op jit(solution)/shard_map/ppermute | solution.py:255
  37.4 0.8 %collective-permute-done.2.refs_3_ = bf16[392,128]{1,0:T(8,128)(2,1)S(1)} collective-permute-done((bf16[392,128]{1,0:T(8,128)(2,1)S(1)}, bf16[392,128]{1,0:T(8,128)(2,1)S(1)}, u32[]{:S(2)}, u32[]{:S(2)}) %collective-permute-start.2) | collective-permute-done | bytes 100384 | tf_op jit(solution)/shard_map/ppermute | solution.py:255
  38.3 1.9 %collective-permute-done.4.refs_5_ = bf16[392,128]{1,0:T(8,128)(2,1)S(1)} collective-permute-done((bf16[392,128]{1,0:T(8,128)(2,1)S(1)}, bf16[392,128]{1,0:T(8,128)(2,1)S(1)}, u32[]{:S(2)}, u32[]{:S(2)}) %collective-permute-start.4) | collective-permute-done | bytes 100384 | tf_op jit(solution)/shard_map/ppermute | solution.py:255
  40.2 3.7 %collective-permute-done.6.refs_7_ = bf16[392,128]{1,0:T(8,128)(2,1)S(1)} collective-permute-done((bf16[392,128]{1,0:T(8,128)(2,1)S(1)}, bf16[392,128]{1,0:T(8,128)(2,1)S(1)}, u32[]{:S(2)}, u32[]{:S(2)}) %collective-permute-start.6) | collective-permute-done | bytes 100384 | tf_op jit(solution)/shard_map/ppermute | solution.py:255
  44.3 1.1 %shard_map.42 = (f32[8,512]{1,0:T(8,128)S(1)}, f32[8,512]{1,0:T(8,128)S(1)}) custom-call(bf16[512,896]{1,0:T(8,128)(2,1)S(1)} %get-tuple-element.54.refs_0_.refs_5_, bf16[512,896]{1,0:T(8,128)(2,1)S(1)} %get-tuple-element.52.refs_0_.refs_2_.refs_1_.refs_4_, f32[8,512]{1,0:T(8,128)S(1)} %get-tuple-element.55.refs_2_, ...), custom_call_target="tpu_custom_call" | custom-call | flops 1 | bytes 1 | tf_op jit(solution)/shard_map/pallas_call | solution.py:185
  45.3 1.0 %shard_map.43 = (f32[8,512]{1,0:T(8,128)S(1)}, f32[8,512]{1,0:T(8,128)S(1)}) custom-call(bf16[512,896]{1,0:T(8,128)(2,1)S(1)} %get-tuple-element.54.refs_0_.refs_5_, bf16[512,896]{1,0:T(8,128)(2,1)S(1)} %get-tuple-element.52.refs_0_.refs_2_.refs_1_.refs_4_, f32[8,512]{1,0:T(8,128)S(1)} %get-tuple-element.55.refs_2_, ...), custom_call_target="tpu_custom_call" | custom-call | flops 1 | bytes 1 | tf_op jit(solution)/shard_map/pallas_call | solution.py:185
  46.7 1.0 %shard_map.44 = (f32[8,512]{1,0:T(8,128)S(1)}, f32[8,512]{1,0:T(8,128)S(1)}) custom-call(bf16[512,896]{1,0:T(8,128)(2,1)S(1)} %get-tuple-element.54.refs_0_.refs_5_, bf16[512,896]{1,0:T(8,128)(2,1)S(1)} %get-tuple-element.52.refs_0_.refs_2_.refs_1_.refs_4_, f32[8,512]{1,0:T(8,128)S(1)} %get-tuple-element.55.refs_2_, ...), custom_call_target="tpu_custom_call" | custom-call | flops 1 | bytes 1 | tf_op jit(solution)/shard_map/pallas_call | solution.py:185
  47.8 9.6 %all_to_all.5.back_ref = f32[16,1,128]{2,1,0:T(1,128)S(1)} all-to-all(f32[16,1,128]{2,1,0:T(1,128)S(1)} %shard_map.45), channel_id=1, replica_groups={{30,28,26,24,22,20,18,16,14,12,10,8,6,4,2,0},{31,29,27,25,23,21,19,17,1..., dimensions={0} | all-to-all | bytes 16384 | tf_op jit(solution)/shard_map/all_to_all | solution.py:276
  57.4 0.7 %shard_map.46 = f32[1,512]{1,0:T(1,128)} custom-call(f32[16,1,128]{2,1,0:T(1,128)S(1)} %all_to_all.5.back_ref, s32[1,512]{1,0:T(1,128)S(1)} %bitcast.5, s32[1,512]{1,0:T(1,128)S(1)} %get-tuple-element.62.pos_ref), custom_call_target="tpu_custom_call" | custom-call | tf_op jit(solution)/shard_map/pallas_call | solution.py:284
  (27 shorter events, 2.2 us)
Async XLA Ops:
  0.0 0.7 %copy-start.2 = (s32[512]{0:T(512)S(1)}, s32[512]{0:T(512)}, u32[]{:S(2)}) copy-start(s32[512]{0:T(512)} %param.5) | copy-start | bytes 6148
  0.0 0.7 %copy-start = (s32[512]{0:T(512)S(1)}, s32[512]{0:T(512)}, u32[]{:S(2)}) copy-start(s32[512]{0:T(512)} %param.4) | copy-start | bytes 6148
  0.0 1.2 %copy-start.1 = (bf16[512,768]{1,0:T(8,128)(2,1)S(1)}, bf16[512,768]{1,0:T(8,128)(2,1)}, u32[]{:S(2)}) copy-start(bf16[512,768]{1,0:T(8,128)(2,1)} %x_ref.1) | copy-start | bytes 2359300
  2.7 11.0 %collective-permute-start.10 = (bf16[392,128]{1,0:T(8,128)(2,1)S(1)}, bf16[392,128]{1,0:T(8,128)(2,1)S(1)}, u32[]{:S(2)}, u32[]{:S(2)}) collective-permute-start(bf16[392,128]{1,0:T(8,128)(2,1)S(1)} %get-tuple-element.47), channel_id=1, source_target_pairs={{0,16},{2,18},{4,20},{6,22},{8,24},{10,26},{12,28},{14,30},{16,0},... | collective-permute-start | bytes 301064 | tf_op jit(solution)/shard_map/ppermute | solution.py:255
  6.7 8.3 %collective-permute-start.11 = (bf16[392,128]{1,0:T(8,128)(2,1)S(1)}, bf16[392,128]{1,0:T(8,128)(2,1)S(1)}, u32[]{:S(2)}, u32[]{:S(2)}) collective-permute-start(bf16[392,128]{1,0:T(8,128)(2,1)S(1)} %get-tuple-element.48), channel_id=1, source_target_pairs={{0,2},{2,0},{4,6},{6,4},{8,10},{10,8},{12,14},{14,12},{16,18},{18,... | collective-permute-start | bytes 301064 | tf_op jit(solution)/shard_map/ppermute | solution.py:255
  8.2 11.0 %collective-permute-start.12 = (bf16[392,128]{1,0:T(8,128)(2,1)S(1)}, bf16[392,128]{1,0:T(8,128)(2,1)S(1)}, u32[]{:S(2)}, u32[]{:S(2)}) collective-permute-start(bf16[392,128]{1,0:T(8,128)(2,1)S(1)} %get-tuple-element.49), channel_id=1, source_target_pairs={{0,30},{2,28},{4,26},{6,24},{8,22},{10,20},{12,18},{14,16},{16,14}... | collective-permute-start | bytes 301064 | tf_op jit(solution)/shard_map/ppermute | solution.py:255
  10.5 11.1 %collective-permute-start.13 = (bf16[392,128]{1,0:T(8,128)(2,1)S(1)}, bf16[392,128]{1,0:T(8,128)(2,1)S(1)}, u32[]{:S(2)}, u32[]{:S(2)}) collective-permute-start(bf16[392,128]{1,0:T(8,128)(2,1)S(1)} %get-tuple-element.50), channel_id=1, source_target_pairs={{0,8},{2,10},{4,12},{6,14},{8,0},{10,2},{12,4},{14,6},{16,24},{18,... | collective-permute-start | bytes 301064 | tf_op jit(solution)/shard_map/ppermute | solution.py:255
  10.5 15.6 %collective-permute-start.14 = (bf16[392,128]{1,0:T(8,128)(2,1)S(1)}, bf16[392,128]{1,0:T(8,128)(2,1)S(1)}, u32[]{:S(2)}, u32[]{:S(2)}) collective-permute-start(bf16[392,128]{1,0:T(8,128)(2,1)S(1)} %get-tuple-element.51), channel_id=1, source_target_pairs={{0,24},{2,26},{4,28},{6,30},{8,16},{10,18},{12,20},{14,22},{16,8},... | collective-permute-start | bytes 301064 | tf_op jit(solution)/shard_map/ppermute | solution.py:255
  13.6 12.4 %collective-permute-start.7 = (bf16[392,128]{1,0:T(8,128)(2,1)S(1)}, bf16[392,128]{1,0:T(8,128)(2,1)S(1)}, u32[]{:S(2)}, u32[]{:S(2)}) collective-permute-start(bf16[392,128]{1,0:T(8,128)(2,1)S(1)} %get-tuple-element.44), channel_id=1, source_target_pairs={{0,10},{2,8},{4,14},{6,12},{8,2},{10,0},{12,6},{14,4},{16,26},{18,... | collective-permute-start | bytes 301064 | tf_op jit(solution)/shard_map/ppermute | solution.py:255
  15.0 12.8 %collective-permute-start.8 = (bf16[392,128]{1,0:T(8,128)(2,1)S(1)}, bf16[392,128]{1,0:T(8,128)(2,1)S(1)}, u32[]{:S(2)}, u32[]{:S(2)}) collective-permute-start(bf16[392,128]{1,0:T(8,128)(2,1)S(1)} %get-tuple-element.45), channel_id=1, source_target_pairs={{0,26},{2,24},{4,30},{6,28},{8,18},{10,16},{12,22},{14,20},{16,10}... | collective-permute-start | bytes 301064 | tf_op jit(solution)/shard_map/ppermute | solution.py:255
  19.2 9.9 %collective-permute-start.9 = (bf16[392,128]{1,0:T(8,128)(2,1)S(1)}, bf16[392,128]{1,0:T(8,128)(2,1)S(1)}, u32[]{:S(2)}, u32[]{:S(2)}) collective-permute-start(bf16[392,128]{1,0:T(8,128)(2,1)S(1)} %get-tuple-element.46), channel_id=1, source_target_pairs={{0,12},{2,14},{4,8},{6,10},{8,4},{10,6},{12,0},{14,2},{16,28},{18,... | collective-permute-start | bytes 301064 | tf_op jit(solution)/shard_map/ppermute | solution.py:255
  21.6 10.1 %collective-permute-start = (bf16[392,128]{1,0:T(8,128)(2,1)S(1)}, bf16[392,128]{1,0:T(8,128)(2,1)S(1)}, u32[]{:S(2)}, u32[]{:S(2)}) collective-permute-start(bf16[392,128]{1,0:T(8,128)(2,1)S(1)} %get-tuple-element.37), channel_id=1, source_target_pairs={{0,28},{2,30},{4,24},{6,26},{8,20},{10,22},{12,16},{14,18},{16,12}... | collective-permute-start | bytes 301064 | tf_op jit(solution)/shard_map/ppermute | solution.py:255
  26.1 8.4 %collective-permute-start.1 = (bf16[392,128]{1,0:T(8,128)(2,1)S(1)}, bf16[392,128]{1,0:T(8,128)(2,1)S(1)}, u32[]{:S(2)}, u32[]{:S(2)}) collective-permute-start(bf16[392,128]{1,0:T(8,128)(2,1)S(1)} %get-tuple-element.38), channel_id=1, source_target_pairs={{0,14},{2,12},{4,10},{6,8},{8,6},{10,4},{12,2},{14,0},{16,30},{18,... | collective-permute-start | bytes 301064 | tf_op jit(solution)/shard_map/ppermute | solution.py:255
  26.1 12.2 %collective-permute-start.2 = (bf16[392,128]{1,0:T(8,128)(2,1)S(1)}, bf16[392,128]{1,0:T(8,128)(2,1)S(1)}, u32[]{:S(2)}, u32[]{:S(2)}) collective-permute-start(bf16[392,128]{1,0:T(8,128)(2,1)S(1)} %get-tuple-element.39), channel_id=1, source_target_pairs={{0,18},{2,16},{4,22},{6,20},{8,26},{10,24},{12,30},{14,28},{16,2},... | collective-permute-start | bytes 301064 | tf_op jit(solution)/shard_map/ppermute | solution.py:255
  27.8 10.5 %collective-permute-start.3 = (bf16[392,128]{1,0:T(8,128)(2,1)S(1)}, bf16[392,128]{1,0:T(8,128)(2,1)S(1)}, u32[]{:S(2)}, u32[]{:S(2)}) collective-permute-start(bf16[392,128]{1,0:T(8,128)(2,1)S(1)} %get-tuple-element.40), channel_id=1, source_target_pairs={{0,4},{2,6},{4,0},{6,2},{8,12},{10,14},{12,8},{14,10},{16,20},{18,... | collective-permute-start | bytes 301064 | tf_op jit(solution)/shard_map/ppermute | solution.py:255
  29.1 11.1 %collective-permute-start.4 = (bf16[392,128]{1,0:T(8,128)(2,1)S(1)}, bf16[392,128]{1,0:T(8,128)(2,1)S(1)}, u32[]{:S(2)}, u32[]{:S(2)}) collective-permute-start(bf16[392,128]{1,0:T(8,128)(2,1)S(1)} %get-tuple-element.41), channel_id=1, source_target_pairs={{0,20},{2,22},{4,16},{6,18},{8,28},{10,30},{12,24},{14,26},{16,4},... | collective-permute-start | bytes 301064 | tf_op jit(solution)/shard_map/ppermute | solution.py:255
  31.7 8.5 %collective-permute-start.5 = (bf16[392,128]{1,0:T(8,128)(2,1)S(1)}, bf16[392,128]{1,0:T(8,128)(2,1)S(1)}, u32[]{:S(2)}, u32[]{:S(2)}) collective-permute-start(bf16[392,128]{1,0:T(8,128)(2,1)S(1)} %get-tuple-element.42), channel_id=1, source_target_pairs={{0,6},{2,4},{4,2},{6,0},{8,14},{10,12},{12,10},{14,8},{16,22},{18,... | collective-permute-start | bytes 301064 | tf_op jit(solution)/shard_map/ppermute | solution.py:255
  34.5 9.5 %collective-permute-start.6 = (bf16[392,128]{1,0:T(8,128)(2,1)S(1)}, bf16[392,128]{1,0:T(8,128)(2,1)S(1)}, u32[]{:S(2)}, u32[]{:S(2)}) collective-permute-start(bf16[392,128]{1,0:T(8,128)(2,1)S(1)} %get-tuple-element.43), channel_id=1, source_target_pairs={{0,22},{2,20},{4,18},{6,16},{8,30},{10,28},{12,26},{14,24},{16,6},... | collective-permute-start | bytes 301064 | tf_op jit(solution)/shard_map/ppermute | solution.py:255
  38.3 7.0 %collective-permute-start.16 = (bf16[512,896]{1,0:T(8,128)(2,1)S(1)}, bf16[512,896]{1,0:T(8,128)(2,1)S(1)}, u32[]{:S(2)}, u32[]{:S(2)}) collective-permute-start(bf16[512,896]{1,0:T(8,128)(2,1)S(1)} %get-tuple-element.52.refs_0_.refs_2_.refs_1_.refs_4_), channel_id=1, source_target_pairs={{0,1},{1,0},{2,3},{3,2},{4,5},{5,4},{6,7},{7,6},{8,9},{9,8},{10,11... | collective-permute-start | bytes 2752520 | tf_op jit(solution)/shard_map/ppermute | solution.py:258
  44.2 2.5 %collective-permute-start.15 = (bf16[512,896]{1,0:T(8,128)(2,1)S(1)}, bf16[512,896]{1,0:T(8,128)(2,1)S(1)}, u32[]{:S(2)}, u32[]{:S(2)}) collective-permute-start(bf16[512,896]{1,0:T(8,128)(2,1)S(1)} %get-tuple-element.54.refs_0_.refs_5_), channel_id=1, source_target_pairs={{0,1},{1,0},{2,3},{3,2},{4,5},{5,4},{6,7},{7,6},{8,9},{9,8},{10,11... | collective-permute-start | bytes 2752520 | tf_op jit(solution)/shard_map/ppermute | solution.py:258

commit v2 on v1

--- a/solution.py
+++ b/solution.py
@@ -26,8 +26,9 @@
 
 def partners(nodes):
     half = nodes // 2
-    far = [half, nodes - 1, *range(half + half // 2, nodes - 1), *range(half + 1, half + half // 2)]
-    near = [1, *range(half // 2, half), *range(2, half // 2)]
+    quarter = half // 2
+    far = [flip for i in range(quarter) for flip in (half + quarter + i, half + i)]
+    near = [*range(quarter, half), *range(1, quarter)]
     sequence = [far[0]]
     for pair in zip(near, far[1:]):
         sequence.extend(pair)
@@ -72,28 +73,33 @@
         digits_ref[at, :] = jnp.transpose(digits).astype(jnp.bfloat16)
 
 
-def pack_kernel(x_ref, target_ref, digits_ref, *out_refs, capacity):
-    nodes = len(out_refs)
-    rows, width = x_ref.shape
+def pack_kernel(rows_ref, target_ref, digits_ref, *refs, chosen, capacity, first):
+    *out_refs, whole_ref = refs if first else (*refs, None)
+    rows = rows_ref.shape[0]
+    slot = lax.broadcasted_iota(jnp.int32, (capacity, rows), 0)
+    place = [(slot + g * capacity == target_ref[...]).astype(jnp.float32) for g in chosen]
+    place = jnp.concatenate(place, axis=0).astype(jnp.bfloat16)
+    if first:
+        widened = rows_ref[...].astype(jnp.float32)
+        squares = jnp.sum(widened * widened, axis=1, keepdims=True)
+        normed = (widened * lax.rsqrt(squares + 1e-06)).astype(jnp.bfloat16)
+        whole = jnp.concatenate([normed, digits_ref[...]], axis=1)
+        whole_ref[...] = whole
+    else:
+        whole = rows_ref[...]
+    width = whole.shape[1] - LANES
     pieces = width // LANES
-    slots = nodes * capacity
-    place = lax.broadcasted_iota(jnp.int32, (slots, rows), 0) == target_ref[...]
-    place = place.astype(jnp.float32).astype(jnp.bfloat16)
-    widened = x_ref[...].astype(jnp.float32)
-    squares = jnp.sum(widened * widened, axis=1, keepdims=True)
-    normed = (widened * lax.rsqrt(squares + 1e-06)).astype(jnp.bfloat16)
-    whole = jnp.concatenate([normed, digits_ref[...]], axis=1)
     moved = jnp.dot(place, whole, preferred_element_type=jnp.float32)
-    for first in range(0, slots, LANES):
-        lines = jnp.transpose(moved[first : first + LANES, width:])[0:EXTRA, :].astype(jnp.bfloat16)
-        for g in range(first // capacity, (first + LANES) // capacity):
-            at = g * capacity
-            for p in range(pieces):
-                out_refs[g][p * capacity : (p + 1) * capacity, :] = moved[
-                    at : at + capacity, p * LANES : (p + 1) * LANES
-                ].astype(jnp.bfloat16)
-            out_refs[g][pieces * capacity :, :] = jnp.zeros((EXTRA, LANES), jnp.bfloat16)
-            out_refs[g][pieces * capacity :, 0:capacity] = lines[:, at - first : at - first + capacity]
+    for i, out_ref in enumerate(out_refs):
+        at = slice(i * capacity, (i + 1) * capacity)
+        for p in range(pieces):
+            out_ref[p * capacity : (p + 1) * capacity, :] = moved[
+                at, p * LANES : (p + 1) * LANES
+            ].astype(jnp.bfloat16)
+        square = jnp.concatenate(
+            [moved[at, width:], jnp.zeros((LANES - capacity, LANES), jnp.float32)], axis=0
+        )
+        out_ref[pieces * capacity :, :] = jnp.transpose(square)[0:EXTRA, :].astype(jnp.bfloat16)
 
 
 def assemble_kernel(*refs, messages, capacity, pieces):
@@ -134,7 +140,7 @@
     )(*messages, *after, *held)
 
 
-def match_kernel(*refs, width, queries, candidates, pairs, mirrored, carried):
+def match_kernel(*refs, width, queries, candidates, foreign, pairs, mirrored, carried):
     q_refs, refs = refs[:queries], refs[queries:]
     line_refs, refs = refs[:queries], refs[queries:]
     k_refs, refs = refs[:candidates], refs[candidates:]
@@ -143,6 +149,8 @@
     for q in range(queries):
         rows = q_refs[q].shape[0]
         best[q] = carry_refs[q][0:1, :] if q in carry_refs else jnp.full((1, rows), -1.0, jnp.float32)
+    for extra in range(queries, queries + foreign):
+        best[extra] = jnp.full((1, out_refs[extra].shape[1]), -1.0, jnp.float32)
     for k in range(candidates):
         for first in range(0, k_refs[k].shape[0], TILE):
             at = slice(first, min(first + TILE, k_refs[k].shape[0]))
@@ -170,11 +178,11 @@
                         folded = jnp.maximum(folded, kept[:, lane : lane + LANES])
                     found = jnp.max(jnp.transpose(folded), axis=0, keepdims=True)
                     best[asked] = jnp.maximum(best[asked], found)
-    for q in range(queries):
+    for q in range(queries + foreign):
         out_refs[q][0:1, :] = best[q]
 
 
-def match(groups, candidates, pairs, carry, width, mirrored=None):
+def match(groups, candidates, pairs, carry, width, mirrored=None, foreign=0):
     carried = tuple(sorted(carry))
     operands = [
         *[rows for rows, _ in groups],
@@ -188,24 +196,29 @@
             width=width,
             queries=len(groups),
             candidates=len(candidates),
+            foreign=foreign,
             pairs=frozenset(pairs),
             mirrored=mirrored or {},
             carried=carried,
         ),
-        out_shape=[jax.ShapeDtypeStruct(line.shape, jnp.float32) for _, line in groups],
+        out_shape=[jax.ShapeDtypeStruct(line.shape, jnp.float32) for _, line in groups]
+        + [jax.ShapeDtypeStruct(groups[0][1].shape, jnp.float32)] * foreign,
         in_specs=[VMEM] * len(operands),
-        out_specs=[VMEM] * len(groups),
+        out_specs=[VMEM] * (len(groups) + foreign),
         compiler_params=PARAMS,
         cost_estimate=LIGHT,
     )(*operands)
 
 
-def address_kernel(me_ref, *refs, flips, capacity):
-    *lines, out_ref = refs
+def address_kernel(me_ref, first_ref, second_ref, other_ref, out_ref, *, flips, capacity):
     out_ref[...] = jnp.zeros(out_ref.shape, jnp.float32)
+    second = jnp.maximum(second_ref[0:1, :], other_ref[0:1, :])
+    lines = [first_ref[0:1, :], second]
     blocks = [(line, i) for line in lines for i in range(line.shape[1] // capacity)]
     for flip, (line, i) in zip(flips, blocks):
-        out_ref[(out_ref.shape[0] - 1) - (me_ref[0] ^ flip), 0:1, 0:capacity] = line[0:1, i * capacity : (i + 1) * capacity]
+        out_ref[(out_ref.shape[0] - 1) - (me_ref[0] ^ flip), 0:1, 0:capacity] = line[
+            :, i * capacity : (i + 1) * capacity
+        ]
 
 
 def unpack_kernel(back_ref, cid_ref, pos_ref, out_ref):
@@ -240,17 +253,27 @@
         compiler_params=PARAMS,
         cost_estimate=pl.CostEstimate(flops=2**28, bytes_accessed=2**12, transcendentals=0),
     )(me, cid, rank.reshape(1, rows))
-    messages = pl.pallas_call(
-        functools.partial(pack_kernel, capacity=capacity),
-        out_shape=[jax.ShapeDtypeStruct((height, LANES), jnp.bfloat16)] * nodes,
-        in_specs=[VMEM] * 3,
-        out_specs=[VMEM] * nodes,
-        compiler_params=PARAMS,
-        cost_estimate=pl.CostEstimate(
-            flops=2 * nodes * capacity * rows * (width + LANES), bytes_accessed=2**12, transcendentals=0
-        ),
-    )(embeddings, target, digits)
-    messages = list(messages)
+    early = range(half, nodes)
+    messages = [None] * nodes
+    given = embeddings
+    for chosen in (list(early), [g for g in range(nodes) if g not in early]):
+        first = given is embeddings
+        packed = pl.pallas_call(
+            functools.partial(pack_kernel, chosen=chosen, capacity=capacity, first=first),
+            out_shape=[jax.ShapeDtypeStruct((height, LANES), jnp.bfloat16)] * len(chosen)
+            + [jax.ShapeDtypeStruct((rows, width + LANES), jnp.bfloat16)] * first,
+            in_specs=[VMEM] * 3,
+            out_specs=[VMEM] * (len(chosen) + first),
+            compiler_params=PARAMS,
+            cost_estimate=pl.CostEstimate(
+                flops=2 * len(chosen) * capacity * rows * (width + LANES),
+                bytes_accessed=2**12,
+                transcendentals=0,
+            ),
+        )(given, target, digits)
+        for g, message in zip(chosen, packed):
+            messages[g] = message
+        given = packed[-1]
     for g in range(1, nodes):
         messages[g] = lax.ppermute(messages[g], "ingest", [(i, i ^ flips[g]) for i in range(nodes)])
 
@@ -261,18 +284,25 @@
     (best_b,) = match([(b, b_line)], [b], [(0, 0)], {}, width)
     a, a_line = assemble(messages[:half], half, [best_b], [], width)
     groups = [(a, a_line), (b, b_line)]
+    b_other = across(b)
+    best_a, for_other = match([(a, a_line)], [b_other], [(0, 0)], {}, width, {(0, 0): 1}, foreign=1)
+    from_other = across(for_other)
     best_a, best_b = match(
-        groups, [b, a], [(0, 1), (0, 0)], {1: best_b}, width, mirrored={(0, 0): 1}
+        groups,
+        [b, a, b_other],
+        [(0, 1), (0, 0), (1, 2)],
+        {0: best_a, 1: best_b},
+        width,
+        {(0, 0): 1},
     )
-    for other in (across(b), across(a)):
-        best_a, best_b = match(groups, [other], [(0, 0), (1, 0)], {0: best_a, 1: best_b}, width)
+    (best_a,) = match([(a, a_line)], [across(a)], [(0, 0)], {0: best_a}, width)
     highest = pl.pallas_call(
         functools.partial(address_kernel, flips=flips, capacity=capacity),
         out_shape=jax.ShapeDtypeStruct((nodes, 1, LANES), jnp.float32),
-        in_specs=[SMEM] + [VMEM] * 2,
+        in_specs=[SMEM] + [VMEM] * 3,
         out_specs=VMEM,
         compiler_params=PARAMS,
-    )(me, best_a, best_b)
+    )(me, best_a, best_b, from_other)
     back = lax.all_to_all(
         highest,
         "ingest",

time: 58.3 us -> 57.3 us (0.983)
  starting transfers between devices: 30.7 us -> 28.2 us
  waiting for transfers between devices: 10.1 us -> 12.1 us
    ppermute x15, starting transfers between devices: 30.6 us -> 27.6 us  [body(): lax.ppermute(messages[g], 'ingest', [(i, i ^ flips[g]) for i in range(nod...]
    ppermute x15, waiting for transfers between devices: 9.79 us -> 12.1 us  [body(): lax.ppermute(messages[g], 'ingest', [(i, i ^ flips[g]) for i in range(nod...]
    pallas_call x1 -> x2, Pallas kernels: 1.51 us -> 1.7 us  [body(): pl.pallas_call(functools.partial(pack_kernel, chosen=chosen, capacity=cap...]
  transfers between devices with their start and end apart: 17 -> 18, of which waited for: 6 -> 6; matrix products, arithmetic and copies ran while one was open for 0% -> 0% of each run, Pallas kernels for 5% -> 8%
where the time goes in v2:
time: 57.3 us; the launch traced here: 57.1 us
  starting transfers between devices  28.2 us (49%)
  waiting for transfers between devices  12.1 us (21%)
  blocking collectives  9.07 us (16%)
  Pallas kernels  6.56 us (11%)
  local copies, waits for them, and re-layouts  1 us (2%)
    ppermute x15, starting transfers between devices, body(): lax.ppermute(messages[g], 'ingest', [(i, i ^ flips[g]) for i in range(nod...  27.6 us
    ppermute x15, waiting for transfers between devices, body(): lax.ppermute(messages[g], 'ingest', [(i, i ^ flips[g]) for i in range(nod...  12.1 us
    all_to_all x1, blocking collectives, body(): lax.all_to_all(highest, 'ingest', split_axis=0, concat_axis=0, tiled=True...  9.07 us
    pallas_call x4, Pallas kernels, match(): pl.pallas_call(functools.partial(match_kernel, width=width, queries=len(g...  3.51 us
    pallas_call x2, Pallas kernels, body(): pl.pallas_call(functools.partial(pack_kernel, chosen=chosen, capacity=cap...  1.7 us
  transfers between devices with their start and end apart: 18, of which 6 were waited for; matrix products, arithmetic and copies ran while one was open for 0% of the time, Pallas kernels for 8%

profile of v2, /device:TPU:0, one launch (start us, length us, event | category | flops | bytes accessed | tf_op | source)
XLA Modules:
  0.0 57.1 jit_solution(13356540938549390585)
XLA Ops:
  0.0 0.7 %copy-done.2 = s32[512]{0:T(512)S(1)} copy-done((s32[512]{0:T(512)S(1)}, s32[512]{0:T(512)}, u32[]{:S(2)}) %copy-start.2) | copy-done | bytes 2072
  1.2 0.9 %shard_map.38 = (bf16[392,128]{1,0:T(8,128)(2,1)S(1)}, bf16[392,128]{1,0:T(8,128)(2,1)S(1)}, bf16[392,128]{1,0:T(8,128)(2,1)S(1)}, bf16[392,128]{1,0:T(8,128)(2,...) custom-call(bf16[512,768]{1,0:T(8,128)(2,1)S(1)} %copy-done.1, ...), custom_call_target="tpu_custom_call" | custom-call | flops 469762048 | bytes 4096 | tf_op jit(solution)/shard_map/pallas_call | solution.py:261
  2.1 5.1 %collective-permute-start.10 = (bf16[392,128]{1,0:T(8,128)(2,1)S(1)}, bf16[392,128]{1,0:T(8,128)(2,1)S(1)}, u32[]{:S(2)}, u32[]{:S(2)}) collective-permute-start(bf16[392,128]{1,0:T(8,128)(2,1)S(1)} %get-tuple-element.47), channel_id=1, source_target_pairs={{0,24},{2,26},{4,28},{6,30},{8,16},{10,18},{12,20},{14,22},{16,8},... | collective-permute-start | bytes 301064 | tf_op jit(solution)/shard_map/ppermute | solution.py:278
  7.2 0.6 %collective-permute-start.12 = (bf16[392,128]{1,0:T(8,128)(2,1)S(1)}, bf16[392,128]{1,0:T(8,128)(2,1)S(1)}, u32[]{:S(2)}, u32[]{:S(2)}) collective-permute-start(bf16[392,128]{1,0:T(8,128)(2,1)S(1)} %get-tuple-element.49), channel_id=1, source_target_pairs={{0,16},{2,18},{4,20},{6,22},{8,24},{10,26},{12,28},{14,30},{16,0},... | collective-permute-start | bytes 301064 | tf_op jit(solution)/shard_map/ppermute | solution.py:278
  7.8 2.3 %collective-permute-start.13 = (bf16[392,128]{1,0:T(8,128)(2,1)S(1)}, bf16[392,128]{1,0:T(8,128)(2,1)S(1)}, u32[]{:S(2)}, u32[]{:S(2)}) collective-permute-start(bf16[392,128]{1,0:T(8,128)(2,1)S(1)} %get-tuple-element.50), channel_id=1, source_target_pairs={{0,10},{2,8},{4,14},{6,12},{8,2},{10,0},{12,6},{14,4},{16,26},{18,... | collective-permute-start | bytes 301064 | tf_op jit(solution)/shard_map/ppermute | solution.py:278
  10.1 2.4 %collective-permute-start.14 = (bf16[392,128]{1,0:T(8,128)(2,1)S(1)}, bf16[392,128]{1,0:T(8,128)(2,1)S(1)}, u32[]{:S(2)}, u32[]{:S(2)}) collective-permute-start(bf16[392,128]{1,0:T(8,128)(2,1)S(1)} %get-tuple-element.51), channel_id=1, source_target_pairs={{0,26},{2,24},{4,30},{6,28},{8,18},{10,16},{12,22},{14,20},{16,10}... | collective-permute-start | bytes 301064 | tf_op jit(solution)/shard_map/ppermute | solution.py:278
  12.5 2.1 %collective-permute-start.7 = (bf16[392,128]{1,0:T(8,128)(2,1)S(1)}, bf16[392,128]{1,0:T(8,128)(2,1)S(1)}, u32[]{:S(2)}, u32[]{:S(2)}) collective-permute-start(bf16[392,128]{1,0:T(8,128)(2,1)S(1)} %get-tuple-element.44), channel_id=1, source_target_pairs={{0,12},{2,14},{4,8},{6,10},{8,4},{10,6},{12,0},{14,2},{16,28},{18,... | collective-permute-start | bytes 301064 | tf_op jit(solution)/shard_map/ppermute | solution.py:278
  14.6 0.8 %shard_map.39 = (bf16[392,128]{1,0:T(8,128)(2,1)S(1)}, bf16[392,128]{1,0:T(8,128)(2,1)S(1)}, bf16[392,128]{1,0:T(8,128)(2,1)S(1)}, bf16[392,128]{1,0:T(8,128)(2,...) custom-call(bf16[512,896]{1,0:T(8,128)(2,1)S(1)} %get-tuple-element., ...), custom_call_target="tpu_custom_call" | custom-call | flops 469762048 | bytes 4096 | tf_op jit(solution)/shard_map/pallas_call | solution.py:261
  15.3 2.6 %collective-permute-start.8 = (bf16[392,128]{1,0:T(8,128)(2,1)S(1)}, bf16[392,128]{1,0:T(8,128)(2,1)S(1)}, u32[]{:S(2)}, u32[]{:S(2)}) collective-permute-start(bf16[392,128]{1,0:T(8,128)(2,1)S(1)} %get-tuple-element.45), channel_id=1, source_target_pairs={{0,18},{2,16},{4,22},{6,20},{8,26},{10,24},{12,30},{14,28},{16,2},... | collective-permute-start | bytes 301064 | tf_op jit(solution)/shard_map/ppermute | solution.py:278
  18.2 2.4 %collective-permute-done.13.refs_6_ = bf16[392,128]{1,0:T(8,128)(2,1)S(1)} collective-permute-done((bf16[392,128]{1,0:T(8,128)(2,1)S(1)}, bf16[392,128]{1,0:T(8,128)(2,1)S(1)}, u32[]{:S(2)}, u32[]{:S(2)}) %collective-permute-start.13) | collective-permute-done | bytes 100384 | tf_op jit(solution)/shard_map/ppermute | solution.py:278
  20.6 0.9 %collective-permute-start = (bf16[392,128]{1,0:T(8,128)(2,1)S(1)}, bf16[392,128]{1,0:T(8,128)(2,1)S(1)}, u32[]{:S(2)}, u32[]{:S(2)}) collective-permute-start(bf16[392,128]{1,0:T(8,128)(2,1)S(1)} %get-tuple-element.37), channel_id=1, source_target_pairs={{0,28},{2,30},{4,24},{6,26},{8,20},{10,22},{12,16},{14,18},{16,12}... | collective-permute-start | bytes 301064 | tf_op jit(solution)/shard_map/ppermute | solution.py:278
  21.5 1.5 %collective-permute-start.1 = (bf16[392,128]{1,0:T(8,128)(2,1)S(1)}, bf16[392,128]{1,0:T(8,128)(2,1)S(1)}, u32[]{:S(2)}, u32[]{:S(2)}) collective-permute-start(bf16[392,128]{1,0:T(8,128)(2,1)S(1)} %get-tuple-element.38), channel_id=1, source_target_pairs={{0,2},{2,0},{4,6},{6,4},{8,10},{10,8},{12,14},{14,12},{16,18},{18,... | collective-permute-start | bytes 301064 | tf_op jit(solution)/shard_map/ppermute | solution.py:278
  23.0 1.0 %collective-permute-done.7.refs_0_ = bf16[392,128]{1,0:T(8,128)(2,1)S(1)} collective-permute-done((bf16[392,128]{1,0:T(8,128)(2,1)S(1)}, bf16[392,128]{1,0:T(8,128)(2,1)S(1)}, u32[]{:S(2)}, u32[]{:S(2)}) %collective-permute-start.7) | collective-permute-done | bytes 100384 | tf_op jit(solution)/shard_map/ppermute | solution.py:278
  24.0 2.3 %collective-permute-done.8.refs_1_ = bf16[392,128]{1,0:T(8,128)(2,1)S(1)} collective-permute-done((bf16[392,128]{1,0:T(8,128)(2,1)S(1)}, bf16[392,128]{1,0:T(8,128)(2,1)S(1)}, u32[]{:S(2)}, u32[]{:S(2)}) %collective-permute-start.8) | collective-permute-done | bytes 100384 | tf_op jit(solution)/shard_map/ppermute | solution.py:278
  26.4 1.5 %collective-permute-start.3 = (bf16[392,128]{1,0:T(8,128)(2,1)S(1)}, bf16[392,128]{1,0:T(8,128)(2,1)S(1)}, u32[]{:S(2)}, u32[]{:S(2)}) collective-permute-start(bf16[392,128]{1,0:T(8,128)(2,1)S(1)} %get-tuple-element.40), channel_id=1, source_target_pairs={{0,4},{2,6},{4,0},{6,2},{8,12},{10,14},{12,8},{14,10},{16,20},{18,... | collective-permute-start | bytes 301064 | tf_op jit(solution)/shard_map/ppermute | solution.py:278
  28.5 0.8 %collective-permute-start.4 = (bf16[392,128]{1,0:T(8,128)(2,1)S(1)}, bf16[392,128]{1,0:T(8,128)(2,1)S(1)}, u32[]{:S(2)}, u32[]{:S(2)}) collective-permute-start(bf16[392,128]{1,0:T(8,128)(2,1)S(1)} %get-tuple-element.41), channel_id=1, source_target_pairs={{0,30},{2,28},{4,26},{6,24},{8,22},{10,20},{12,18},{14,16},{16,14}... | collective-permute-start | bytes 301064 | tf_op jit(solution)/shard_map/ppermute | solution.py:278
  29.3 2.3 %collective-permute-start.5 = (bf16[392,128]{1,0:T(8,128)(2,1)S(1)}, bf16[392,128]{1,0:T(8,128)(2,1)S(1)}, u32[]{:S(2)}, u32[]{:S(2)}) collective-permute-start(bf16[392,128]{1,0:T(8,128)(2,1)S(1)} %get-tuple-element.42), channel_id=1, source_target_pairs={{0,6},{2,4},{4,2},{6,0},{8,14},{10,12},{12,10},{14,8},{16,22},{18,... | collective-permute-start | bytes 301064 | tf_op jit(solution)/shard_map/ppermute | solution.py:278
  31.7 5.2 %collective-permute-start.6 = (bf16[392,128]{1,0:T(8,128)(2,1)S(1)}, bf16[392,128]{1,0:T(8,128)(2,1)S(1)}, u32[]{:S(2)}, u32[]{:S(2)}) collective-permute-start(bf16[392,128]{1,0:T(8,128)(2,1)S(1)} %get-tuple-element.43), channel_id=1, source_target_pairs={{0,22},{2,20},{4,18},{6,16},{8,30},{10,28},{12,26},{14,24},{16,6},... | collective-permute-start | bytes 301064 | tf_op jit(solution)/shard_map/ppermute | solution.py:278
  37.1 0.8 %collective-permute-done.2.refs_3_ = bf16[392,128]{1,0:T(8,128)(2,1)S(1)} collective-permute-done((bf16[392,128]{1,0:T(8,128)(2,1)S(1)}, bf16[392,128]{1,0:T(8,128)(2,1)S(1)}, u32[]{:S(2)}, u32[]{:S(2)}) %collective-permute-start.2) | collective-permute-done | bytes 100384 | tf_op jit(solution)/shard_map/ppermute | solution.py:278
  38.6 4.9 %collective-permute-done.6.refs_7_ = bf16[392,128]{1,0:T(8,128)(2,1)S(1)} collective-permute-done((bf16[392,128]{1,0:T(8,128)(2,1)S(1)}, bf16[392,128]{1,0:T(8,128)(2,1)S(1)}, u32[]{:S(2)}, u32[]{:S(2)}) %collective-permute-start.6) | collective-permute-done | bytes 100384 | tf_op jit(solution)/shard_map/ppermute | solution.py:278
  43.8 0.8 %shard_map.43 = (f32[8,512]{1,0:T(8,128)S(1)}, f32[8,512]{1,0:T(8,128)S(1)}) custom-call(bf16[512,896]{1,0:T(8,128)(2,1)S(1)} %get-tuple-element.54.refs_0_.refs_5_, f32[8,512]{1,0:T(8,128)S(1)} %get-tuple-element.55.refs_1_.refs_2_, bf16[512,896]{1,0:T(8,128)(2,1)S(1)} %collective-permute-done.16.refs_2_.refs_6_), custom_call_target="tpu_custom_call" | custom-call | flops 1 | bytes 1 | tf_op jit(solution)/shard_map/pallas_call | solution.py:193
  45.1 1.5 %shard_map.44 = (f32[8,512]{1,0:T(8,128)S(1)}, f32[8,512]{1,0:T(8,128)S(1)}) custom-call(bf16[512,896]{1,0:T(8,128)(2,1)S(1)} %get-tuple-element.54.refs_0_.refs_5_, bf16[512,896]{1,0:T(8,128)(2,1)S(1)} %get-tuple-element.52.refs_0_.refs_2_.refs_1_.refs_4_, f32[8,512]{1,0:T(8,128)S(1)} %get-tuple-element.55.refs_1_.refs_2_, ...), custom_call_target="tpu_custom_call" | custom-call | flops 1 | bytes 1 | tf_op jit(solution)/shard_map/pallas_call | solution.py:193
  47.3 9.1 %all_to_all.5.back_ref = f32[16,1,128]{2,1,0:T(1,128)S(1)} all-to-all(f32[16,1,128]{2,1,0:T(1,128)S(1)} %shard_map.46), channel_id=1, replica_groups={{30,28,26,24,22,20,18,16,14,12,10,8,6,4,2,0},{31,29,27,25,23,21,19,17,1..., dimensions={0} | all-to-all | bytes 16384 | tf_op jit(solution)/shard_map/all_to_all | solution.py:306
  56.4 0.7 %shard_map.47 = f32[1,512]{1,0:T(1,128)} custom-call(f32[16,1,128]{2,1,0:T(1,128)S(1)} %all_to_all.5.back_ref, s32[1,512]{1,0:T(1,128)S(1)} %bitcast.5, s32[1,512]{1,0:T(1,128)S(1)} %get-tuple-element.60.pos_ref), custom_call_target="tpu_custom_call" | custom-call | tf_op jit(solution)/shard_map/pallas_call | solution.py:314
  (30 shorter events, 3.8 us)
Async XLA Ops:
  0.0 0.7 %copy-start.2 = (s32[512]{0:T(512)S(1)}, s32[512]{0:T(512)}, u32[]{:S(2)}) copy-start(s32[512]{0:T(512)} %param.5) | copy-start | bytes 6148
  0.0 0.7 %copy-start = (s32[512]{0:T(512)S(1)}, s32[512]{0:T(512)}, u32[]{:S(2)}) copy-start(s32[512]{0:T(512)} %param.4) | copy-start | bytes 6148
  0.0 1.2 %copy-start.1 = (bf16[512,768]{1,0:T(8,128)(2,1)S(1)}, bf16[512,768]{1,0:T(8,128)(2,1)}, u32[]{:S(2)}) copy-start(bf16[512,768]{1,0:T(8,128)(2,1)} %rows_ref.1) | copy-start | bytes 2359300
  2.1 10.4 %collective-permute-start.10 = (bf16[392,128]{1,0:T(8,128)(2,1)S(1)}, bf16[392,128]{1,0:T(8,128)(2,1)S(1)}, u32[]{:S(2)}, u32[]{:S(2)}) collective-permute-start(bf16[392,128]{1,0:T(8,128)(2,1)S(1)} %get-tuple-element.47), channel_id=1, source_target_pairs={{0,24},{2,26},{4,28},{6,30},{8,16},{10,18},{12,20},{14,22},{16,8},... | collective-permute-start | bytes 301064 | tf_op jit(solution)/shard_map/ppermute | solution.py:278
  7.2 8.1 %collective-permute-start.11 = (bf16[392,128]{1,0:T(8,128)(2,1)S(1)}, bf16[392,128]{1,0:T(8,128)(2,1)S(1)}, u32[]{:S(2)}, u32[]{:S(2)}) collective-permute-start(bf16[392,128]{1,0:T(8,128)(2,1)S(1)} %get-tuple-element.48), channel_id=1, source_target_pairs={{0,8},{2,10},{4,12},{6,14},{8,0},{10,2},{12,4},{14,6},{16,24},{18,... | collective-permute-start | bytes 301064 | tf_op jit(solution)/shard_map/ppermute | solution.py:278
  7.2 10.8 %collective-permute-start.12 = (bf16[392,128]{1,0:T(8,128)(2,1)S(1)}, bf16[392,128]{1,0:T(8,128)(2,1)S(1)}, u32[]{:S(2)}, u32[]{:S(2)}) collective-permute-start(bf16[392,128]{1,0:T(8,128)(2,1)S(1)} %get-tuple-element.49), channel_id=1, source_target_pairs={{0,16},{2,18},{4,20},{6,22},{8,24},{10,26},{12,28},{14,30},{16,0},... | collective-permute-start | bytes 301064 | tf_op jit(solution)/shard_map/ppermute | solution.py:278
  7.8 12.8 %collective-permute-start.13 = (bf16[392,128]{1,0:T(8,128)(2,1)S(1)}, bf16[392,128]{1,0:T(8,128)(2,1)S(1)}, u32[]{:S(2)}, u32[]{:S(2)}) collective-permute-start(bf16[392,128]{1,0:T(8,128)(2,1)S(1)} %get-tuple-element.50), channel_id=1, source_target_pairs={{0,10},{2,8},{4,14},{6,12},{8,2},{10,0},{12,6},{14,4},{16,26},{18,... | collective-permute-start | bytes 301064 | tf_op jit(solution)/shard_map/ppermute | solution.py:278
  10.1 11.4 %collective-permute-start.14 = (bf16[392,128]{1,0:T(8,128)(2,1)S(1)}, bf16[392,128]{1,0:T(8,128)(2,1)S(1)}, u32[]{:S(2)}, u32[]{:S(2)}) collective-permute-start(bf16[392,128]{1,0:T(8,128)(2,1)S(1)} %get-tuple-element.51), channel_id=1, source_target_pairs={{0,26},{2,24},{4,30},{6,28},{8,18},{10,16},{12,22},{14,20},{16,10}... | collective-permute-start | bytes 301064 | tf_op jit(solution)/shard_map/ppermute | solution.py:278
  12.5 11.5 %collective-permute-start.7 = (bf16[392,128]{1,0:T(8,128)(2,1)S(1)}, bf16[392,128]{1,0:T(8,128)(2,1)S(1)}, u32[]{:S(2)}, u32[]{:S(2)}) collective-permute-start(bf16[392,128]{1,0:T(8,128)(2,1)S(1)} %get-tuple-element.44), channel_id=1, source_target_pairs={{0,12},{2,14},{4,8},{6,10},{8,4},{10,6},{12,0},{14,2},{16,28},{18,... | collective-permute-start | bytes 301064 | tf_op jit(solution)/shard_map/ppermute | solution.py:278
  15.3 11.1 %collective-permute-start.8 = (bf16[392,128]{1,0:T(8,128)(2,1)S(1)}, bf16[392,128]{1,0:T(8,128)(2,1)S(1)}, u32[]{:S(2)}, u32[]{:S(2)}) collective-permute-start(bf16[392,128]{1,0:T(8,128)(2,1)S(1)} %get-tuple-element.45), channel_id=1, source_target_pairs={{0,18},{2,16},{4,22},{6,20},{8,26},{10,24},{12,30},{14,28},{16,2},... | collective-permute-start | bytes 301064 | tf_op jit(solution)/shard_map/ppermute | solution.py:278
  17.9 10.6 %collective-permute-start.9 = (bf16[392,128]{1,0:T(8,128)(2,1)S(1)}, bf16[392,128]{1,0:T(8,128)(2,1)S(1)}, u32[]{:S(2)}, u32[]{:S(2)}) collective-permute-start(bf16[392,128]{1,0:T(8,128)(2,1)S(1)} %get-tuple-element.46), channel_id=1, source_target_pairs={{0,14},{2,12},{4,10},{6,8},{8,6},{10,4},{12,2},{14,0},{16,30},{18,... | collective-permute-start | bytes 301064 | tf_op jit(solution)/shard_map/ppermute | solution.py:278
  20.6 8.7 %collective-permute-start = (bf16[392,128]{1,0:T(8,128)(2,1)S(1)}, bf16[392,128]{1,0:T(8,128)(2,1)S(1)}, u32[]{:S(2)}, u32[]{:S(2)}) collective-permute-start(bf16[392,128]{1,0:T(8,128)(2,1)S(1)} %get-tuple-element.37), channel_id=1, source_target_pairs={{0,28},{2,30},{4,24},{6,26},{8,20},{10,22},{12,16},{14,18},{16,12}... | collective-permute-start | bytes 301064 | tf_op jit(solution)/shard_map/ppermute | solution.py:278
  21.5 10.1 %collective-permute-start.1 = (bf16[392,128]{1,0:T(8,128)(2,1)S(1)}, bf16[392,128]{1,0:T(8,128)(2,1)S(1)}, u32[]{:S(2)}, u32[]{:S(2)}) collective-permute-start(bf16[392,128]{1,0:T(8,128)(2,1)S(1)} %get-tuple-element.38), channel_id=1, source_target_pairs={{0,2},{2,0},{4,6},{6,4},{8,10},{10,8},{12,14},{14,12},{16,18},{18,... | collective-permute-start | bytes 301064 | tf_op jit(solution)/shard_map/ppermute | solution.py:278
  24.0 13.9 %collective-permute-start.2 = (bf16[392,128]{1,0:T(8,128)(2,1)S(1)}, bf16[392,128]{1,0:T(8,128)(2,1)S(1)}, u32[]{:S(2)}, u32[]{:S(2)}) collective-permute-start(bf16[392,128]{1,0:T(8,128)(2,1)S(1)} %get-tuple-element.39), channel_id=1, source_target_pairs={{0,20},{2,22},{4,16},{6,18},{8,28},{10,30},{12,24},{14,26},{16,4},... | collective-permute-start | bytes 301064 | tf_op jit(solution)/shard_map/ppermute | solution.py:278
  26.4 12.2 %collective-permute-start.3 = (bf16[392,128]{1,0:T(8,128)(2,1)S(1)}, bf16[392,128]{1,0:T(8,128)(2,1)S(1)}, u32[]{:S(2)}, u32[]{:S(2)}) collective-permute-start(bf16[392,128]{1,0:T(8,128)(2,1)S(1)} %get-tuple-element.40), channel_id=1, source_target_pairs={{0,4},{2,6},{4,0},{6,2},{8,12},{10,14},{12,8},{14,10},{16,20},{18,... | collective-permute-start | bytes 301064 | tf_op jit(solution)/shard_map/ppermute | solution.py:278
  28.5 10.0 %collective-permute-start.4 = (bf16[392,128]{1,0:T(8,128)(2,1)S(1)}, bf16[392,128]{1,0:T(8,128)(2,1)S(1)}, u32[]{:S(2)}, u32[]{:S(2)}) collective-permute-start(bf16[392,128]{1,0:T(8,128)(2,1)S(1)} %get-tuple-element.41), channel_id=1, source_target_pairs={{0,30},{2,28},{4,26},{6,24},{8,22},{10,20},{12,18},{14,16},{16,14}... | collective-permute-start | bytes 301064 | tf_op jit(solution)/shard_map/ppermute | solution.py:278
  29.3 9.3 %collective-permute-start.5 = (bf16[392,128]{1,0:T(8,128)(2,1)S(1)}, bf16[392,128]{1,0:T(8,128)(2,1)S(1)}, u32[]{:S(2)}, u32[]{:S(2)}) collective-permute-start(bf16[392,128]{1,0:T(8,128)(2,1)S(1)} %get-tuple-element.42), channel_id=1, source_target_pairs={{0,6},{2,4},{4,2},{6,0},{8,14},{10,12},{12,10},{14,8},{16,22},{18,... | collective-permute-start | bytes 301064 | tf_op jit(solution)/shard_map/ppermute | solution.py:278
  31.7 11.8 %collective-permute-start.6 = (bf16[392,128]{1,0:T(8,128)(2,1)S(1)}, bf16[392,128]{1,0:T(8,128)(2,1)S(1)}, u32[]{:S(2)}, u32[]{:S(2)}) collective-permute-start(bf16[392,128]{1,0:T(8,128)(2,1)S(1)} %get-tuple-element.43), channel_id=1, source_target_pairs={{0,22},{2,20},{4,18},{6,16},{8,30},{10,28},{12,26},{14,24},{16,6},... | collective-permute-start | bytes 301064 | tf_op jit(solution)/shard_map/ppermute | solution.py:278
  37.9 5.8 %collective-permute-start.16 = (bf16[512,896]{1,0:T(8,128)(2,1)S(1)}, bf16[512,896]{1,0:T(8,128)(2,1)S(1)}, u32[]{:S(2)}, u32[]{:S(2)}) collective-permute-start(bf16[512,896]{1,0:T(8,128)(2,1)S(1)} %get-tuple-element.52.refs_0_.refs_2_.refs_1_.refs_4_), channel_id=1, source_target_pairs={{0,1},{1,0},{2,3},{3,2},{4,5},{5,4},{6,7},{7,6},{8,9},{9,8},{10,11... | collective-permute-start | bytes 2752520 | tf_op jit(solution)/shard_map/ppermute | solution.py:281
  43.7 2.9 %collective-permute-start.15 = (bf16[512,896]{1,0:T(8,128)(2,1)S(1)}, bf16[512,896]{1,0:T(8,128)(2,1)S(1)}, u32[]{:S(2)}, u32[]{:S(2)}) collective-permute-start(bf16[512,896]{1,0:T(8,128)(2,1)S(1)} %get-tuple-element.54.refs_0_.refs_5_), channel_id=1, source_target_pairs={{0,1},{1,0},{2,3},{3,2},{4,5},{5,4},{6,7},{7,6},{8,9},{9,8},{10,11... | collective-permute-start | bytes 2752520 | tf_op jit(solution)/shard_map/ppermute | solution.py:281
  44.5 2.7 %collective-permute-start.17 = (f32[8,512]{1,0:T(8,128)S(1)}, f32[8,512]{1,0:T(8,128)S(1)}, u32[]{:S(2)}, u32[]{:S(2)}) collective-permute-start(f32[8,512]{1,0:T(8,128)S(1)} %get-tuple-element.59), channel_id=1, source_target_pairs={{0,1},{1,0},{2,3},{3,2},{4,5},{5,4},{6,7},{7,6},{8,9},{9,8},{10,11... | collective-permute-start | bytes 49160 | tf_op jit(solution)/shard_map/ppermute | solution.py:281

commit v3 on v2

--- a/solution.py
+++ b/solution.py
@@ -27,7 +27,7 @@
 def partners(nodes):
     half = nodes // 2
     quarter = half // 2
-    far = [flip for i in range(quarter) for flip in (half + quarter + i, half + i)]
+    far = [*range(half + quarter, nodes), *range(half, half + quarter)]
     near = [*range(quarter, half), *range(1, quarter)]
     sequence = [far[0]]
     for pair in zip(near, far[1:]):

time: 57.3 us -> 57.6 us (level)
  starting transfers between devices: 28.2 us -> 25.3 us
  waiting for transfers between devices: 12.1 us -> 14.9 us
    ppermute x15, starting transfers between devices: 27.6 us -> 24.7 us  [body(): lax.ppermute(messages[g], 'ingest', [(i, i ^ flips[g]) for i in range(nod...]
    ppermute x15, waiting for transfers between devices: 12.1 us -> 14.9 us  [body(): lax.ppermute(messages[g], 'ingest', [(i, i ^ flips[g]) for i in range(nod...]
  transfers between devices with their start and end apart: 18 -> 18, of which waited for: 6 -> 8; matrix products, arithmetic and copies ran while one was open for 0% -> 0% of each run, Pallas kernels for 8% -> 8%
where the time goes in v3:
time: 57.6 us; the launch traced here: 57.4 us
  starting transfers between devices  25.3 us (44%)
  waiting for transfers between devices  14.9 us (26%)
  blocking collectives  9.58 us (17%)
  Pallas kernels  6.56 us (11%)
  local copies, waits for them, and re-layouts  1 us (2%)
    ppermute x15, starting transfers between devices, body(): lax.ppermute(messages[g], 'ingest', [(i, i ^ flips[g]) for i in range(nod...  24.7 us
    ppermute x15, waiting for transfers between devices, body(): lax.ppermute(messages[g], 'ingest', [(i, i ^ flips[g]) for i in range(nod...  14.9 us
    all_to_all x1, blocking collectives, body(): lax.all_to_all(highest, 'ingest', split_axis=0, concat_axis=0, tiled=True...  9.58 us
    pallas_call x4, Pallas kernels, match(): pl.pallas_call(functools.partial(match_kernel, width=width, queries=len(g...  3.5 us
    pallas_call x2, Pallas kernels, body(): pl.pallas_call(functools.partial(pack_kernel, chosen=chosen, capacity=cap...  1.71 us
  transfers between devices with their start and end apart: 18, of which 8 were waited for; matrix products, arithmetic and copies ran while one was open for 0% of the time, Pallas kernels for 8%

profile of v3, /device:TPU:0, one launch (start us, length us, event | category | flops | bytes accessed | tf_op | source)
XLA Modules:
  0.0 57.4 jit_solution(4993429108622457625)
XLA Ops:
  0.0 0.7 %copy-done.2 = s32[512]{0:T(512)S(1)} copy-done((s32[512]{0:T(512)S(1)}, s32[512]{0:T(512)}, u32[]{:S(2)}) %copy-start.2) | copy-done | bytes 2072
  1.2 0.9 %shard_map.38 = (bf16[392,128]{1,0:T(8,128)(2,1)S(1)}, bf16[392,128]{1,0:T(8,128)(2,1)S(1)}, bf16[392,128]{1,0:T(8,128)(2,1)S(1)}, bf16[392,128]{1,0:T(8,128)(2,...) custom-call(bf16[512,768]{1,0:T(8,128)(2,1)S(1)} %copy-done.1, ...), custom_call_target="tpu_custom_call" | custom-call | flops 469762048 | bytes 4096 | tf_op jit(solution)/shard_map/pallas_call | solution.py:261
  2.1 5.1 %collective-permute-start.10 = (bf16[392,128]{1,0:T(8,128)(2,1)S(1)}, bf16[392,128]{1,0:T(8,128)(2,1)S(1)}, u32[]{:S(2)}, u32[]{:S(2)}) collective-permute-start(bf16[392,128]{1,0:T(8,128)(2,1)S(1)} %get-tuple-element.47), channel_id=1, source_target_pairs={{0,24},{2,26},{4,28},{6,30},{8,16},{10,18},{12,20},{14,22},{16,8},... | collective-permute-start | bytes 301064 | tf_op jit(solution)/shard_map/ppermute | solution.py:278
  7.2 1.8 %collective-permute-start.12 = (bf16[392,128]{1,0:T(8,128)(2,1)S(1)}, bf16[392,128]{1,0:T(8,128)(2,1)S(1)}, u32[]{:S(2)}, u32[]{:S(2)}) collective-permute-start(bf16[392,128]{1,0:T(8,128)(2,1)S(1)} %get-tuple-element.49), channel_id=1, source_target_pairs={{0,26},{2,24},{4,30},{6,28},{8,18},{10,16},{12,22},{14,20},{16,10}... | collective-permute-start | bytes 301064 | tf_op jit(solution)/shard_map/ppermute | solution.py:278
  9.0 1.1 %collective-permute-start.13 = (bf16[392,128]{1,0:T(8,128)(2,1)S(1)}, bf16[392,128]{1,0:T(8,128)(2,1)S(1)}, u32[]{:S(2)}, u32[]{:S(2)}) collective-permute-start(bf16[392,128]{1,0:T(8,128)(2,1)S(1)} %get-tuple-element.50), channel_id=1, source_target_pairs={{0,10},{2,8},{4,14},{6,12},{8,2},{10,0},{12,6},{14,4},{16,26},{18,... | collective-permute-start | bytes 301064 | tf_op jit(solution)/shard_map/ppermute | solution.py:278
  10.1 3.8 %collective-permute-start.14 = (bf16[392,128]{1,0:T(8,128)(2,1)S(1)}, bf16[392,128]{1,0:T(8,128)(2,1)S(1)}, u32[]{:S(2)}, u32[]{:S(2)}) collective-permute-start(bf16[392,128]{1,0:T(8,128)(2,1)S(1)} %get-tuple-element.51), channel_id=1, source_target_pairs={{0,28},{2,30},{4,24},{6,26},{8,20},{10,22},{12,16},{14,18},{16,12}... | collective-permute-start | bytes 301064 | tf_op jit(solution)/shard_map/ppermute | solution.py:278
  14.0 0.8 %shard_map.39 = (bf16[392,128]{1,0:T(8,128)(2,1)S(1)}, bf16[392,128]{1,0:T(8,128)(2,1)S(1)}, bf16[392,128]{1,0:T(8,128)(2,1)S(1)}, bf16[392,128]{1,0:T(8,128)(2,...) custom-call(bf16[512,896]{1,0:T(8,128)(2,1)S(1)} %get-tuple-element., ...), custom_call_target="tpu_custom_call" | custom-call | flops 469762048 | bytes 4096 | tf_op jit(solution)/shard_map/pallas_call | solution.py:261
  14.8 2.7 %collective-permute-start.8 = (bf16[392,128]{1,0:T(8,128)(2,1)S(1)}, bf16[392,128]{1,0:T(8,128)(2,1)S(1)}, u32[]{:S(2)}, u32[]{:S(2)}) collective-permute-start(bf16[392,128]{1,0:T(8,128)(2,1)S(1)} %get-tuple-element.45), channel_id=1, source_target_pairs={{0,30},{2,28},{4,26},{6,24},{8,22},{10,20},{12,18},{14,16},{16,14}... | collective-permute-start | bytes 301064 | tf_op jit(solution)/shard_map/ppermute | solution.py:278
  17.5 2.7 %collective-permute-start.9 = (bf16[392,128]{1,0:T(8,128)(2,1)S(1)}, bf16[392,128]{1,0:T(8,128)(2,1)S(1)}, u32[]{:S(2)}, u32[]{:S(2)}) collective-permute-start(bf16[392,128]{1,0:T(8,128)(2,1)S(1)} %get-tuple-element.46), channel_id=1, source_target_pairs={{0,14},{2,12},{4,10},{6,8},{8,6},{10,4},{12,2},{14,0},{16,30},{18,... | collective-permute-start | bytes 301064 | tf_op jit(solution)/shard_map/ppermute | solution.py:278
  20.4 1.1 %collective-permute-start = (bf16[392,128]{1,0:T(8,128)(2,1)S(1)}, bf16[392,128]{1,0:T(8,128)(2,1)S(1)}, u32[]{:S(2)}, u32[]{:S(2)}) collective-permute-start(bf16[392,128]{1,0:T(8,128)(2,1)S(1)} %get-tuple-element.37), channel_id=1, source_target_pairs={{0,16},{2,18},{4,20},{6,22},{8,24},{10,26},{12,28},{14,30},{16,0},... | collective-permute-start | bytes 301064 | tf_op jit(solution)/shard_map/ppermute | solution.py:278
  21.4 1.5 %collective-permute-start.1 = (bf16[392,128]{1,0:T(8,128)(2,1)S(1)}, bf16[392,128]{1,0:T(8,128)(2,1)S(1)}, u32[]{:S(2)}, u32[]{:S(2)}) collective-permute-start(bf16[392,128]{1,0:T(8,128)(2,1)S(1)} %get-tuple-element.38), channel_id=1, source_target_pairs={{0,2},{2,0},{4,6},{6,4},{8,10},{10,8},{12,14},{14,12},{16,18},{18,... | collective-permute-start | bytes 301064 | tf_op jit(solution)/shard_map/ppermute | solution.py:278
  22.9 2.2 %collective-permute-done.7.refs_0_ = bf16[392,128]{1,0:T(8,128)(2,1)S(1)} collective-permute-done((bf16[392,128]{1,0:T(8,128)(2,1)S(1)}, bf16[392,128]{1,0:T(8,128)(2,1)S(1)}, u32[]{:S(2)}, u32[]{:S(2)}) %collective-permute-start.7) | collective-permute-done | bytes 100384 | tf_op jit(solution)/shard_map/ppermute | solution.py:278
  25.1 0.8 %collective-permute-done.8.refs_1_ = bf16[392,128]{1,0:T(8,128)(2,1)S(1)} collective-permute-done((bf16[392,128]{1,0:T(8,128)(2,1)S(1)}, bf16[392,128]{1,0:T(8,128)(2,1)S(1)}, u32[]{:S(2)}, u32[]{:S(2)}) %collective-permute-start.8) | collective-permute-done | bytes 100384 | tf_op jit(solution)/shard_map/ppermute | solution.py:278
  26.4 1.6 %collective-permute-done.9.refs_2_ = bf16[392,128]{1,0:T(8,128)(2,1)S(1)} collective-permute-done((bf16[392,128]{1,0:T(8,128)(2,1)S(1)}, bf16[392,128]{1,0:T(8,128)(2,1)S(1)}, u32[]{:S(2)}, u32[]{:S(2)}) %collective-permute-start.9) | collective-permute-done | bytes 100384 | tf_op jit(solution)/shard_map/ppermute | solution.py:278
  28.0 2.2 %collective-permute-start.4 = (bf16[392,128]{1,0:T(8,128)(2,1)S(1)}, bf16[392,128]{1,0:T(8,128)(2,1)S(1)}, u32[]{:S(2)}, u32[]{:S(2)}) collective-permute-start(bf16[392,128]{1,0:T(8,128)(2,1)S(1)} %get-tuple-element.41), channel_id=1, source_target_pairs={{0,20},{2,22},{4,16},{6,18},{8,28},{10,30},{12,24},{14,26},{16,4},... | collective-permute-start | bytes 301064 | tf_op jit(solution)/shard_map/ppermute | solution.py:278
  30.2 2.3 %collective-permute-done.refs_1_ = bf16[392,128]{1,0:T(8,128)(2,1)S(1)} collective-permute-done((bf16[392,128]{1,0:T(8,128)(2,1)S(1)}, bf16[392,128]{1,0:T(8,128)(2,1)S(1)}, u32[]{:S(2)}, u32[]{:S(2)}) %collective-permute-start) | collective-permute-done | bytes 100384 | tf_op jit(solution)/shard_map/ppermute | solution.py:278
  32.5 2.2 %collective-permute-start.5 = (bf16[392,128]{1,0:T(8,128)(2,1)S(1)}, bf16[392,128]{1,0:T(8,128)(2,1)S(1)}, u32[]{:S(2)}, u32[]{:S(2)}) collective-permute-start(bf16[392,128]{1,0:T(8,128)(2,1)S(1)} %get-tuple-element.42), channel_id=1, source_target_pairs={{0,6},{2,4},{4,2},{6,0},{8,14},{10,12},{12,10},{14,8},{16,22},{18,... | collective-permute-start | bytes 301064 | tf_op jit(solution)/shard_map/ppermute | solution.py:278
  34.9 1.5 %collective-permute-done.2.refs_3_ = bf16[392,128]{1,0:T(8,128)(2,1)S(1)} collective-permute-done((bf16[392,128]{1,0:T(8,128)(2,1)S(1)}, bf16[392,128]{1,0:T(8,128)(2,1)S(1)}, u32[]{:S(2)}, u32[]{:S(2)}) %collective-permute-start.2) | collective-permute-done | bytes 100384 | tf_op jit(solution)/shard_map/ppermute | solution.py:278
  37.0 4.3 %collective-permute-done.4.refs_5_ = bf16[392,128]{1,0:T(8,128)(2,1)S(1)} collective-permute-done((bf16[392,128]{1,0:T(8,128)(2,1)S(1)}, bf16[392,128]{1,0:T(8,128)(2,1)S(1)}, u32[]{:S(2)}, u32[]{:S(2)}) %collective-permute-start.4) | collective-permute-done | bytes 100384 | tf_op jit(solution)/shard_map/ppermute | solution.py:278
  41.3 2.0 %collective-permute-done.6.refs_7_ = bf16[392,128]{1,0:T(8,128)(2,1)S(1)} collective-permute-done((bf16[392,128]{1,0:T(8,128)(2,1)S(1)}, bf16[392,128]{1,0:T(8,128)(2,1)S(1)}, u32[]{:S(2)}, u32[]{:S(2)}) %collective-permute-start.6) | collective-permute-done | bytes 100384 | tf_op jit(solution)/shard_map/ppermute | solution.py:278
  43.6 0.8 %shard_map.43 = (f32[8,512]{1,0:T(8,128)S(1)}, f32[8,512]{1,0:T(8,128)S(1)}) custom-call(bf16[512,896]{1,0:T(8,128)(2,1)S(1)} %get-tuple-element.54.refs_0_.refs_5_, f32[8,512]{1,0:T(8,128)S(1)} %get-tuple-element.55.refs_1_.refs_2_, bf16[512,896]{1,0:T(8,128)(2,1)S(1)} %collective-permute-done.16.refs_2_.refs_6_), custom_call_target="tpu_custom_call" | custom-call | flops 1 | bytes 1 | tf_op jit(solution)/shard_map/pallas_call | solution.py:193
  44.9 1.5 %shard_map.44 = (f32[8,512]{1,0:T(8,128)S(1)}, f32[8,512]{1,0:T(8,128)S(1)}) custom-call(bf16[512,896]{1,0:T(8,128)(2,1)S(1)} %get-tuple-element.54.refs_0_.refs_5_, bf16[512,896]{1,0:T(8,128)(2,1)S(1)} %get-tuple-element.52.refs_0_.refs_2_.refs_1_.refs_4_, f32[8,512]{1,0:T(8,128)S(1)} %get-tuple-element.55.refs_1_.refs_2_, ...), custom_call_target="tpu_custom_call" | custom-call | flops 1 | bytes 1 | tf_op jit(solution)/shard_map/pallas_call | solution.py:193
  47.2 9.6 %all_to_all.5.back_ref = f32[16,1,128]{2,1,0:T(1,128)S(1)} all-to-all(f32[16,1,128]{2,1,0:T(1,128)S(1)} %shard_map.46), channel_id=1, replica_groups={{30,28,26,24,22,20,18,16,14,12,10,8,6,4,2,0},{31,29,27,25,23,21,19,17,1..., dimensions={0} | all-to-all | bytes 16384 | tf_op jit(solution)/shard_map/all_to_all | solution.py:306
  56.8 0.7 %shard_map.47 = f32[1,512]{1,0:T(1,128)} custom-call(f32[16,1,128]{2,1,0:T(1,128)S(1)} %all_to_all.5.back_ref, s32[1,512]{1,0:T(1,128)S(1)} %bitcast.5, s32[1,512]{1,0:T(1,128)S(1)} %get-tuple-element.60.pos_ref), custom_call_target="tpu_custom_call" | custom-call | tf_op jit(solution)/shard_map/pallas_call | solution.py:314
  (30 shorter events, 3.6 us)
Async XLA Ops:
  0.0 0.7 %copy-start.2 = (s32[512]{0:T(512)S(1)}, s32[512]{0:T(512)}, u32[]{:S(2)}) copy-start(s32[512]{0:T(512)} %param.5) | copy-start | bytes 6148
  0.0 0.7 %copy-start = (s32[512]{0:T(512)S(1)}, s32[512]{0:T(512)}, u32[]{:S(2)}) copy-start(s32[512]{0:T(512)} %param.4) | copy-start | bytes 6148
  0.0 1.2 %copy-start.1 = (bf16[512,768]{1,0:T(8,128)(2,1)S(1)}, bf16[512,768]{1,0:T(8,128)(2,1)}, u32[]{:S(2)}) copy-start(bf16[512,768]{1,0:T(8,128)(2,1)} %rows_ref.1) | copy-start | bytes 2359300
  2.1 11.9 %collective-permute-start.10 = (bf16[392,128]{1,0:T(8,128)(2,1)S(1)}, bf16[392,128]{1,0:T(8,128)(2,1)S(1)}, u32[]{:S(2)}, u32[]{:S(2)}) collective-permute-start(bf16[392,128]{1,0:T(8,128)(2,1)S(1)} %get-tuple-element.47), channel_id=1, source_target_pairs={{0,24},{2,26},{4,28},{6,30},{8,16},{10,18},{12,20},{14,22},{16,8},... | collective-permute-start | bytes 301064 | tf_op jit(solution)/shard_map/ppermute | solution.py:278
  7.2 7.6 %collective-permute-start.11 = (bf16[392,128]{1,0:T(8,128)(2,1)S(1)}, bf16[392,128]{1,0:T(8,128)(2,1)S(1)}, u32[]{:S(2)}, u32[]{:S(2)}) collective-permute-start(bf16[392,128]{1,0:T(8,128)(2,1)S(1)} %get-tuple-element.48), channel_id=1, source_target_pairs={{0,8},{2,10},{4,12},{6,14},{8,0},{10,2},{12,4},{14,6},{16,24},{18,... | collective-permute-start | bytes 301064 | tf_op jit(solution)/shard_map/ppermute | solution.py:278
  7.2 10.3 %collective-permute-start.12 = (bf16[392,128]{1,0:T(8,128)(2,1)S(1)}, bf16[392,128]{1,0:T(8,128)(2,1)S(1)}, u32[]{:S(2)}, u32[]{:S(2)}) collective-permute-start(bf16[392,128]{1,0:T(8,128)(2,1)S(1)} %get-tuple-element.49), channel_id=1, source_target_pairs={{0,26},{2,24},{4,30},{6,28},{8,18},{10,16},{12,22},{14,20},{16,10}... | collective-permute-start | bytes 301064 | tf_op jit(solution)/shard_map/ppermute | solution.py:278
  9.0 11.4 %collective-permute-start.13 = (bf16[392,128]{1,0:T(8,128)(2,1)S(1)}, bf16[392,128]{1,0:T(8,128)(2,1)S(1)}, u32[]{:S(2)}, u32[]{:S(2)}) collective-permute-start(bf16[392,128]{1,0:T(8,128)(2,1)S(1)} %get-tuple-element.50), channel_id=1, source_target_pairs={{0,10},{2,8},{4,14},{6,12},{8,2},{10,0},{12,6},{14,4},{16,26},{18,... | collective-permute-start | bytes 301064 | tf_op jit(solution)/shard_map/ppermute | solution.py:278
  10.1 11.3 %collective-permute-start.14 = (bf16[392,128]{1,0:T(8,128)(2,1)S(1)}, bf16[392,128]{1,0:T(8,128)(2,1)S(1)}, u32[]{:S(2)}, u32[]{:S(2)}) collective-permute-start(bf16[392,128]{1,0:T(8,128)(2,1)S(1)} %get-tuple-element.51), channel_id=1, source_target_pairs={{0,28},{2,30},{4,24},{6,26},{8,20},{10,22},{12,16},{14,18},{16,12}... | collective-permute-start | bytes 301064 | tf_op jit(solution)/shard_map/ppermute | solution.py:278
  14.0 11.1 %collective-permute-start.7 = (bf16[392,128]{1,0:T(8,128)(2,1)S(1)}, bf16[392,128]{1,0:T(8,128)(2,1)S(1)}, u32[]{:S(2)}, u32[]{:S(2)}) collective-permute-start(bf16[392,128]{1,0:T(8,128)(2,1)S(1)} %get-tuple-element.44), channel_id=1, source_target_pairs={{0,12},{2,14},{4,8},{6,10},{8,4},{10,6},{12,0},{14,2},{16,28},{18,... | collective-permute-start | bytes 301064 | tf_op jit(solution)/shard_map/ppermute | solution.py:278
  14.8 11.1 %collective-permute-start.8 = (bf16[392,128]{1,0:T(8,128)(2,1)S(1)}, bf16[392,128]{1,0:T(8,128)(2,1)S(1)}, u32[]{:S(2)}, u32[]{:S(2)}) collective-permute-start(bf16[392,128]{1,0:T(8,128)(2,1)S(1)} %get-tuple-element.45), channel_id=1, source_target_pairs={{0,30},{2,28},{4,26},{6,24},{8,22},{10,20},{12,18},{14,16},{16,14}... | collective-permute-start | bytes 301064 | tf_op jit(solution)/shard_map/ppermute | solution.py:278
  17.5 10.5 %collective-permute-start.9 = (bf16[392,128]{1,0:T(8,128)(2,1)S(1)}, bf16[392,128]{1,0:T(8,128)(2,1)S(1)}, u32[]{:S(2)}, u32[]{:S(2)}) collective-permute-start(bf16[392,128]{1,0:T(8,128)(2,1)S(1)} %get-tuple-element.46), channel_id=1, source_target_pairs={{0,14},{2,12},{4,10},{6,8},{8,6},{10,4},{12,2},{14,0},{16,30},{18,... | collective-permute-start | bytes 301064 | tf_op jit(solution)/shard_map/ppermute | solution.py:278
  20.4 12.1 %collective-permute-start = (bf16[392,128]{1,0:T(8,128)(2,1)S(1)}, bf16[392,128]{1,0:T(8,128)(2,1)S(1)}, u32[]{:S(2)}, u32[]{:S(2)}) collective-permute-start(bf16[392,128]{1,0:T(8,128)(2,1)S(1)} %get-tuple-element.37), channel_id=1, source_target_pairs={{0,16},{2,18},{4,20},{6,22},{8,24},{10,26},{12,28},{14,30},{16,0},... | collective-permute-start | bytes 301064 | tf_op jit(solution)/shard_map/ppermute | solution.py:278
  21.4 13.2 %collective-permute-start.1 = (bf16[392,128]{1,0:T(8,128)(2,1)S(1)}, bf16[392,128]{1,0:T(8,128)(2,1)S(1)}, u32[]{:S(2)}, u32[]{:S(2)}) collective-permute-start(bf16[392,128]{1,0:T(8,128)(2,1)S(1)} %get-tuple-element.38), channel_id=1, source_target_pairs={{0,2},{2,0},{4,6},{6,4},{8,10},{10,8},{12,14},{14,12},{16,18},{18,... | collective-permute-start | bytes 301064 | tf_op jit(solution)/shard_map/ppermute | solution.py:278
  25.1 11.3 %collective-permute-start.2 = (bf16[392,128]{1,0:T(8,128)(2,1)S(1)}, bf16[392,128]{1,0:T(8,128)(2,1)S(1)}, u32[]{:S(2)}, u32[]{:S(2)}) collective-permute-start(bf16[392,128]{1,0:T(8,128)(2,1)S(1)} %get-tuple-element.39), channel_id=1, source_target_pairs={{0,18},{2,16},{4,22},{6,20},{8,26},{10,24},{12,30},{14,28},{16,2},... | collective-permute-start | bytes 301064 | tf_op jit(solution)/shard_map/ppermute | solution.py:278
  25.9 11.1 %collective-permute-start.3 = (bf16[392,128]{1,0:T(8,128)(2,1)S(1)}, bf16[392,128]{1,0:T(8,128)(2,1)S(1)}, u32[]{:S(2)}, u32[]{:S(2)}) collective-permute-start(bf16[392,128]{1,0:T(8,128)(2,1)S(1)} %get-tuple-element.40), channel_id=1, source_target_pairs={{0,4},{2,6},{4,0},{6,2},{8,12},{10,14},{12,8},{14,10},{16,20},{18,... | collective-permute-start | bytes 301064 | tf_op jit(solution)/shard_map/ppermute | solution.py:278
  28.0 13.2 %collective-permute-start.4 = (bf16[392,128]{1,0:T(8,128)(2,1)S(1)}, bf16[392,128]{1,0:T(8,128)(2,1)S(1)}, u32[]{:S(2)}, u32[]{:S(2)}) collective-permute-start(bf16[392,128]{1,0:T(8,128)(2,1)S(1)} %get-tuple-element.41), channel_id=1, source_target_pairs={{0,20},{2,22},{4,16},{6,18},{8,28},{10,30},{12,24},{14,26},{16,4},... | collective-permute-start | bytes 301064 | tf_op jit(solution)/shard_map/ppermute | solution.py:278
  32.5 8.8 %collective-permute-start.5 = (bf16[392,128]{1,0:T(8,128)(2,1)S(1)}, bf16[392,128]{1,0:T(8,128)(2,1)S(1)}, u32[]{:S(2)}, u32[]{:S(2)}) collective-permute-start(bf16[392,128]{1,0:T(8,128)(2,1)S(1)} %get-tuple-element.42), channel_id=1, source_target_pairs={{0,6},{2,4},{4,2},{6,0},{8,14},{10,12},{12,10},{14,8},{16,22},{18,... | collective-permute-start | bytes 301064 | tf_op jit(solution)/shard_map/ppermute | solution.py:278
  34.7 8.6 %collective-permute-start.6 = (bf16[392,128]{1,0:T(8,128)(2,1)S(1)}, bf16[392,128]{1,0:T(8,128)(2,1)S(1)}, u32[]{:S(2)}, u32[]{:S(2)}) collective-permute-start(bf16[392,128]{1,0:T(8,128)(2,1)S(1)} %get-tuple-element.43), channel_id=1, source_target_pairs={{0,22},{2,20},{4,18},{6,16},{8,30},{10,28},{12,26},{14,24},{16,6},... | collective-permute-start | bytes 301064 | tf_op jit(solution)/shard_map/ppermute | solution.py:278
  36.4 7.2 %collective-permute-start.16 = (bf16[512,896]{1,0:T(8,128)(2,1)S(1)}, bf16[512,896]{1,0:T(8,128)(2,1)S(1)}, u32[]{:S(2)}, u32[]{:S(2)}) collective-permute-start(bf16[512,896]{1,0:T(8,128)(2,1)S(1)} %get-tuple-element.52.refs_0_.refs_2_.refs_1_.refs_4_), channel_id=1, source_target_pairs={{0,1},{1,0},{2,3},{3,2},{4,5},{5,4},{6,7},{7,6},{8,9},{9,8},{10,11... | collective-permute-start | bytes 2752520 | tf_op jit(solution)/shard_map/ppermute | solution.py:281
  43.5 2.9 %collective-permute-start.15 = (bf16[512,896]{1,0:T(8,128)(2,1)S(1)}, bf16[512,896]{1,0:T(8,128)(2,1)S(1)}, u32[]{:S(2)}, u32[]{:S(2)}) collective-permute-start(bf16[512,896]{1,0:T(8,128)(2,1)S(1)} %get-tuple-element.54.refs_0_.refs_5_), channel_id=1, source_target_pairs={{0,1},{1,0},{2,3},{3,2},{4,5},{5,4},{6,7},{7,6},{8,9},{9,8},{10,11... | collective-permute-start | bytes 2752520 | tf_op jit(solution)/shard_map/ppermute | solution.py:281
  44.4 2.7 %collective-permute-start.17 = (f32[8,512]{1,0:T(8,128)S(1)}, f32[8,512]{1,0:T(8,128)S(1)}, u32[]{:S(2)}, u32[]{:S(2)}) collective-permute-start(f32[8,512]{1,0:T(8,128)S(1)} %get-tuple-element.59), channel_id=1, source_target_pairs={{0,1},{1,0},{2,3},{3,2},{4,5},{5,4},{6,7},{7,6},{8,9},{9,8},{10,11... | collective-permute-start | bytes 49160 | tf_op jit(solution)/shard_map/ppermute | solution.py:281

commit v4 on v2

--- a/solution.py
+++ b/solution.py
@@ -8,7 +8,7 @@
 from jax.sharding import PartitionSpec as P
 
 LANES = 128
-EXTRA = 8
+EXTRA = 16
 NEVER = 2.0**24
 TILE = 512
 PARAMS = pltpu.CompilerParams(vmem_limit_bytes=40 * 2**20)

time: 57.3 us -> 58 us (1.012)
  starting transfers between devices: 28.2 us -> 29.4 us
    ppermute x15, starting transfers between devices: 27.6 us -> 28.7 us  [body(): lax.ppermute(messages[g], 'ingest', [(i, i ^ flips[g]) for i in range(nod...]
  transfers between devices with their start and end apart: 18 -> 18, of which waited for: 6 -> 5; matrix products, arithmetic and copies ran while one was open for 0% -> 0% of each run, Pallas kernels for 8% -> 8%
where the time goes in v4:
time: 58 us; the launch traced here: 57.9 us
  starting transfers between devices  29.4 us (51%)
  waiting for transfers between devices  11.7 us (20%)
  blocking collectives  9.07 us (16%)
  Pallas kernels  6.56 us (11%)
  local copies, waits for them, and re-layouts  1 us (2%)
    ppermute x15, starting transfers between devices, body(): lax.ppermute(messages[g], 'ingest', [(i, i ^ flips[g]) for i in range(nod...  28.7 us
    ppermute x15, waiting for transfers between devices, body(): lax.ppermute(messages[g], 'ingest', [(i, i ^ flips[g]) for i in range(nod...  11.7 us
    all_to_all x1, blocking collectives, body(): lax.all_to_all(highest, 'ingest', split_axis=0, concat_axis=0, tiled=True...  9.07 us
    pallas_call x4, Pallas kernels, match(): pl.pallas_call(functools.partial(match_kernel, width=width, queries=len(g...  3.51 us
    pallas_call x2, Pallas kernels, body(): pl.pallas_call(functools.partial(pack_kernel, chosen=chosen, capacity=cap...  1.7 us
  transfers between devices with their start and end apart: 18, of which 5 were waited for; matrix products, arithmetic and copies ran while one was open for 0% of the time, Pallas kernels for 8%

profile of v4, /device:TPU:0, one launch (start us, length us, event | category | flops | bytes accessed | tf_op | source)
XLA Modules:
  0.0 57.9 jit_solution(14853099381095277186)
XLA Ops:
  0.0 0.7 %copy-done.2 = s32[512]{0:T(512)S(1)} copy-done((s32[512]{0:T(512)S(1)}, s32[512]{0:T(512)}, u32[]{:S(2)}) %copy-start.2) | copy-done | bytes 2072
  1.2 0.9 %shard_map.38 = (bf16[400,128]{1,0:T(8,128)(2,1)S(1)}, bf16[400,128]{1,0:T(8,128)(2,1)S(1)}, bf16[400,128]{1,0:T(8,128)(2,1)S(1)}, bf16[400,128]{1,0:T(8,128)(2,...) custom-call(bf16[512,768]{1,0:T(8,128)(2,1)S(1)} %copy-done.1, ...), custom_call_target="tpu_custom_call" | custom-call | flops 469762048 | bytes 4096 | tf_op jit(solution)/shard_map/pallas_call | solution.py:261
  2.1 5.1 %collective-permute-start.10 = (bf16[400,128]{1,0:T(8,128)(2,1)S(1)}, bf16[400,128]{1,0:T(8,128)(2,1)S(1)}, u32[]{:S(2)}, u32[]{:S(2)}) collective-permute-start(bf16[400,128]{1,0:T(8,128)(2,1)S(1)} %get-tuple-element.47), channel_id=1, source_target_pairs={{0,24},{2,26},{4,28},{6,30},{8,16},{10,18},{12,20},{14,22},{16,8},... | collective-permute-start | bytes 307208 | tf_op jit(solution)/shard_map/ppermute | solution.py:278
  7.2 0.6 %collective-permute-start.12 = (bf16[400,128]{1,0:T(8,128)(2,1)S(1)}, bf16[400,128]{1,0:T(8,128)(2,1)S(1)}, u32[]{:S(2)}, u32[]{:S(2)}) collective-permute-start(bf16[400,128]{1,0:T(8,128)(2,1)S(1)} %get-tuple-element.49), channel_id=1, source_target_pairs={{0,16},{2,18},{4,20},{6,22},{8,24},{10,26},{12,28},{14,30},{16,0},... | collective-permute-start | bytes 307208 | tf_op jit(solution)/shard_map/ppermute | solution.py:278
  7.8 2.3 %collective-permute-start.13 = (bf16[400,128]{1,0:T(8,128)(2,1)S(1)}, bf16[400,128]{1,0:T(8,128)(2,1)S(1)}, u32[]{:S(2)}, u32[]{:S(2)}) collective-permute-start(bf16[400,128]{1,0:T(8,128)(2,1)S(1)} %get-tuple-element.50), channel_id=1, source_target_pairs={{0,10},{2,8},{4,14},{6,12},{8,2},{10,0},{12,6},{14,4},{16,26},{18,... | collective-permute-start | bytes 307208 | tf_op jit(solution)/shard_map/ppermute | solution.py:278
  10.1 2.4 %collective-permute-start.14 = (bf16[400,128]{1,0:T(8,128)(2,1)S(1)}, bf16[400,128]{1,0:T(8,128)(2,1)S(1)}, u32[]{:S(2)}, u32[]{:S(2)}) collective-permute-start(bf16[400,128]{1,0:T(8,128)(2,1)S(1)} %get-tuple-element.51), channel_id=1, source_target_pairs={{0,26},{2,24},{4,30},{6,28},{8,18},{10,16},{12,22},{14,20},{16,10}... | collective-permute-start | bytes 307208 | tf_op jit(solution)/shard_map/ppermute | solution.py:278
  12.5 2.1 %collective-permute-start.7 = (bf16[400,128]{1,0:T(8,128)(2,1)S(1)}, bf16[400,128]{1,0:T(8,128)(2,1)S(1)}, u32[]{:S(2)}, u32[]{:S(2)}) collective-permute-start(bf16[400,128]{1,0:T(8,128)(2,1)S(1)} %get-tuple-element.44), channel_id=1, source_target_pairs={{0,12},{2,14},{4,8},{6,10},{8,4},{10,6},{12,0},{14,2},{16,28},{18,... | collective-permute-start | bytes 307208 | tf_op jit(solution)/shard_map/ppermute | solution.py:278
  14.6 0.8 %shard_map.39 = (bf16[400,128]{1,0:T(8,128)(2,1)S(1)}, bf16[400,128]{1,0:T(8,128)(2,1)S(1)}, bf16[400,128]{1,0:T(8,128)(2,1)S(1)}, bf16[400,128]{1,0:T(8,128)(2,...) custom-call(bf16[512,896]{1,0:T(8,128)(2,1)S(1)} %get-tuple-element., ...), custom_call_target="tpu_custom_call" | custom-call | flops 469762048 | bytes 4096 | tf_op jit(solution)/shard_map/pallas_call | solution.py:261
  15.3 2.7 %collective-permute-start.8 = (bf16[400,128]{1,0:T(8,128)(2,1)S(1)}, bf16[400,128]{1,0:T(8,128)(2,1)S(1)}, u32[]{:S(2)}, u32[]{:S(2)}) collective-permute-start(bf16[400,128]{1,0:T(8,128)(2,1)S(1)} %get-tuple-element.45), channel_id=1, source_target_pairs={{0,18},{2,16},{4,22},{6,20},{8,26},{10,24},{12,30},{14,28},{16,2},... | collective-permute-start | bytes 307208 | tf_op jit(solution)/shard_map/ppermute | solution.py:278
  18.3 2.5 %collective-permute-done.13.refs_6_ = bf16[400,128]{1,0:T(8,128)(2,1)S(1)} collective-permute-done((bf16[400,128]{1,0:T(8,128)(2,1)S(1)}, bf16[400,128]{1,0:T(8,128)(2,1)S(1)}, u32[]{:S(2)}, u32[]{:S(2)}) %collective-permute-start.13) | collective-permute-done | bytes 102432 | tf_op jit(solution)/shard_map/ppermute | solution.py:278
  20.8 0.8 %collective-permute-start = (bf16[400,128]{1,0:T(8,128)(2,1)S(1)}, bf16[400,128]{1,0:T(8,128)(2,1)S(1)}, u32[]{:S(2)}, u32[]{:S(2)}) collective-permute-start(bf16[400,128]{1,0:T(8,128)(2,1)S(1)} %get-tuple-element.37), channel_id=1, source_target_pairs={{0,28},{2,30},{4,24},{6,26},{8,20},{10,22},{12,16},{14,18},{16,12}... | collective-permute-start | bytes 307208 | tf_op jit(solution)/shard_map/ppermute | solution.py:278
  21.5 1.5 %collective-permute-start.1 = (bf16[400,128]{1,0:T(8,128)(2,1)S(1)}, bf16[400,128]{1,0:T(8,128)(2,1)S(1)}, u32[]{:S(2)}, u32[]{:S(2)}) collective-permute-start(bf16[400,128]{1,0:T(8,128)(2,1)S(1)} %get-tuple-element.38), channel_id=1, source_target_pairs={{0,2},{2,0},{4,6},{6,4},{8,10},{10,8},{12,14},{14,12},{16,18},{18,... | collective-permute-start | bytes 307208 | tf_op jit(solution)/shard_map/ppermute | solution.py:278
  23.1 1.0 %collective-permute-done.7.refs_0_ = bf16[400,128]{1,0:T(8,128)(2,1)S(1)} collective-permute-done((bf16[400,128]{1,0:T(8,128)(2,1)S(1)}, bf16[400,128]{1,0:T(8,128)(2,1)S(1)}, u32[]{:S(2)}, u32[]{:S(2)}) %collective-permute-start.7) | collective-permute-done | bytes 102432 | tf_op jit(solution)/shard_map/ppermute | solution.py:278
  24.1 2.7 %collective-permute-done.8.refs_1_ = bf16[400,128]{1,0:T(8,128)(2,1)S(1)} collective-permute-done((bf16[400,128]{1,0:T(8,128)(2,1)S(1)}, bf16[400,128]{1,0:T(8,128)(2,1)S(1)}, u32[]{:S(2)}, u32[]{:S(2)}) %collective-permute-start.8) | collective-permute-done | bytes 102432 | tf_op jit(solution)/shard_map/ppermute | solution.py:278
  26.7 1.5 %collective-permute-start.3 = (bf16[400,128]{1,0:T(8,128)(2,1)S(1)}, bf16[400,128]{1,0:T(8,128)(2,1)S(1)}, u32[]{:S(2)}, u32[]{:S(2)}) collective-permute-start(bf16[400,128]{1,0:T(8,128)(2,1)S(1)} %get-tuple-element.40), channel_id=1, source_target_pairs={{0,4},{2,6},{4,0},{6,2},{8,12},{10,14},{12,8},{14,10},{16,20},{18,... | collective-permute-start | bytes 307208 | tf_op jit(solution)/shard_map/ppermute | solution.py:278
  28.3 0.7 %collective-permute-done.9.refs_2_ = bf16[400,128]{1,0:T(8,128)(2,1)S(1)} collective-permute-done((bf16[400,128]{1,0:T(8,128)(2,1)S(1)}, bf16[400,128]{1,0:T(8,128)(2,1)S(1)}, u32[]{:S(2)}, u32[]{:S(2)}) %collective-permute-start.9) | collective-permute-done | bytes 102432 | tf_op jit(solution)/shard_map/ppermute | solution.py:278
  28.9 0.6 %collective-permute-start.4 = (bf16[400,128]{1,0:T(8,128)(2,1)S(1)}, bf16[400,128]{1,0:T(8,128)(2,1)S(1)}, u32[]{:S(2)}, u32[]{:S(2)}) collective-permute-start(bf16[400,128]{1,0:T(8,128)(2,1)S(1)} %get-tuple-element.41), channel_id=1, source_target_pairs={{0,30},{2,28},{4,26},{6,24},{8,22},{10,20},{12,18},{14,16},{16,14}... | collective-permute-start | bytes 307208 | tf_op jit(solution)/shard_map/ppermute | solution.py:278
  29.6 2.4 %collective-permute-start.5 = (bf16[400,128]{1,0:T(8,128)(2,1)S(1)}, bf16[400,128]{1,0:T(8,128)(2,1)S(1)}, u32[]{:S(2)}, u32[]{:S(2)}) collective-permute-start(bf16[400,128]{1,0:T(8,128)(2,1)S(1)} %get-tuple-element.42), channel_id=1, source_target_pairs={{0,6},{2,4},{4,2},{6,0},{8,14},{10,12},{12,10},{14,8},{16,22},{18,... | collective-permute-start | bytes 307208 | tf_op jit(solution)/shard_map/ppermute | solution.py:278
  32.0 6.5 %collective-permute-start.6 = (bf16[400,128]{1,0:T(8,128)(2,1)S(1)}, bf16[400,128]{1,0:T(8,128)(2,1)S(1)}, u32[]{:S(2)}, u32[]{:S(2)}) collective-permute-start(bf16[400,128]{1,0:T(8,128)(2,1)S(1)} %get-tuple-element.43), channel_id=1, source_target_pairs={{0,22},{2,20},{4,18},{6,16},{8,30},{10,28},{12,26},{14,24},{16,6},... | collective-permute-start | bytes 307208 | tf_op jit(solution)/shard_map/ppermute | solution.py:278
  39.5 4.8 %collective-permute-done.6.refs_7_ = bf16[400,128]{1,0:T(8,128)(2,1)S(1)} collective-permute-done((bf16[400,128]{1,0:T(8,128)(2,1)S(1)}, bf16[400,128]{1,0:T(8,128)(2,1)S(1)}, u32[]{:S(2)}, u32[]{:S(2)}) %collective-permute-start.6) | collective-permute-done | bytes 102432 | tf_op jit(solution)/shard_map/ppermute | solution.py:278
  44.6 0.8 %shard_map.43 = (f32[8,512]{1,0:T(8,128)S(1)}, f32[8,512]{1,0:T(8,128)S(1)}) custom-call(bf16[512,896]{1,0:T(8,128)(2,1)S(1)} %get-tuple-element.54.refs_0_.refs_5_, f32[8,512]{1,0:T(8,128)S(1)} %get-tuple-element.55.refs_1_.refs_2_, bf16[512,896]{1,0:T(8,128)(2,1)S(1)} %collective-permute-done.16.refs_2_.refs_6_), custom_call_target="tpu_custom_call" | custom-call | flops 1 | bytes 1 | tf_op jit(solution)/shard_map/pallas_call | solution.py:193
  45.9 1.5 %shard_map.44 = (f32[8,512]{1,0:T(8,128)S(1)}, f32[8,512]{1,0:T(8,128)S(1)}) custom-call(bf16[512,896]{1,0:T(8,128)(2,1)S(1)} %get-tuple-element.54.refs_0_.refs_5_, bf16[512,896]{1,0:T(8,128)(2,1)S(1)} %get-tuple-element.52.refs_0_.refs_2_.refs_1_.refs_4_, f32[8,512]{1,0:T(8,128)S(1)} %get-tuple-element.55.refs_1_.refs_2_, ...), custom_call_target="tpu_custom_call" | custom-call | flops 1 | bytes 1 | tf_op jit(solution)/shard_map/pallas_call | solution.py:193
  48.1 9.1 %all_to_all.5.back_ref = f32[16,1,128]{2,1,0:T(1,128)S(1)} all-to-all(f32[16,1,128]{2,1,0:T(1,128)S(1)} %shard_map.46), channel_id=1, replica_groups={{30,28,26,24,22,20,18,16,14,12,10,8,6,4,2,0},{31,29,27,25,23,21,19,17,1..., dimensions={0} | all-to-all | bytes 16384 | tf_op jit(solution)/shard_map/all_to_all | solution.py:306
  57.2 0.7 %shard_map.47 = f32[1,512]{1,0:T(1,128)} custom-call(f32[16,1,128]{2,1,0:T(1,128)S(1)} %all_to_all.5.back_ref, s32[1,512]{1,0:T(1,128)S(1)} %bitcast.5, s32[1,512]{1,0:T(1,128)S(1)} %get-tuple-element.60.pos_ref), custom_call_target="tpu_custom_call" | custom-call | tf_op jit(solution)/shard_map/pallas_call | solution.py:314
  (30 shorter events, 3.2 us)
Async XLA Ops:
  0.0 0.7 %copy-start.2 = (s32[512]{0:T(512)S(1)}, s32[512]{0:T(512)}, u32[]{:S(2)}) copy-start(s32[512]{0:T(512)} %param.5) | copy-start | bytes 6148
  0.0 0.7 %copy-start = (s32[512]{0:T(512)S(1)}, s32[512]{0:T(512)}, u32[]{:S(2)}) copy-start(s32[512]{0:T(512)} %param.4) | copy-start | bytes 6148
  0.0 1.2 %copy-start.1 = (bf16[512,768]{1,0:T(8,128)(2,1)S(1)}, bf16[512,768]{1,0:T(8,128)(2,1)}, u32[]{:S(2)}) copy-start(bf16[512,768]{1,0:T(8,128)(2,1)} %rows_ref.1) | copy-start | bytes 2359300
  2.1 10.4 %collective-permute-start.10 = (bf16[400,128]{1,0:T(8,128)(2,1)S(1)}, bf16[400,128]{1,0:T(8,128)(2,1)S(1)}, u32[]{:S(2)}, u32[]{:S(2)}) collective-permute-start(bf16[400,128]{1,0:T(8,128)(2,1)S(1)} %get-tuple-element.47), channel_id=1, source_target_pairs={{0,24},{2,26},{4,28},{6,30},{8,16},{10,18},{12,20},{14,22},{16,8},... | collective-permute-start | bytes 307208 | tf_op jit(solution)/shard_map/ppermute | solution.py:278
  7.2 8.1 %collective-permute-start.11 = (bf16[400,128]{1,0:T(8,128)(2,1)S(1)}, bf16[400,128]{1,0:T(8,128)(2,1)S(1)}, u32[]{:S(2)}, u32[]{:S(2)}) collective-permute-start(bf16[400,128]{1,0:T(8,128)(2,1)S(1)} %get-tuple-element.48), channel_id=1, source_target_pairs={{0,8},{2,10},{4,12},{6,14},{8,0},{10,2},{12,4},{14,6},{16,24},{18,... | collective-permute-start | bytes 307208 | tf_op jit(solution)/shard_map/ppermute | solution.py:278
  7.2 10.8 %collective-permute-start.12 = (bf16[400,128]{1,0:T(8,128)(2,1)S(1)}, bf16[400,128]{1,0:T(8,128)(2,1)S(1)}, u32[]{:S(2)}, u32[]{:S(2)}) collective-permute-start(bf16[400,128]{1,0:T(8,128)(2,1)S(1)} %get-tuple-element.49), channel_id=1, source_target_pairs={{0,16},{2,18},{4,20},{6,22},{8,24},{10,26},{12,28},{14,30},{16,0},... | collective-permute-start | bytes 307208 | tf_op jit(solution)/shard_map/ppermute | solution.py:278
  7.8 13.0 %collective-permute-start.13 = (bf16[400,128]{1,0:T(8,128)(2,1)S(1)}, bf16[400,128]{1,0:T(8,128)(2,1)S(1)}, u32[]{:S(2)}, u32[]{:S(2)}) collective-permute-start(bf16[400,128]{1,0:T(8,128)(2,1)S(1)} %get-tuple-element.50), channel_id=1, source_target_pairs={{0,10},{2,8},{4,14},{6,12},{8,2},{10,0},{12,6},{14,4},{16,26},{18,... | collective-permute-start | bytes 307208 | tf_op jit(solution)/shard_map/ppermute | solution.py:278
  10.1 11.4 %collective-permute-start.14 = (bf16[400,128]{1,0:T(8,128)(2,1)S(1)}, bf16[400,128]{1,0:T(8,128)(2,1)S(1)}, u32[]{:S(2)}, u32[]{:S(2)}) collective-permute-start(bf16[400,128]{1,0:T(8,128)(2,1)S(1)} %get-tuple-element.51), channel_id=1, source_target_pairs={{0,26},{2,24},{4,30},{6,28},{8,18},{10,16},{12,22},{14,20},{16,10}... | collective-permute-start | bytes 307208 | tf_op jit(solution)/shard_map/ppermute | solution.py:278
  12.5 11.6 %collective-permute-start.7 = (bf16[400,128]{1,0:T(8,128)(2,1)S(1)}, bf16[400,128]{1,0:T(8,128)(2,1)S(1)}, u32[]{:S(2)}, u32[]{:S(2)}) collective-permute-start(bf16[400,128]{1,0:T(8,128)(2,1)S(1)} %get-tuple-element.44), channel_id=1, source_target_pairs={{0,12},{2,14},{4,8},{6,10},{8,4},{10,6},{12,0},{14,2},{16,28},{18,... | collective-permute-start | bytes 307208 | tf_op jit(solution)/shard_map/ppermute | solution.py:278
  15.3 11.4 %collective-permute-start.8 = (bf16[400,128]{1,0:T(8,128)(2,1)S(1)}, bf16[400,128]{1,0:T(8,128)(2,1)S(1)}, u32[]{:S(2)}, u32[]{:S(2)}) collective-permute-start(bf16[400,128]{1,0:T(8,128)(2,1)S(1)} %get-tuple-element.45), channel_id=1, source_target_pairs={{0,18},{2,16},{4,22},{6,20},{8,26},{10,24},{12,30},{14,28},{16,2},... | collective-permute-start | bytes 307208 | tf_op jit(solution)/shard_map/ppermute | solution.py:278
  18.0 10.9 %collective-permute-start.9 = (bf16[400,128]{1,0:T(8,128)(2,1)S(1)}, bf16[400,128]{1,0:T(8,128)(2,1)S(1)}, u32[]{:S(2)}, u32[]{:S(2)}) collective-permute-start(bf16[400,128]{1,0:T(8,128)(2,1)S(1)} %get-tuple-element.46), channel_id=1, source_target_pairs={{0,14},{2,12},{4,10},{6,8},{8,6},{10,4},{12,2},{14,0},{16,30},{18,... | collective-permute-start | bytes 307208 | tf_op jit(solution)/shard_map/ppermute | solution.py:278
  20.8 8.8 %collective-permute-start = (bf16[400,128]{1,0:T(8,128)(2,1)S(1)}, bf16[400,128]{1,0:T(8,128)(2,1)S(1)}, u32[]{:S(2)}, u32[]{:S(2)}) collective-permute-start(bf16[400,128]{1,0:T(8,128)(2,1)S(1)} %get-tuple-element.37), channel_id=1, source_target_pairs={{0,28},{2,30},{4,24},{6,26},{8,20},{10,22},{12,16},{14,18},{16,12}... | collective-permute-start | bytes 307208 | tf_op jit(solution)/shard_map/ppermute | solution.py:278
  21.5 10.4 %collective-permute-start.1 = (bf16[400,128]{1,0:T(8,128)(2,1)S(1)}, bf16[400,128]{1,0:T(8,128)(2,1)S(1)}, u32[]{:S(2)}, u32[]{:S(2)}) collective-permute-start(bf16[400,128]{1,0:T(8,128)(2,1)S(1)} %get-tuple-element.38), channel_id=1, source_target_pairs={{0,2},{2,0},{4,6},{6,4},{8,10},{10,8},{12,14},{14,12},{16,18},{18,... | collective-permute-start | bytes 307208 | tf_op jit(solution)/shard_map/ppermute | solution.py:278
  24.1 14.6 %collective-permute-start.2 = (bf16[400,128]{1,0:T(8,128)(2,1)S(1)}, bf16[400,128]{1,0:T(8,128)(2,1)S(1)}, u32[]{:S(2)}, u32[]{:S(2)}) collective-permute-start(bf16[400,128]{1,0:T(8,128)(2,1)S(1)} %get-tuple-element.39), channel_id=1, source_target_pairs={{0,20},{2,22},{4,16},{6,18},{8,28},{10,30},{12,24},{14,26},{16,4},... | collective-permute-start | bytes 307208 | tf_op jit(solution)/shard_map/ppermute | solution.py:278
  26.7 12.7 %collective-permute-start.3 = (bf16[400,128]{1,0:T(8,128)(2,1)S(1)}, bf16[400,128]{1,0:T(8,128)(2,1)S(1)}, u32[]{:S(2)}, u32[]{:S(2)}) collective-permute-start(bf16[400,128]{1,0:T(8,128)(2,1)S(1)} %get-tuple-element.40), channel_id=1, source_target_pairs={{0,4},{2,6},{4,0},{6,2},{8,12},{10,14},{12,8},{14,10},{16,20},{18,... | collective-permute-start | bytes 307208 | tf_op jit(solution)/shard_map/ppermute | solution.py:278
  28.9 10.5 %collective-permute-start.4 = (bf16[400,128]{1,0:T(8,128)(2,1)S(1)}, bf16[400,128]{1,0:T(8,128)(2,1)S(1)}, u32[]{:S(2)}, u32[]{:S(2)}) collective-permute-start(bf16[400,128]{1,0:T(8,128)(2,1)S(1)} %get-tuple-element.41), channel_id=1, source_target_pairs={{0,30},{2,28},{4,26},{6,24},{8,22},{10,20},{12,18},{14,16},{16,14}... | collective-permute-start | bytes 307208 | tf_op jit(solution)/shard_map/ppermute | solution.py:278
  29.6 9.9 %collective-permute-start.5 = (bf16[400,128]{1,0:T(8,128)(2,1)S(1)}, bf16[400,128]{1,0:T(8,128)(2,1)S(1)}, u32[]{:S(2)}, u32[]{:S(2)}) collective-permute-start(bf16[400,128]{1,0:T(8,128)(2,1)S(1)} %get-tuple-element.42), channel_id=1, source_target_pairs={{0,6},{2,4},{4,2},{6,0},{8,14},{10,12},{12,10},{14,8},{16,22},{18,... | collective-permute-start | bytes 307208 | tf_op jit(solution)/shard_map/ppermute | solution.py:278
  32.0 12.3 %collective-permute-start.6 = (bf16[400,128]{1,0:T(8,128)(2,1)S(1)}, bf16[400,128]{1,0:T(8,128)(2,1)S(1)}, u32[]{:S(2)}, u32[]{:S(2)}) collective-permute-start(bf16[400,128]{1,0:T(8,128)(2,1)S(1)} %get-tuple-element.43), channel_id=1, source_target_pairs={{0,22},{2,20},{4,18},{6,16},{8,30},{10,28},{12,26},{14,24},{16,6},... | collective-permute-start | bytes 307208 | tf_op jit(solution)/shard_map/ppermute | solution.py:278
  38.7 5.8 %collective-permute-start.16 = (bf16[512,896]{1,0:T(8,128)(2,1)S(1)}, bf16[512,896]{1,0:T(8,128)(2,1)S(1)}, u32[]{:S(2)}, u32[]{:S(2)}) collective-permute-start(bf16[512,896]{1,0:T(8,128)(2,1)S(1)} %get-tuple-element.52.refs_0_.refs_2_.refs_1_.refs_4_), channel_id=1, source_target_pairs={{0,1},{1,0},{2,3},{3,2},{4,5},{5,4},{6,7},{7,6},{8,9},{9,8},{10,11... | collective-permute-start | bytes 2752520 | tf_op jit(solution)/shard_map/ppermute | solution.py:281
  44.5 2.9 %collective-permute-start.15 = (bf16[512,896]{1,0:T(8,128)(2,1)S(1)}, bf16[512,896]{1,0:T(8,128)(2,1)S(1)}, u32[]{:S(2)}, u32[]{:S(2)}) collective-permute-start(bf16[512,896]{1,0:T(8,128)(2,1)S(1)} %get-tuple-element.54.refs_0_.refs_5_), channel_id=1, source_target_pairs={{0,1},{1,0},{2,3},{3,2},{4,5},{5,4},{6,7},{7,6},{8,9},{9,8},{10,11... | collective-permute-start | bytes 2752520 | tf_op jit(solution)/shard_map/ppermute | solution.py:281
  45.3 2.7 %collective-permute-start.17 = (f32[8,512]{1,0:T(8,128)S(1)}, f32[8,512]{1,0:T(8,128)S(1)}, u32[]{:S(2)}, u32[]{:S(2)}) collective-permute-start(f32[8,512]{1,0:T(8,128)S(1)} %get-tuple-element.59), channel_id=1, source_target_pairs={{0,1},{1,0},{2,3},{3,2},{4,5},{5,4},{6,7},{7,6},{8,9},{9,8},{10,11... | collective-permute-start | bytes 49160 | tf_op jit(solution)/shard_map/ppermute | solution.py:281

commit v5 on v4

--- a/solution.py
+++ b/solution.py
@@ -11,6 +11,7 @@
 EXTRA = 16
 NEVER = 2.0**24
 TILE = 512
+PIECE = 256
 PARAMS = pltpu.CompilerParams(vmem_limit_bytes=40 * 2**20)
 VMEM = pl.BlockSpec(memory_space=pltpu.VMEM)
 SMEM = pl.BlockSpec(memory_space=pltpu.SMEM)
@@ -146,11 +147,10 @@
     k_refs, refs = refs[:candidates], refs[candidates:]
     carry_refs, out_refs = dict(zip(carried, refs)), refs[len(carried) :]
     best = {}
-    for q in range(queries):
-        rows = q_refs[q].shape[0]
-        best[q] = carry_refs[q][0:1, :] if q in carry_refs else jnp.full((1, rows), -1.0, jnp.float32)
-    for extra in range(queries, queries + foreign):
-        best[extra] = jnp.full((1, out_refs[extra].shape[1]), -1.0, jnp.float32)
+    for q in range(queries + foreign):
+        rows = out_refs[q].shape[1]
+        start = carry_refs[q][0:1, :] if q in carry_refs else jnp.full((1, rows), -1.0, jnp.float32)
+        best[q] = [start[:, first : first + PIECE] for first in range(0, rows, PIECE)]
     for k in range(candidates):
         for first in range(0, k_refs[k].shape[0], TILE):
             at = slice(first, min(first + TILE, k_refs[k].shape[0]))
@@ -160,26 +160,33 @@
             for q in range(queries):
                 if (q, k) not in pairs:
                     continue
-                scores = lax.dot_general(
-                    k_refs[k][at, 0:width],
-                    q_refs[q][:, 0:width],
-                    (((1,), (1,)), ((), ())),
-                    preferred_element_type=jnp.float32,
-                )
-                kept = jnp.where(other < line_refs[q][0:1, :], scores, -1.0)
-                best[q] = jnp.maximum(best[q], jnp.max(kept, axis=0, keepdims=True))
+                folded = None
+                for piece, low in enumerate(range(0, q_refs[q].shape[0], PIECE)):
+                    part = slice(low, low + PIECE)
+                    scores = lax.dot_general(
+                        k_refs[k][at, 0:width],
+                        q_refs[q][part, 0:width],
+                        (((1,), (1,)), ((), ())),
+                        preferred_element_type=jnp.float32,
+                    )
+                    line = line_refs[q][0:1, part]
+                    kept = jnp.where(other < line, scores, -1.0)
+                    found = jnp.max(kept, axis=0, keepdims=True)
+                    best[q][piece] = jnp.maximum(best[q][piece], found)
+                    if (q, k) in mirrored:
+                        line = jnp.where(line > 0.0, line, NEVER)
+                        kept = jnp.where(line < theirs, scores, -1.0)
+                        for lane in range(0, PIECE, LANES):
+                            column = kept[:, lane : lane + LANES]
+                            folded = column if folded is None else jnp.maximum(folded, column)
                 if (q, k) in mirrored:
-                    asked = mirrored[q, k]
-                    line = line_refs[q][0:1, :]
-                    line = jnp.where(line > 0.0, line, NEVER)
-                    kept = jnp.where(line < theirs, scores, -1.0)
-                    folded = kept[:, 0:LANES]
-                    for lane in range(LANES, kept.shape[1], LANES):
-                        folded = jnp.maximum(folded, kept[:, lane : lane + LANES])
                     found = jnp.max(jnp.transpose(folded), axis=0, keepdims=True)
-                    best[asked] = jnp.maximum(best[asked], found)
+                    asked = best[mirrored[q, k]]
+                    for piece in range(len(asked)):
+                        part = slice(piece * PIECE, (piece + 1) * PIECE)
+                        asked[piece] = jnp.maximum(asked[piece], found[:, part])
     for q in range(queries + foreign):
-        out_refs[q][0:1, :] = best[q]
+        out_refs[q][0:1, :] = jnp.concatenate(best[q], axis=1)
 
 
 def match(groups, candidates, pairs, carry, width, mirrored=None, foreign=0):

time: 58 us -> 58 us (level)
  no operation moved by 1% of the time
where the time goes in v5:
time: 58 us; the launch traced here: 57.9 us
  starting transfers between devices  29.4 us (51%)
  waiting for transfers between devices  11.7 us (20%)
  blocking collectives  9.07 us (16%)
  Pallas kernels  6.57 us (11%)
  local copies, waits for them, and re-layouts  1 us (2%)
    ppermute x15, starting transfers between devices, body(): lax.ppermute(messages[g], 'ingest', [(i, i ^ flips[g]) for i in range(nod...  28.7 us
    ppermute x15, waiting for transfers between devices, body(): lax.ppermute(messages[g], 'ingest', [(i, i ^ flips[g]) for i in range(nod...  11.7 us
    all_to_all x1, blocking collectives, body(): lax.all_to_all(highest, 'ingest', split_axis=0, concat_axis=0, tiled=True...  9.07 us
    pallas_call x4, Pallas kernels, match(): pl.pallas_call(functools.partial(match_kernel, width=width, queries=len(g...  3.51 us
    pallas_call x2, Pallas kernels, body(): pl.pallas_call(functools.partial(pack_kernel, chosen=chosen, capacity=cap...  1.7 us
  transfers between devices with their start and end apart: 18, of which 5 were waited for; matrix products, arithmetic and copies ran while one was open for 0% of the time, Pallas kernels for 8%

profile of v5, /device:TPU:0, one launch (start us, length us, event | category | flops | bytes accessed | tf_op | source)
XLA Modules:
  0.0 57.9 jit_solution(9296725781695765751)
XLA Ops:
  0.0 0.7 %copy-done.2 = s32[512]{0:T(512)S(1)} copy-done((s32[512]{0:T(512)S(1)}, s32[512]{0:T(512)}, u32[]{:S(2)}) %copy-start.2) | copy-done | bytes 2072
  1.2 0.9 %shard_map.38 = (bf16[400,128]{1,0:T(8,128)(2,1)S(1)}, bf16[400,128]{1,0:T(8,128)(2,1)S(1)}, bf16[400,128]{1,0:T(8,128)(2,1)S(1)}, bf16[400,128]{1,0:T(8,128)(2,...) custom-call(bf16[512,768]{1,0:T(8,128)(2,1)S(1)} %copy-done.1, ...), custom_call_target="tpu_custom_call" | custom-call | flops 469762048 | bytes 4096 | tf_op jit(solution)/shard_map/pallas_call | solution.py:268
  2.1 5.1 %collective-permute-start.10 = (bf16[400,128]{1,0:T(8,128)(2,1)S(1)}, bf16[400,128]{1,0:T(8,128)(2,1)S(1)}, u32[]{:S(2)}, u32[]{:S(2)}) collective-permute-start(bf16[400,128]{1,0:T(8,128)(2,1)S(1)} %get-tuple-element.47), channel_id=1, source_target_pairs={{0,24},{2,26},{4,28},{6,30},{8,16},{10,18},{12,20},{14,22},{16,8},... | collective-permute-start | bytes 307208 | tf_op jit(solution)/shard_map/ppermute | solution.py:285
  7.2 0.6 %collective-permute-start.12 = (bf16[400,128]{1,0:T(8,128)(2,1)S(1)}, bf16[400,128]{1,0:T(8,128)(2,1)S(1)}, u32[]{:S(2)}, u32[]{:S(2)}) collective-permute-start(bf16[400,128]{1,0:T(8,128)(2,1)S(1)} %get-tuple-element.49), channel_id=1, source_target_pairs={{0,16},{2,18},{4,20},{6,22},{8,24},{10,26},{12,28},{14,30},{16,0},... | collective-permute-start | bytes 307208 | tf_op jit(solution)/shard_map/ppermute | solution.py:285
  7.8 2.3 %collective-permute-start.13 = (bf16[400,128]{1,0:T(8,128)(2,1)S(1)}, bf16[400,128]{1,0:T(8,128)(2,1)S(1)}, u32[]{:S(2)}, u32[]{:S(2)}) collective-permute-start(bf16[400,128]{1,0:T(8,128)(2,1)S(1)} %get-tuple-element.50), channel_id=1, source_target_pairs={{0,10},{2,8},{4,14},{6,12},{8,2},{10,0},{12,6},{14,4},{16,26},{18,... | collective-permute-start | bytes 307208 | tf_op jit(solution)/shard_map/ppermute | solution.py:285
  10.1 2.4 %collective-permute-start.14 = (bf16[400,128]{1,0:T(8,128)(2,1)S(1)}, bf16[400,128]{1,0:T(8,128)(2,1)S(1)}, u32[]{:S(2)}, u32[]{:S(2)}) collective-permute-start(bf16[400,128]{1,0:T(8,128)(2,1)S(1)} %get-tuple-element.51), channel_id=1, source_target_pairs={{0,26},{2,24},{4,30},{6,28},{8,18},{10,16},{12,22},{14,20},{16,10}... | collective-permute-start | bytes 307208 | tf_op jit(solution)/shard_map/ppermute | solution.py:285
  12.5 2.1 %collective-permute-start.7 = (bf16[400,128]{1,0:T(8,128)(2,1)S(1)}, bf16[400,128]{1,0:T(8,128)(2,1)S(1)}, u32[]{:S(2)}, u32[]{:S(2)}) collective-permute-start(bf16[400,128]{1,0:T(8,128)(2,1)S(1)} %get-tuple-element.44), channel_id=1, source_target_pairs={{0,12},{2,14},{4,8},{6,10},{8,4},{10,6},{12,0},{14,2},{16,28},{18,... | collective-permute-start | bytes 307208 | tf_op jit(solution)/shard_map/ppermute | solution.py:285
  14.6 0.8 %shard_map.39 = (bf16[400,128]{1,0:T(8,128)(2,1)S(1)}, bf16[400,128]{1,0:T(8,128)(2,1)S(1)}, bf16[400,128]{1,0:T(8,128)(2,1)S(1)}, bf16[400,128]{1,0:T(8,128)(2,...) custom-call(bf16[512,896]{1,0:T(8,128)(2,1)S(1)} %get-tuple-element., ...), custom_call_target="tpu_custom_call" | custom-call | flops 469762048 | bytes 4096 | tf_op jit(solution)/shard_map/pallas_call | solution.py:268
  15.3 2.7 %collective-permute-start.8 = (bf16[400,128]{1,0:T(8,128)(2,1)S(1)}, bf16[400,128]{1,0:T(8,128)(2,1)S(1)}, u32[]{:S(2)}, u32[]{:S(2)}) collective-permute-start(bf16[400,128]{1,0:T(8,128)(2,1)S(1)} %get-tuple-element.45), channel_id=1, source_target_pairs={{0,18},{2,16},{4,22},{6,20},{8,26},{10,24},{12,30},{14,28},{16,2},... | collective-permute-start | bytes 307208 | tf_op jit(solution)/shard_map/ppermute | solution.py:285
  18.3 2.5 %collective-permute-done.13.refs_6_ = bf16[400,128]{1,0:T(8,128)(2,1)S(1)} collective-permute-done((bf16[400,128]{1,0:T(8,128)(2,1)S(1)}, bf16[400,128]{1,0:T(8,128)(2,1)S(1)}, u32[]{:S(2)}, u32[]{:S(2)}) %collective-permute-start.13) | collective-permute-done | bytes 102432 | tf_op jit(solution)/shard_map/ppermute | solution.py:285
  20.8 0.8 %collective-permute-start = (bf16[400,128]{1,0:T(8,128)(2,1)S(1)}, bf16[400,128]{1,0:T(8,128)(2,1)S(1)}, u32[]{:S(2)}, u32[]{:S(2)}) collective-permute-start(bf16[400,128]{1,0:T(8,128)(2,1)S(1)} %get-tuple-element.37), channel_id=1, source_target_pairs={{0,28},{2,30},{4,24},{6,26},{8,20},{10,22},{12,16},{14,18},{16,12}... | collective-permute-start | bytes 307208 | tf_op jit(solution)/shard_map/ppermute | solution.py:285
  21.5 1.5 %collective-permute-start.1 = (bf16[400,128]{1,0:T(8,128)(2,1)S(1)}, bf16[400,128]{1,0:T(8,128)(2,1)S(1)}, u32[]{:S(2)}, u32[]{:S(2)}) collective-permute-start(bf16[400,128]{1,0:T(8,128)(2,1)S(1)} %get-tuple-element.38), channel_id=1, source_target_pairs={{0,2},{2,0},{4,6},{6,4},{8,10},{10,8},{12,14},{14,12},{16,18},{18,... | collective-permute-start | bytes 307208 | tf_op jit(solution)/shard_map/ppermute | solution.py:285
  23.1 1.0 %collective-permute-done.7.refs_0_ = bf16[400,128]{1,0:T(8,128)(2,1)S(1)} collective-permute-done((bf16[400,128]{1,0:T(8,128)(2,1)S(1)}, bf16[400,128]{1,0:T(8,128)(2,1)S(1)}, u32[]{:S(2)}, u32[]{:S(2)}) %collective-permute-start.7) | collective-permute-done | bytes 102432 | tf_op jit(solution)/shard_map/ppermute | solution.py:285
  24.1 2.7 %collective-permute-done.8.refs_1_ = bf16[400,128]{1,0:T(8,128)(2,1)S(1)} collective-permute-done((bf16[400,128]{1,0:T(8,128)(2,1)S(1)}, bf16[400,128]{1,0:T(8,128)(2,1)S(1)}, u32[]{:S(2)}, u32[]{:S(2)}) %collective-permute-start.8) | collective-permute-done | bytes 102432 | tf_op jit(solution)/shard_map/ppermute | solution.py:285
  26.7 1.5 %collective-permute-start.3 = (bf16[400,128]{1,0:T(8,128)(2,1)S(1)}, bf16[400,128]{1,0:T(8,128)(2,1)S(1)}, u32[]{:S(2)}, u32[]{:S(2)}) collective-permute-start(bf16[400,128]{1,0:T(8,128)(2,1)S(1)} %get-tuple-element.40), channel_id=1, source_target_pairs={{0,4},{2,6},{4,0},{6,2},{8,12},{10,14},{12,8},{14,10},{16,20},{18,... | collective-permute-start | bytes 307208 | tf_op jit(solution)/shard_map/ppermute | solution.py:285
  28.3 0.7 %collective-permute-done.9.refs_2_ = bf16[400,128]{1,0:T(8,128)(2,1)S(1)} collective-permute-done((bf16[400,128]{1,0:T(8,128)(2,1)S(1)}, bf16[400,128]{1,0:T(8,128)(2,1)S(1)}, u32[]{:S(2)}, u32[]{:S(2)}) %collective-permute-start.9) | collective-permute-done | bytes 102432 | tf_op jit(solution)/shard_map/ppermute | solution.py:285
  28.9 0.6 %collective-permute-start.4 = (bf16[400,128]{1,0:T(8,128)(2,1)S(1)}, bf16[400,128]{1,0:T(8,128)(2,1)S(1)}, u32[]{:S(2)}, u32[]{:S(2)}) collective-permute-start(bf16[400,128]{1,0:T(8,128)(2,1)S(1)} %get-tuple-element.41), channel_id=1, source_target_pairs={{0,30},{2,28},{4,26},{6,24},{8,22},{10,20},{12,18},{14,16},{16,14}... | collective-permute-start | bytes 307208 | tf_op jit(solution)/shard_map/ppermute | solution.py:285
  29.6 2.4 %collective-permute-start.5 = (bf16[400,128]{1,0:T(8,128)(2,1)S(1)}, bf16[400,128]{1,0:T(8,128)(2,1)S(1)}, u32[]{:S(2)}, u32[]{:S(2)}) collective-permute-start(bf16[400,128]{1,0:T(8,128)(2,1)S(1)} %get-tuple-element.42), channel_id=1, source_target_pairs={{0,6},{2,4},{4,2},{6,0},{8,14},{10,12},{12,10},{14,8},{16,22},{18,... | collective-permute-start | bytes 307208 | tf_op jit(solution)/shard_map/ppermute | solution.py:285
  32.0 6.5 %collective-permute-start.6 = (bf16[400,128]{1,0:T(8,128)(2,1)S(1)}, bf16[400,128]{1,0:T(8,128)(2,1)S(1)}, u32[]{:S(2)}, u32[]{:S(2)}) collective-permute-start(bf16[400,128]{1,0:T(8,128)(2,1)S(1)} %get-tuple-element.43), channel_id=1, source_target_pairs={{0,22},{2,20},{4,18},{6,16},{8,30},{10,28},{12,26},{14,24},{16,6},... | collective-permute-start | bytes 307208 | tf_op jit(solution)/shard_map/ppermute | solution.py:285
  39.5 4.8 %collective-permute-done.6.refs_7_ = bf16[400,128]{1,0:T(8,128)(2,1)S(1)} collective-permute-done((bf16[400,128]{1,0:T(8,128)(2,1)S(1)}, bf16[400,128]{1,0:T(8,128)(2,1)S(1)}, u32[]{:S(2)}, u32[]{:S(2)}) %collective-permute-start.6) | collective-permute-done | bytes 102432 | tf_op jit(solution)/shard_map/ppermute | solution.py:285
  44.6 0.8 %shard_map.43 = (f32[8,512]{1,0:T(8,128)S(1)}, f32[8,512]{1,0:T(8,128)S(1)}) custom-call(bf16[512,896]{1,0:T(8,128)(2,1)S(1)} %get-tuple-element.54.refs_0_.refs_5_, f32[8,512]{1,0:T(8,128)S(1)} %get-tuple-element.55.refs_1_.refs_2_, bf16[512,896]{1,0:T(8,128)(2,1)S(1)} %collective-permute-done.16.refs_2_.refs_6_), custom_call_target="tpu_custom_call" | custom-call | flops 1 | bytes 1 | tf_op jit(solution)/shard_map/pallas_call | solution.py:200
  45.9 1.5 %shard_map.44 = (f32[8,512]{1,0:T(8,128)S(1)}, f32[8,512]{1,0:T(8,128)S(1)}) custom-call(bf16[512,896]{1,0:T(8,128)(2,1)S(1)} %get-tuple-element.54.refs_0_.refs_5_, bf16[512,896]{1,0:T(8,128)(2,1)S(1)} %get-tuple-element.52.refs_0_.refs_2_.refs_1_.refs_4_, f32[8,512]{1,0:T(8,128)S(1)} %get-tuple-element.55.refs_1_.refs_2_, ...), custom_call_target="tpu_custom_call" | custom-call | flops 1 | bytes 1 | tf_op jit(solution)/shard_map/pallas_call | solution.py:200
  48.1 9.1 %all_to_all.5.back_ref = f32[16,1,128]{2,1,0:T(1,128)S(1)} all-to-all(f32[16,1,128]{2,1,0:T(1,128)S(1)} %shard_map.46), channel_id=1, replica_groups={{30,28,26,24,22,20,18,16,14,12,10,8,6,4,2,0},{31,29,27,25,23,21,19,17,1..., dimensions={0} | all-to-all | bytes 16384 | tf_op jit(solution)/shard_map/all_to_all | solution.py:313
  57.2 0.7 %shard_map.47 = f32[1,512]{1,0:T(1,128)} custom-call(f32[16,1,128]{2,1,0:T(1,128)S(1)} %all_to_all.5.back_ref, s32[1,512]{1,0:T(1,128)S(1)} %bitcast.5, s32[1,512]{1,0:T(1,128)S(1)} %get-tuple-element.60.pos_ref), custom_call_target="tpu_custom_call" | custom-call | tf_op jit(solution)/shard_map/pallas_call | solution.py:321
  (30 shorter events, 3.2 us)
Async XLA Ops:
  0.0 0.7 %copy-start.2 = (s32[512]{0:T(512)S(1)}, s32[512]{0:T(512)}, u32[]{:S(2)}) copy-start(s32[512]{0:T(512)} %param.5) | copy-start | bytes 6148
  0.0 0.7 %copy-start = (s32[512]{0:T(512)S(1)}, s32[512]{0:T(512)}, u32[]{:S(2)}) copy-start(s32[512]{0:T(512)} %param.4) | copy-start | bytes 6148
  0.0 1.2 %copy-start.1 = (bf16[512,768]{1,0:T(8,128)(2,1)S(1)}, bf16[512,768]{1,0:T(8,128)(2,1)}, u32[]{:S(2)}) copy-start(bf16[512,768]{1,0:T(8,128)(2,1)} %rows_ref.1) | copy-start | bytes 2359300
  2.1 10.4 %collective-permute-start.10 = (bf16[400,128]{1,0:T(8,128)(2,1)S(1)}, bf16[400,128]{1,0:T(8,128)(2,1)S(1)}, u32[]{:S(2)}, u32[]{:S(2)}) collective-permute-start(bf16[400,128]{1,0:T(8,128)(2,1)S(1)} %get-tuple-element.47), channel_id=1, source_target_pairs={{0,24},{2,26},{4,28},{6,30},{8,16},{10,18},{12,20},{14,22},{16,8},... | collective-permute-start | bytes 307208 | tf_op jit(solution)/shard_map/ppermute | solution.py:285
  7.2 8.1 %collective-permute-start.11 = (bf16[400,128]{1,0:T(8,128)(2,1)S(1)}, bf16[400,128]{1,0:T(8,128)(2,1)S(1)}, u32[]{:S(2)}, u32[]{:S(2)}) collective-permute-start(bf16[400,128]{1,0:T(8,128)(2,1)S(1)} %get-tuple-element.48), channel_id=1, source_target_pairs={{0,8},{2,10},{4,12},{6,14},{8,0},{10,2},{12,4},{14,6},{16,24},{18,... | collective-permute-start | bytes 307208 | tf_op jit(solution)/shard_map/ppermute | solution.py:285
  7.2 10.8 %collective-permute-start.12 = (bf16[400,128]{1,0:T(8,128)(2,1)S(1)}, bf16[400,128]{1,0:T(8,128)(2,1)S(1)}, u32[]{:S(2)}, u32[]{:S(2)}) collective-permute-start(bf16[400,128]{1,0:T(8,128)(2,1)S(1)} %get-tuple-element.49), channel_id=1, source_target_pairs={{0,16},{2,18},{4,20},{6,22},{8,24},{10,26},{12,28},{14,30},{16,0},... | collective-permute-start | bytes 307208 | tf_op jit(solution)/shard_map/ppermute | solution.py:285
  7.8 13.0 %collective-permute-start.13 = (bf16[400,128]{1,0:T(8,128)(2,1)S(1)}, bf16[400,128]{1,0:T(8,128)(2,1)S(1)}, u32[]{:S(2)}, u32[]{:S(2)}) collective-permute-start(bf16[400,128]{1,0:T(8,128)(2,1)S(1)} %get-tuple-element.50), channel_id=1, source_target_pairs={{0,10},{2,8},{4,14},{6,12},{8,2},{10,0},{12,6},{14,4},{16,26},{18,... | collective-permute-start | bytes 307208 | tf_op jit(solution)/shard_map/ppermute | solution.py:285
  10.1 11.4 %collective-permute-start.14 = (bf16[400,128]{1,0:T(8,128)(2,1)S(1)}, bf16[400,128]{1,0:T(8,128)(2,1)S(1)}, u32[]{:S(2)}, u32[]{:S(2)}) collective-permute-start(bf16[400,128]{1,0:T(8,128)(2,1)S(1)} %get-tuple-element.51), channel_id=1, source_target_pairs={{0,26},{2,24},{4,30},{6,28},{8,18},{10,16},{12,22},{14,20},{16,10}... | collective-permute-start | bytes 307208 | tf_op jit(solution)/shard_map/ppermute | solution.py:285
  12.5 11.6 %collective-permute-start.7 = (bf16[400,128]{1,0:T(8,128)(2,1)S(1)}, bf16[400,128]{1,0:T(8,128)(2,1)S(1)}, u32[]{:S(2)}, u32[]{:S(2)}) collective-permute-start(bf16[400,128]{1,0:T(8,128)(2,1)S(1)} %get-tuple-element.44), channel_id=1, source_target_pairs={{0,12},{2,14},{4,8},{6,10},{8,4},{10,6},{12,0},{14,2},{16,28},{18,... | collective-permute-start | bytes 307208 | tf_op jit(solution)/shard_map/ppermute | solution.py:285
  15.3 11.4 %collective-permute-start.8 = (bf16[400,128]{1,0:T(8,128)(2,1)S(1)}, bf16[400,128]{1,0:T(8,128)(2,1)S(1)}, u32[]{:S(2)}, u32[]{:S(2)}) collective-permute-start(bf16[400,128]{1,0:T(8,128)(2,1)S(1)} %get-tuple-element.45), channel_id=1, source_target_pairs={{0,18},{2,16},{4,22},{6,20},{8,26},{10,24},{12,30},{14,28},{16,2},... | collective-permute-start | bytes 307208 | tf_op jit(solution)/shard_map/ppermute | solution.py:285
  18.0 10.9 %collective-permute-start.9 = (bf16[400,128]{1,0:T(8,128)(2,1)S(1)}, bf16[400,128]{1,0:T(8,128)(2,1)S(1)}, u32[]{:S(2)}, u32[]{:S(2)}) collective-permute-start(bf16[400,128]{1,0:T(8,128)(2,1)S(1)} %get-tuple-element.46), channel_id=1, source_target_pairs={{0,14},{2,12},{4,10},{6,8},{8,6},{10,4},{12,2},{14,0},{16,30},{18,... | collective-permute-start | bytes 307208 | tf_op jit(solution)/shard_map/ppermute | solution.py:285
  20.8 8.8 %collective-permute-start = (bf16[400,128]{1,0:T(8,128)(2,1)S(1)}, bf16[400,128]{1,0:T(8,128)(2,1)S(1)}, u32[]{:S(2)}, u32[]{:S(2)}) collective-permute-start(bf16[400,128]{1,0:T(8,128)(2,1)S(1)} %get-tuple-element.37), channel_id=1, source_target_pairs={{0,28},{2,30},{4,24},{6,26},{8,20},{10,22},{12,16},{14,18},{16,12}... | collective-permute-start | bytes 307208 | tf_op jit(solution)/shard_map/ppermute | solution.py:285
  21.5 10.4 %collective-permute-start.1 = (bf16[400,128]{1,0:T(8,128)(2,1)S(1)}, bf16[400,128]{1,0:T(8,128)(2,1)S(1)}, u32[]{:S(2)}, u32[]{:S(2)}) collective-permute-start(bf16[400,128]{1,0:T(8,128)(2,1)S(1)} %get-tuple-element.38), channel_id=1, source_target_pairs={{0,2},{2,0},{4,6},{6,4},{8,10},{10,8},{12,14},{14,12},{16,18},{18,... | collective-permute-start | bytes 307208 | tf_op jit(solution)/shard_map/ppermute | solution.py:285
  24.1 14.6 %collective-permute-start.2 = (bf16[400,128]{1,0:T(8,128)(2,1)S(1)}, bf16[400,128]{1,0:T(8,128)(2,1)S(1)}, u32[]{:S(2)}, u32[]{:S(2)}) collective-permute-start(bf16[400,128]{1,0:T(8,128)(2,1)S(1)} %get-tuple-element.39), channel_id=1, source_target_pairs={{0,20},{2,22},{4,16},{6,18},{8,28},{10,30},{12,24},{14,26},{16,4},... | collective-permute-start | bytes 307208 | tf_op jit(solution)/shard_map/ppermute | solution.py:285
  26.7 12.7 %collective-permute-start.3 = (bf16[400,128]{1,0:T(8,128)(2,1)S(1)}, bf16[400,128]{1,0:T(8,128)(2,1)S(1)}, u32[]{:S(2)}, u32[]{:S(2)}) collective-permute-start(bf16[400,128]{1,0:T(8,128)(2,1)S(1)} %get-tuple-element.40), channel_id=1, source_target_pairs={{0,4},{2,6},{4,0},{6,2},{8,12},{10,14},{12,8},{14,10},{16,20},{18,... | collective-permute-start | bytes 307208 | tf_op jit(solution)/shard_map/ppermute | solution.py:285
  28.9 10.5 %collective-permute-start.4 = (bf16[400,128]{1,0:T(8,128)(2,1)S(1)}, bf16[400,128]{1,0:T(8,128)(2,1)S(1)}, u32[]{:S(2)}, u32[]{:S(2)}) collective-permute-start(bf16[400,128]{1,0:T(8,128)(2,1)S(1)} %get-tuple-element.41), channel_id=1, source_target_pairs={{0,30},{2,28},{4,26},{6,24},{8,22},{10,20},{12,18},{14,16},{16,14}... | collective-permute-start | bytes 307208 | tf_op jit(solution)/shard_map/ppermute | solution.py:285
  29.6 9.9 %collective-permute-start.5 = (bf16[400,128]{1,0:T(8,128)(2,1)S(1)}, bf16[400,128]{1,0:T(8,128)(2,1)S(1)}, u32[]{:S(2)}, u32[]{:S(2)}) collective-permute-start(bf16[400,128]{1,0:T(8,128)(2,1)S(1)} %get-tuple-element.42), channel_id=1, source_target_pairs={{0,6},{2,4},{4,2},{6,0},{8,14},{10,12},{12,10},{14,8},{16,22},{18,... | collective-permute-start | bytes 307208 | tf_op jit(solution)/shard_map/ppermute | solution.py:285
  32.0 12.3 %collective-permute-start.6 = (bf16[400,128]{1,0:T(8,128)(2,1)S(1)}, bf16[400,128]{1,0:T(8,128)(2,1)S(1)}, u32[]{:S(2)}, u32[]{:S(2)}) collective-permute-start(bf16[400,128]{1,0:T(8,128)(2,1)S(1)} %get-tuple-element.43), channel_id=1, source_target_pairs={{0,22},{2,20},{4,18},{6,16},{8,30},{10,28},{12,26},{14,24},{16,6},... | collective-permute-start | bytes 307208 | tf_op jit(solution)/shard_map/ppermute | solution.py:285
  38.7 5.8 %collective-permute-start.16 = (bf16[512,896]{1,0:T(8,128)(2,1)S(1)}, bf16[512,896]{1,0:T(8,128)(2,1)S(1)}, u32[]{:S(2)}, u32[]{:S(2)}) collective-permute-start(bf16[512,896]{1,0:T(8,128)(2,1)S(1)} %get-tuple-element.52.refs_0_.refs_2_.refs_1_.refs_4_), channel_id=1, source_target_pairs={{0,1},{1,0},{2,3},{3,2},{4,5},{5,4},{6,7},{7,6},{8,9},{9,8},{10,11... | collective-permute-start | bytes 2752520 | tf_op jit(solution)/shard_map/ppermute | solution.py:288
  44.5 2.9 %collective-permute-start.15 = (bf16[512,896]{1,0:T(8,128)(2,1)S(1)}, bf16[512,896]{1,0:T(8,128)(2,1)S(1)}, u32[]{:S(2)}, u32[]{:S(2)}) collective-permute-start(bf16[512,896]{1,0:T(8,128)(2,1)S(1)} %get-tuple-element.54.refs_0_.refs_5_), channel_id=1, source_target_pairs={{0,1},{1,0},{2,3},{3,2},{4,5},{5,4},{6,7},{7,6},{8,9},{9,8},{10,11... | collective-permute-start | bytes 2752520 | tf_op jit(solution)/shard_map/ppermute | solution.py:288
  45.3 2.7 %collective-permute-start.17 = (f32[8,512]{1,0:T(8,128)S(1)}, f32[8,512]{1,0:T(8,128)S(1)}, u32[]{:S(2)}, u32[]{:S(2)}) collective-permute-start(f32[8,512]{1,0:T(8,128)S(1)} %get-tuple-element.59), channel_id=1, source_target_pairs={{0,1},{1,0},{2,3},{3,2},{4,5},{5,4},{6,7},{7,6},{8,9},{9,8},{10,11... | collective-permute-start | bytes 49160 | tf_op jit(solution)/shard_map/ppermute | solution.py:288

commit v6 on v5

--- a/solution.py
+++ b/solution.py
@@ -291,17 +291,16 @@
     (best_b,) = match([(b, b_line)], [b], [(0, 0)], {}, width)
     a, a_line = assemble(messages[:half], half, [best_b], [], width)
     groups = [(a, a_line), (b, b_line)]
-    b_other = across(b)
-    best_a, for_other = match([(a, a_line)], [b_other], [(0, 0)], {}, width, {(0, 0): 1}, foreign=1)
+    best_a, best_b, for_other = match(
+        groups,
+        [across(b), b, a],
+        [(0, 0), (1, 0), (0, 1), (0, 2)],
+        {1: best_b},
+        width,
+        {(0, 0): 2, (0, 1): 1},
+        foreign=1,
+    )
     from_other = across(for_other)
-    best_a, best_b = match(
-        groups,
-        [b, a, b_other],
-        [(0, 1), (0, 0), (1, 2)],
-        {0: best_a, 1: best_b},
-        width,
-        {(0, 0): 1},
-    )
     (best_a,) = match([(a, a_line)], [across(a)], [(0, 0)], {0: best_a}, width)
     highest = pl.pallas_call(
         functools.partial(address_kernel, flips=flips, capacity=capacity),

time: 58 us -> 58 us (level)
    pallas_call x4 -> x3, Pallas kernels: 3.51 us -> 3.21 us  [match(): pl.pallas_call(functools.partial(match_kernel, width=width, queries=len(g...]
  transfers between devices with their start and end apart: 18 -> 18, of which waited for: 5 -> 6; matrix products, arithmetic and copies ran while one was open for 0% -> 0% of each run, Pallas kernels for 8% -> 8%
where the time goes in v6:
time: 58 us; the launch traced here: 57.8 us
  starting transfers between devices  29.4 us (51%)
  waiting for transfers between devices  11.9 us (21%)
  blocking collectives  9.07 us (16%)
  Pallas kernels  6.26 us (11%)
  local copies, waits for them, and re-layouts  1 us (2%)
    ppermute x15, starting transfers between devices, body(): lax.ppermute(messages[g], 'ingest', [(i, i ^ flips[g]) for i in range(nod...  28.7 us
    ppermute x15, waiting for transfers between devices, body(): lax.ppermute(messages[g], 'ingest', [(i, i ^ flips[g]) for i in range(nod...  11.7 us
    all_to_all x1, blocking collectives, body(): lax.all_to_all(highest, 'ingest', split_axis=0, concat_axis=0, tiled=True...  9.07 us
    pallas_call x3, Pallas kernels, match(): pl.pallas_call(functools.partial(match_kernel, width=width, queries=len(g...  3.21 us
    pallas_call x2, Pallas kernels, body(): pl.pallas_call(functools.partial(pack_kernel, chosen=chosen, capacity=cap...  1.7 us
  transfers between devices with their start and end apart: 18, of which 6 were waited for; matrix products, arithmetic and copies ran while one was open for 0% of the time, Pallas kernels for 8%

profile of v6, /device:TPU:0, one launch (start us, length us, event | category | flops | bytes accessed | tf_op | source)
XLA Modules:
  0.0 57.8 jit_solution(8066367768321879280)
XLA Ops:
  0.0 0.7 %copy-done.2 = s32[512]{0:T(512)S(1)} copy-done((s32[512]{0:T(512)S(1)}, s32[512]{0:T(512)}, u32[]{:S(2)}) %copy-start.2) | copy-done | bytes 2072
  1.2 0.9 %shard_map.38 = (bf16[400,128]{1,0:T(8,128)(2,1)S(1)}, bf16[400,128]{1,0:T(8,128)(2,1)S(1)}, bf16[400,128]{1,0:T(8,128)(2,1)S(1)}, bf16[400,128]{1,0:T(8,128)(2,...) custom-call(bf16[512,768]{1,0:T(8,128)(2,1)S(1)} %copy-done.1, ...), custom_call_target="tpu_custom_call" | custom-call | flops 469762048 | bytes 4096 | tf_op jit(solution)/shard_map/pallas_call | solution.py:268
  2.1 5.1 %collective-permute-start.10 = (bf16[400,128]{1,0:T(8,128)(2,1)S(1)}, bf16[400,128]{1,0:T(8,128)(2,1)S(1)}, u32[]{:S(2)}, u32[]{:S(2)}) collective-permute-start(bf16[400,128]{1,0:T(8,128)(2,1)S(1)} %get-tuple-element.46), channel_id=1, source_target_pairs={{0,24},{2,26},{4,28},{6,30},{8,16},{10,18},{12,20},{14,22},{16,8},... | collective-permute-start | bytes 307208 | tf_op jit(solution)/shard_map/ppermute | solution.py:285
  7.2 0.6 %collective-permute-start.12 = (bf16[400,128]{1,0:T(8,128)(2,1)S(1)}, bf16[400,128]{1,0:T(8,128)(2,1)S(1)}, u32[]{:S(2)}, u32[]{:S(2)}) collective-permute-start(bf16[400,128]{1,0:T(8,128)(2,1)S(1)} %get-tuple-element.48), channel_id=1, source_target_pairs={{0,16},{2,18},{4,20},{6,22},{8,24},{10,26},{12,28},{14,30},{16,0},... | collective-permute-start | bytes 307208 | tf_op jit(solution)/shard_map/ppermute | solution.py:285
  7.8 2.3 %collective-permute-start.13 = (bf16[400,128]{1,0:T(8,128)(2,1)S(1)}, bf16[400,128]{1,0:T(8,128)(2,1)S(1)}, u32[]{:S(2)}, u32[]{:S(2)}) collective-permute-start(bf16[400,128]{1,0:T(8,128)(2,1)S(1)} %get-tuple-element.49), channel_id=1, source_target_pairs={{0,10},{2,8},{4,14},{6,12},{8,2},{10,0},{12,6},{14,4},{16,26},{18,... | collective-permute-start | bytes 307208 | tf_op jit(solution)/shard_map/ppermute | solution.py:285
  10.1 2.4 %collective-permute-start.14 = (bf16[400,128]{1,0:T(8,128)(2,1)S(1)}, bf16[400,128]{1,0:T(8,128)(2,1)S(1)}, u32[]{:S(2)}, u32[]{:S(2)}) collective-permute-start(bf16[400,128]{1,0:T(8,128)(2,1)S(1)} %get-tuple-element.50), channel_id=1, source_target_pairs={{0,26},{2,24},{4,30},{6,28},{8,18},{10,16},{12,22},{14,20},{16,10}... | collective-permute-start | bytes 307208 | tf_op jit(solution)/shard_map/ppermute | solution.py:285
  12.5 2.1 %collective-permute-start.7 = (bf16[400,128]{1,0:T(8,128)(2,1)S(1)}, bf16[400,128]{1,0:T(8,128)(2,1)S(1)}, u32[]{:S(2)}, u32[]{:S(2)}) collective-permute-start(bf16[400,128]{1,0:T(8,128)(2,1)S(1)} %get-tuple-element.43), channel_id=1, source_target_pairs={{0,12},{2,14},{4,8},{6,10},{8,4},{10,6},{12,0},{14,2},{16,28},{18,... | collective-permute-start | bytes 307208 | tf_op jit(solution)/shard_map/ppermute | solution.py:285
  14.6 0.8 %shard_map.39 = (bf16[400,128]{1,0:T(8,128)(2,1)S(1)}, bf16[400,128]{1,0:T(8,128)(2,1)S(1)}, bf16[400,128]{1,0:T(8,128)(2,1)S(1)}, bf16[400,128]{1,0:T(8,128)(2,...) custom-call(bf16[512,896]{1,0:T(8,128)(2,1)S(1)} %get-tuple-element., ...), custom_call_target="tpu_custom_call" | custom-call | flops 469762048 | bytes 4096 | tf_op jit(solution)/shard_map/pallas_call | solution.py:268
  15.3 2.7 %collective-permute-start.8 = (bf16[400,128]{1,0:T(8,128)(2,1)S(1)}, bf16[400,128]{1,0:T(8,128)(2,1)S(1)}, u32[]{:S(2)}, u32[]{:S(2)}) collective-permute-start(bf16[400,128]{1,0:T(8,128)(2,1)S(1)} %get-tuple-element.44), channel_id=1, source_target_pairs={{0,18},{2,16},{4,22},{6,20},{8,26},{10,24},{12,30},{14,28},{16,2},... | collective-permute-start | bytes 307208 | tf_op jit(solution)/shard_map/ppermute | solution.py:285
  18.3 2.5 %collective-permute-done.13.refs_6_ = bf16[400,128]{1,0:T(8,128)(2,1)S(1)} collective-permute-done((bf16[400,128]{1,0:T(8,128)(2,1)S(1)}, bf16[400,128]{1,0:T(8,128)(2,1)S(1)}, u32[]{:S(2)}, u32[]{:S(2)}) %collective-permute-start.13) | collective-permute-done | bytes 102432 | tf_op jit(solution)/shard_map/ppermute | solution.py:285
  20.8 0.8 %collective-permute-start = (bf16[400,128]{1,0:T(8,128)(2,1)S(1)}, bf16[400,128]{1,0:T(8,128)(2,1)S(1)}, u32[]{:S(2)}, u32[]{:S(2)}) collective-permute-start(bf16[400,128]{1,0:T(8,128)(2,1)S(1)} %get-tuple-element.36), channel_id=1, source_target_pairs={{0,28},{2,30},{4,24},{6,26},{8,20},{10,22},{12,16},{14,18},{16,12}... | collective-permute-start | bytes 307208 | tf_op jit(solution)/shard_map/ppermute | solution.py:285
  21.5 1.5 %collective-permute-start.1 = (bf16[400,128]{1,0:T(8,128)(2,1)S(1)}, bf16[400,128]{1,0:T(8,128)(2,1)S(1)}, u32[]{:S(2)}, u32[]{:S(2)}) collective-permute-start(bf16[400,128]{1,0:T(8,128)(2,1)S(1)} %get-tuple-element.37), channel_id=1, source_target_pairs={{0,2},{2,0},{4,6},{6,4},{8,10},{10,8},{12,14},{14,12},{16,18},{18,... | collective-permute-start | bytes 307208 | tf_op jit(solution)/shard_map/ppermute | solution.py:285
  23.1 1.0 %collective-permute-done.7.refs_0_ = bf16[400,128]{1,0:T(8,128)(2,1)S(1)} collective-permute-done((bf16[400,128]{1,0:T(8,128)(2,1)S(1)}, bf16[400,128]{1,0:T(8,128)(2,1)S(1)}, u32[]{:S(2)}, u32[]{:S(2)}) %collective-permute-start.7) | collective-permute-done | bytes 102432 | tf_op jit(solution)/shard_map/ppermute | solution.py:285
  24.1 2.7 %collective-permute-done.8.refs_1_ = bf16[400,128]{1,0:T(8,128)(2,1)S(1)} collective-permute-done((bf16[400,128]{1,0:T(8,128)(2,1)S(1)}, bf16[400,128]{1,0:T(8,128)(2,1)S(1)}, u32[]{:S(2)}, u32[]{:S(2)}) %collective-permute-start.8) | collective-permute-done | bytes 102432 | tf_op jit(solution)/shard_map/ppermute | solution.py:285
  26.7 1.5 %collective-permute-start.3 = (bf16[400,128]{1,0:T(8,128)(2,1)S(1)}, bf16[400,128]{1,0:T(8,128)(2,1)S(1)}, u32[]{:S(2)}, u32[]{:S(2)}) collective-permute-start(bf16[400,128]{1,0:T(8,128)(2,1)S(1)} %get-tuple-element.39), channel_id=1, source_target_pairs={{0,4},{2,6},{4,0},{6,2},{8,12},{10,14},{12,8},{14,10},{16,20},{18,... | collective-permute-start | bytes 307208 | tf_op jit(solution)/shard_map/ppermute | solution.py:285
  28.3 0.7 %collective-permute-done.9.refs_2_ = bf16[400,128]{1,0:T(8,128)(2,1)S(1)} collective-permute-done((bf16[400,128]{1,0:T(8,128)(2,1)S(1)}, bf16[400,128]{1,0:T(8,128)(2,1)S(1)}, u32[]{:S(2)}, u32[]{:S(2)}) %collective-permute-start.9) | collective-permute-done | bytes 102432 | tf_op jit(solution)/shard_map/ppermute | solution.py:285
  28.9 0.6 %collective-permute-start.4 = (bf16[400,128]{1,0:T(8,128)(2,1)S(1)}, bf16[400,128]{1,0:T(8,128)(2,1)S(1)}, u32[]{:S(2)}, u32[]{:S(2)}) collective-permute-start(bf16[400,128]{1,0:T(8,128)(2,1)S(1)} %get-tuple-element.40), channel_id=1, source_target_pairs={{0,30},{2,28},{4,26},{6,24},{8,22},{10,20},{12,18},{14,16},{16,14}... | collective-permute-start | bytes 307208 | tf_op jit(solution)/shard_map/ppermute | solution.py:285
  29.6 2.4 %collective-permute-start.5 = (bf16[400,128]{1,0:T(8,128)(2,1)S(1)}, bf16[400,128]{1,0:T(8,128)(2,1)S(1)}, u32[]{:S(2)}, u32[]{:S(2)}) collective-permute-start(bf16[400,128]{1,0:T(8,128)(2,1)S(1)} %get-tuple-element.41), channel_id=1, source_target_pairs={{0,6},{2,4},{4,2},{6,0},{8,14},{10,12},{12,10},{14,8},{16,22},{18,... | collective-permute-start | bytes 307208 | tf_op jit(solution)/shard_map/ppermute | solution.py:285
  32.0 6.5 %collective-permute-start.6 = (bf16[400,128]{1,0:T(8,128)(2,1)S(1)}, bf16[400,128]{1,0:T(8,128)(2,1)S(1)}, u32[]{:S(2)}, u32[]{:S(2)}) collective-permute-start(bf16[400,128]{1,0:T(8,128)(2,1)S(1)} %get-tuple-element.42), channel_id=1, source_target_pairs={{0,22},{2,20},{4,18},{6,16},{8,30},{10,28},{12,26},{14,24},{16,6},... | collective-permute-start | bytes 307208 | tf_op jit(solution)/shard_map/ppermute | solution.py:285
  39.5 4.8 %collective-permute-done.6.refs_7_ = bf16[400,128]{1,0:T(8,128)(2,1)S(1)} collective-permute-done((bf16[400,128]{1,0:T(8,128)(2,1)S(1)}, bf16[400,128]{1,0:T(8,128)(2,1)S(1)}, u32[]{:S(2)}, u32[]{:S(2)}) %collective-permute-start.6) | collective-permute-done | bytes 102432 | tf_op jit(solution)/shard_map/ppermute | solution.py:285
  44.6 2.0 %shard_map.43 = (f32[8,512]{1,0:T(8,128)S(1)}, f32[8,512]{1,0:T(8,128)S(1)}, f32[8,512]{1,0:T(8,128)S(1)}) custom-call(bf16[512,896]{1,0:T(8,128)(2,1)S(1)} %get-tuple-element.53.refs_0_.refs_6_, bf16[512,896]{1,0:T(8,128)(2,1)S(1)} %get-tuple-element.51.refs_0_.refs_2_.refs_1_.refs_5_, f32[8,512]{1,0:T(8,128)S(1)} %get-tuple-element.54.refs_2_.refs_1_, ...), custom_call_target="tpu_custom_call" | custom-call | flops 1 | bytes 1 | tf_op jit(solution)/shard_map/pallas_call | solution.py:200
  47.1 0.6 %shard_map.44.first_ref = f32[8,512]{1,0:T(8,128)S(1)} custom-call(bf16[512,896]{1,0:T(8,128)(2,1)S(1)} %get-tuple-element.53.refs_0_.refs_6_, f32[8,512]{1,0:T(8,128)S(1)} %get-tuple-element.54.refs_2_.refs_1_, bf16[512,896]{1,0:T(8,128)(2,1)S(1)} %collective-permute-done.15.refs_2_, f32[8,512]{1,0:T(8,128)S(1)} %get-tuple-element.55.refs_3_), custom_call_target="tpu_custom_call" | custom-call | flops 1 | bytes 1 | tf_op jit(solution)/shard_map/pallas_call | solution.py:200
  48.0 9.1 %all_to_all.5.back_ref = f32[16,1,128]{2,1,0:T(1,128)S(1)} all-to-all(f32[16,1,128]{2,1,0:T(1,128)S(1)} %shard_map.45), channel_id=1, replica_groups={{30,28,26,24,22,20,18,16,14,12,10,8,6,4,2,0},{31,29,27,25,23,21,19,17,1..., dimensions={0} | all-to-all | bytes 16384 | tf_op jit(solution)/shard_map/all_to_all | solution.py:312
  57.1 0.7 %shard_map.46 = f32[1,512]{1,0:T(1,128)} custom-call(f32[16,1,128]{2,1,0:T(1,128)S(1)} %all_to_all.5.back_ref, s32[1,512]{1,0:T(1,128)S(1)} %bitcast.5, s32[1,512]{1,0:T(1,128)S(1)} %get-tuple-element.58.pos_ref), custom_call_target="tpu_custom_call" | custom-call | tf_op jit(solution)/shard_map/pallas_call | solution.py:320
  (29 shorter events, 2.8 us)
Async XLA Ops:
  0.0 0.7 %copy-start.2 = (s32[512]{0:T(512)S(1)}, s32[512]{0:T(512)}, u32[]{:S(2)}) copy-start(s32[512]{0:T(512)} %param.5) | copy-start | bytes 6148
  0.0 0.7 %copy-start = (s32[512]{0:T(512)S(1)}, s32[512]{0:T(512)}, u32[]{:S(2)}) copy-start(s32[512]{0:T(512)} %param.4) | copy-start | bytes 6148
  0.0 1.2 %copy-start.1 = (bf16[512,768]{1,0:T(8,128)(2,1)S(1)}, bf16[512,768]{1,0:T(8,128)(2,1)}, u32[]{:S(2)}) copy-start(bf16[512,768]{1,0:T(8,128)(2,1)} %rows_ref.1) | copy-start | bytes 2359300
  2.1 10.4 %collective-permute-start.10 = (bf16[400,128]{1,0:T(8,128)(2,1)S(1)}, bf16[400,128]{1,0:T(8,128)(2,1)S(1)}, u32[]{:S(2)}, u32[]{:S(2)}) collective-permute-start(bf16[400,128]{1,0:T(8,128)(2,1)S(1)} %get-tuple-element.46), channel_id=1, source_target_pairs={{0,24},{2,26},{4,28},{6,30},{8,16},{10,18},{12,20},{14,22},{16,8},... | collective-permute-start | bytes 307208 | tf_op jit(solution)/shard_map/ppermute | solution.py:285
  7.2 8.1 %collective-permute-start.11 = (bf16[400,128]{1,0:T(8,128)(2,1)S(1)}, bf16[400,128]{1,0:T(8,128)(2,1)S(1)}, u32[]{:S(2)}, u32[]{:S(2)}) collective-permute-start(bf16[400,128]{1,0:T(8,128)(2,1)S(1)} %get-tuple-element.47), channel_id=1, source_target_pairs={{0,8},{2,10},{4,12},{6,14},{8,0},{10,2},{12,4},{14,6},{16,24},{18,... | collective-permute-start | bytes 307208 | tf_op jit(solution)/shard_map/ppermute | solution.py:285
  7.2 10.8 %collective-permute-start.12 = (bf16[400,128]{1,0:T(8,128)(2,1)S(1)}, bf16[400,128]{1,0:T(8,128)(2,1)S(1)}, u32[]{:S(2)}, u32[]{:S(2)}) collective-permute-start(bf16[400,128]{1,0:T(8,128)(2,1)S(1)} %get-tuple-element.48), channel_id=1, source_target_pairs={{0,16},{2,18},{4,20},{6,22},{8,24},{10,26},{12,28},{14,30},{16,0},... | collective-permute-start | bytes 307208 | tf_op jit(solution)/shard_map/ppermute | solution.py:285
  7.8 13.0 %collective-permute-start.13 = (bf16[400,128]{1,0:T(8,128)(2,1)S(1)}, bf16[400,128]{1,0:T(8,128)(2,1)S(1)}, u32[]{:S(2)}, u32[]{:S(2)}) collective-permute-start(bf16[400,128]{1,0:T(8,128)(2,1)S(1)} %get-tuple-element.49), channel_id=1, source_target_pairs={{0,10},{2,8},{4,14},{6,12},{8,2},{10,0},{12,6},{14,4},{16,26},{18,... | collective-permute-start | bytes 307208 | tf_op jit(solution)/shard_map/ppermute | solution.py:285
  10.1 11.4 %collective-permute-start.14 = (bf16[400,128]{1,0:T(8,128)(2,1)S(1)}, bf16[400,128]{1,0:T(8,128)(2,1)S(1)}, u32[]{:S(2)}, u32[]{:S(2)}) collective-permute-start(bf16[400,128]{1,0:T(8,128)(2,1)S(1)} %get-tuple-element.50), channel_id=1, source_target_pairs={{0,26},{2,24},{4,30},{6,28},{8,18},{10,16},{12,22},{14,20},{16,10}... | collective-permute-start | bytes 307208 | tf_op jit(solution)/shard_map/ppermute | solution.py:285
  12.5 11.6 %collective-permute-start.7 = (bf16[400,128]{1,0:T(8,128)(2,1)S(1)}, bf16[400,128]{1,0:T(8,128)(2,1)S(1)}, u32[]{:S(2)}, u32[]{:S(2)}) collective-permute-start(bf16[400,128]{1,0:T(8,128)(2,1)S(1)} %get-tuple-element.43), channel_id=1, source_target_pairs={{0,12},{2,14},{4,8},{6,10},{8,4},{10,6},{12,0},{14,2},{16,28},{18,... | collective-permute-start | bytes 307208 | tf_op jit(solution)/shard_map/ppermute | solution.py:285
  15.3 11.4 %collective-permute-start.8 = (bf16[400,128]{1,0:T(8,128)(2,1)S(1)}, bf16[400,128]{1,0:T(8,128)(2,1)S(1)}, u32[]{:S(2)}, u32[]{:S(2)}) collective-permute-start(bf16[400,128]{1,0:T(8,128)(2,1)S(1)} %get-tuple-element.44), channel_id=1, source_target_pairs={{0,18},{2,16},{4,22},{6,20},{8,26},{10,24},{12,30},{14,28},{16,2},... | collective-permute-start | bytes 307208 | tf_op jit(solution)/shard_map/ppermute | solution.py:285
  18.0 10.9 %collective-permute-start.9 = (bf16[400,128]{1,0:T(8,128)(2,1)S(1)}, bf16[400,128]{1,0:T(8,128)(2,1)S(1)}, u32[]{:S(2)}, u32[]{:S(2)}) collective-permute-start(bf16[400,128]{1,0:T(8,128)(2,1)S(1)} %get-tuple-element.45), channel_id=1, source_target_pairs={{0,14},{2,12},{4,10},{6,8},{8,6},{10,4},{12,2},{14,0},{16,30},{18,... | collective-permute-start | bytes 307208 | tf_op jit(solution)/shard_map/ppermute | solution.py:285
  20.8 8.8 %collective-permute-start = (bf16[400,128]{1,0:T(8,128)(2,1)S(1)}, bf16[400,128]{1,0:T(8,128)(2,1)S(1)}, u32[]{:S(2)}, u32[]{:S(2)}) collective-permute-start(bf16[400,128]{1,0:T(8,128)(2,1)S(1)} %get-tuple-element.36), channel_id=1, source_target_pairs={{0,28},{2,30},{4,24},{6,26},{8,20},{10,22},{12,16},{14,18},{16,12}... | collective-permute-start | bytes 307208 | tf_op jit(solution)/shard_map/ppermute | solution.py:285
  21.5 10.4 %collective-permute-start.1 = (bf16[400,128]{1,0:T(8,128)(2,1)S(1)}, bf16[400,128]{1,0:T(8,128)(2,1)S(1)}, u32[]{:S(2)}, u32[]{:S(2)}) collective-permute-start(bf16[400,128]{1,0:T(8,128)(2,1)S(1)} %get-tuple-element.37), channel_id=1, source_target_pairs={{0,2},{2,0},{4,6},{6,4},{8,10},{10,8},{12,14},{14,12},{16,18},{18,... | collective-permute-start | bytes 307208 | tf_op jit(solution)/shard_map/ppermute | solution.py:285
  24.1 14.6 %collective-permute-start.2 = (bf16[400,128]{1,0:T(8,128)(2,1)S(1)}, bf16[400,128]{1,0:T(8,128)(2,1)S(1)}, u32[]{:S(2)}, u32[]{:S(2)}) collective-permute-start(bf16[400,128]{1,0:T(8,128)(2,1)S(1)} %get-tuple-element.38), channel_id=1, source_target_pairs={{0,20},{2,22},{4,16},{6,18},{8,28},{10,30},{12,24},{14,26},{16,4},... | collective-permute-start | bytes 307208 | tf_op jit(solution)/shard_map/ppermute | solution.py:285
  26.7 12.7 %collective-permute-start.3 = (bf16[400,128]{1,0:T(8,128)(2,1)S(1)}, bf16[400,128]{1,0:T(8,128)(2,1)S(1)}, u32[]{:S(2)}, u32[]{:S(2)}) collective-permute-start(bf16[400,128]{1,0:T(8,128)(2,1)S(1)} %get-tuple-element.39), channel_id=1, source_target_pairs={{0,4},{2,6},{4,0},{6,2},{8,12},{10,14},{12,8},{14,10},{16,20},{18,... | collective-permute-start | bytes 307208 | tf_op jit(solution)/shard_map/ppermute | solution.py:285
  28.9 10.5 %collective-permute-start.4 = (bf16[400,128]{1,0:T(8,128)(2,1)S(1)}, bf16[400,128]{1,0:T(8,128)(2,1)S(1)}, u32[]{:S(2)}, u32[]{:S(2)}) collective-permute-start(bf16[400,128]{1,0:T(8,128)(2,1)S(1)} %get-tuple-element.40), channel_id=1, source_target_pairs={{0,30},{2,28},{4,26},{6,24},{8,22},{10,20},{12,18},{14,16},{16,14}... | collective-permute-start | bytes 307208 | tf_op jit(solution)/shard_map/ppermute | solution.py:285
  29.6 9.9 %collective-permute-start.5 = (bf16[400,128]{1,0:T(8,128)(2,1)S(1)}, bf16[400,128]{1,0:T(8,128)(2,1)S(1)}, u32[]{:S(2)}, u32[]{:S(2)}) collective-permute-start(bf16[400,128]{1,0:T(8,128)(2,1)S(1)} %get-tuple-element.41), channel_id=1, source_target_pairs={{0,6},{2,4},{4,2},{6,0},{8,14},{10,12},{12,10},{14,8},{16,22},{18,... | collective-permute-start | bytes 307208 | tf_op jit(solution)/shard_map/ppermute | solution.py:285
  32.0 12.3 %collective-permute-start.6 = (bf16[400,128]{1,0:T(8,128)(2,1)S(1)}, bf16[400,128]{1,0:T(8,128)(2,1)S(1)}, u32[]{:S(2)}, u32[]{:S(2)}) collective-permute-start(bf16[400,128]{1,0:T(8,128)(2,1)S(1)} %get-tuple-element.42), channel_id=1, source_target_pairs={{0,22},{2,20},{4,18},{6,16},{8,30},{10,28},{12,26},{14,24},{16,6},... | collective-permute-start | bytes 307208 | tf_op jit(solution)/shard_map/ppermute | solution.py:285
  38.7 5.8 %collective-permute-start.16 = (bf16[512,896]{1,0:T(8,128)(2,1)S(1)}, bf16[512,896]{1,0:T(8,128)(2,1)S(1)}, u32[]{:S(2)}, u32[]{:S(2)}) collective-permute-start(bf16[512,896]{1,0:T(8,128)(2,1)S(1)} %get-tuple-element.51.refs_0_.refs_2_.refs_1_.refs_5_), channel_id=1, source_target_pairs={{0,1},{1,0},{2,3},{3,2},{4,5},{5,4},{6,7},{7,6},{8,9},{9,8},{10,11... | collective-permute-start | bytes 2752520 | tf_op jit(solution)/shard_map/ppermute | solution.py:288
  44.5 2.6 %collective-permute-start.15 = (bf16[512,896]{1,0:T(8,128)(2,1)S(1)}, bf16[512,896]{1,0:T(8,128)(2,1)S(1)}, u32[]{:S(2)}, u32[]{:S(2)}) collective-permute-start(bf16[512,896]{1,0:T(8,128)(2,1)S(1)} %get-tuple-element.53.refs_0_.refs_6_), channel_id=1, source_target_pairs={{0,1},{1,0},{2,3},{3,2},{4,5},{5,4},{6,7},{7,6},{8,9},{9,8},{10,11... | collective-permute-start | bytes 2752520 | tf_op jit(solution)/shard_map/ppermute | solution.py:288
  46.5 1.4 %collective-permute-start.17 = (f32[8,512]{1,0:T(8,128)S(1)}, f32[8,512]{1,0:T(8,128)S(1)}, u32[]{:S(2)}, u32[]{:S(2)}) collective-permute-start(f32[8,512]{1,0:T(8,128)S(1)} %get-tuple-element.57), channel_id=1, source_target_pairs={{0,1},{1,0},{2,3},{3,2},{4,5},{5,4},{6,7},{7,6},{8,9},{9,8},{10,11... | collective-permute-start | bytes 49160 | tf_op jit(solution)/shard_map/ppermute | solution.py:288

commit v7 on v5

--- a/solution.py
+++ b/solution.py
@@ -27,9 +27,8 @@
 
 def partners(nodes):
     half = nodes // 2
-    quarter = half // 2
-    far = [flip for i in range(quarter) for flip in (half + quarter + i, half + i)]
-    near = [*range(quarter, half), *range(1, quarter)]
+    far = [half, nodes - 1, *range(half + half // 2, nodes - 1), *range(half + 1, half + half // 2)]
+    near = [1, *range(half // 2, half), *range(2, half // 2)]
     sequence = [far[0]]
     for pair in zip(near, far[1:]):
         sequence.extend(pair)

time: 58 us -> 58.2 us (level)
  waiting for transfers between devices: 11.7 us -> 4.44 us
  starting transfers between devices: 29.4 us -> 36.4 us
    ppermute x15, waiting for transfers between devices: 11.7 us -> 4.43 us  [body(): lax.ppermute(messages[g], 'ingest', [(i, i ^ flips[g]) for i in range(nod...]
    ppermute x15, starting transfers between devices: 28.7 us -> 35.7 us  [body(): lax.ppermute(messages[g], 'ingest', [(i, i ^ flips[g]) for i in range(nod...]
  transfers between devices with their start and end apart: 18 -> 18, of which waited for: 5 -> 4; matrix products, arithmetic and copies ran while one was open for 0% -> 0% of each run, Pallas kernels for 8% -> 8%
where the time goes in v7:
time: 58.2 us; the launch traced here: 58 us
  starting transfers between devices  36.4 us (63%)
  blocking collectives  9.52 us (16%)
  Pallas kernels  6.56 us (11%)
  waiting for transfers between devices  4.44 us (8%)
  local copies, waits for them, and re-layouts  1 us (2%)
    ppermute x15, starting transfers between devices, body(): lax.ppermute(messages[g], 'ingest', [(i, i ^ flips[g]) for i in range(nod...  35.7 us
    all_to_all x1, blocking collectives, body(): lax.all_to_all(highest, 'ingest', split_axis=0, concat_axis=0, tiled=True...  9.52 us
    ppermute x15, waiting for transfers between devices, body(): lax.ppermute(messages[g], 'ingest', [(i, i ^ flips[g]) for i in range(nod...  4.43 us
    pallas_call x4, Pallas kernels, match(): pl.pallas_call(functools.partial(match_kernel, width=width, queries=len(g...  3.51 us
    pallas_call x2, Pallas kernels, body(): pl.pallas_call(functools.partial(pack_kernel, chosen=chosen, capacity=cap...  1.7 us
  transfers between devices with their start and end apart: 18, of which 4 were waited for; matrix products, arithmetic and copies ran while one was open for 0% of the time, Pallas kernels for 8%

profile of v7, /device:TPU:0, one launch (start us, length us, event | category | flops | bytes accessed | tf_op | source)
XLA Modules:
  0.0 58.0 jit_solution(17967909073573262758)
XLA Ops:
  0.0 0.7 %copy-done.2 = s32[512]{0:T(512)S(1)} copy-done((s32[512]{0:T(512)S(1)}, s32[512]{0:T(512)}, u32[]{:S(2)}) %copy-start.2) | copy-done | bytes 2072
  1.2 0.9 %shard_map.38 = (bf16[400,128]{1,0:T(8,128)(2,1)S(1)}, bf16[400,128]{1,0:T(8,128)(2,1)S(1)}, bf16[400,128]{1,0:T(8,128)(2,1)S(1)}, bf16[400,128]{1,0:T(8,128)(2,...) custom-call(bf16[512,768]{1,0:T(8,128)(2,1)S(1)} %copy-done.1, ...), custom_call_target="tpu_custom_call" | custom-call | flops 469762048 | bytes 4096 | tf_op jit(solution)/shard_map/pallas_call | solution.py:267
  2.1 4.1 %collective-permute-start.10 = (bf16[400,128]{1,0:T(8,128)(2,1)S(1)}, bf16[400,128]{1,0:T(8,128)(2,1)S(1)}, u32[]{:S(2)}, u32[]{:S(2)}) collective-permute-start(bf16[400,128]{1,0:T(8,128)(2,1)S(1)} %get-tuple-element.47), channel_id=1, source_target_pairs={{0,16},{2,18},{4,20},{6,22},{8,24},{10,26},{12,28},{14,30},{16,0},... | collective-permute-start | bytes 307208 | tf_op jit(solution)/shard_map/ppermute | solution.py:284
  6.2 1.5 %collective-permute-start.11 = (bf16[400,128]{1,0:T(8,128)(2,1)S(1)}, bf16[400,128]{1,0:T(8,128)(2,1)S(1)}, u32[]{:S(2)}, u32[]{:S(2)}) collective-permute-start(bf16[400,128]{1,0:T(8,128)(2,1)S(1)} %get-tuple-element.48), channel_id=1, source_target_pairs={{0,2},{2,0},{4,6},{6,4},{8,10},{10,8},{12,14},{14,12},{16,18},{18,... | collective-permute-start | bytes 307208 | tf_op jit(solution)/shard_map/ppermute | solution.py:284
  7.7 2.3 %collective-permute-start.12 = (bf16[400,128]{1,0:T(8,128)(2,1)S(1)}, bf16[400,128]{1,0:T(8,128)(2,1)S(1)}, u32[]{:S(2)}, u32[]{:S(2)}) collective-permute-start(bf16[400,128]{1,0:T(8,128)(2,1)S(1)} %get-tuple-element.49), channel_id=1, source_target_pairs={{0,30},{2,28},{4,26},{6,24},{8,22},{10,20},{12,18},{14,16},{16,14}... | collective-permute-start | bytes 307208 | tf_op jit(solution)/shard_map/ppermute | solution.py:284
  9.9 3.1 %collective-permute-start.14 = (bf16[400,128]{1,0:T(8,128)(2,1)S(1)}, bf16[400,128]{1,0:T(8,128)(2,1)S(1)}, u32[]{:S(2)}, u32[]{:S(2)}) collective-permute-start(bf16[400,128]{1,0:T(8,128)(2,1)S(1)} %get-tuple-element.51), channel_id=1, source_target_pairs={{0,24},{2,26},{4,28},{6,30},{8,16},{10,18},{12,20},{14,22},{16,8},... | collective-permute-start | bytes 307208 | tf_op jit(solution)/shard_map/ppermute | solution.py:284
  13.1 1.4 %collective-permute-start.7 = (bf16[400,128]{1,0:T(8,128)(2,1)S(1)}, bf16[400,128]{1,0:T(8,128)(2,1)S(1)}, u32[]{:S(2)}, u32[]{:S(2)}) collective-permute-start(bf16[400,128]{1,0:T(8,128)(2,1)S(1)} %get-tuple-element.44), channel_id=1, source_target_pairs={{0,10},{2,8},{4,14},{6,12},{8,2},{10,0},{12,6},{14,4},{16,26},{18,... | collective-permute-start | bytes 307208 | tf_op jit(solution)/shard_map/ppermute | solution.py:284
  14.5 0.8 %shard_map.39 = (bf16[400,128]{1,0:T(8,128)(2,1)S(1)}, bf16[400,128]{1,0:T(8,128)(2,1)S(1)}, bf16[400,128]{1,0:T(8,128)(2,1)S(1)}, bf16[400,128]{1,0:T(8,128)(2,...) custom-call(bf16[512,896]{1,0:T(8,128)(2,1)S(1)} %get-tuple-element., ...), custom_call_target="tpu_custom_call" | custom-call | flops 469762048 | bytes 4096 | tf_op jit(solution)/shard_map/pallas_call | solution.py:267
  15.2 4.4 %collective-permute-start.8 = (bf16[400,128]{1,0:T(8,128)(2,1)S(1)}, bf16[400,128]{1,0:T(8,128)(2,1)S(1)}, u32[]{:S(2)}, u32[]{:S(2)}) collective-permute-start(bf16[400,128]{1,0:T(8,128)(2,1)S(1)} %get-tuple-element.45), channel_id=1, source_target_pairs={{0,26},{2,24},{4,30},{6,28},{8,18},{10,16},{12,22},{14,20},{16,10}... | collective-permute-start | bytes 307208 | tf_op jit(solution)/shard_map/ppermute | solution.py:284
  19.6 2.4 %collective-permute-start.9 = (bf16[400,128]{1,0:T(8,128)(2,1)S(1)}, bf16[400,128]{1,0:T(8,128)(2,1)S(1)}, u32[]{:S(2)}, u32[]{:S(2)}) collective-permute-start(bf16[400,128]{1,0:T(8,128)(2,1)S(1)} %get-tuple-element.46), channel_id=1, source_target_pairs={{0,12},{2,14},{4,8},{6,10},{8,4},{10,6},{12,0},{14,2},{16,28},{18,... | collective-permute-start | bytes 307208 | tf_op jit(solution)/shard_map/ppermute | solution.py:284
  22.0 3.8 %collective-permute-start = (bf16[400,128]{1,0:T(8,128)(2,1)S(1)}, bf16[400,128]{1,0:T(8,128)(2,1)S(1)}, u32[]{:S(2)}, u32[]{:S(2)}) collective-permute-start(bf16[400,128]{1,0:T(8,128)(2,1)S(1)} %get-tuple-element.37), channel_id=1, source_target_pairs={{0,28},{2,30},{4,24},{6,26},{8,20},{10,22},{12,16},{14,18},{16,12}... | collective-permute-start | bytes 307208 | tf_op jit(solution)/shard_map/ppermute | solution.py:284
  25.8 2.4 %collective-permute-start.2 = (bf16[400,128]{1,0:T(8,128)(2,1)S(1)}, bf16[400,128]{1,0:T(8,128)(2,1)S(1)}, u32[]{:S(2)}, u32[]{:S(2)}) collective-permute-start(bf16[400,128]{1,0:T(8,128)(2,1)S(1)} %get-tuple-element.39), channel_id=1, source_target_pairs={{0,18},{2,16},{4,22},{6,20},{8,26},{10,24},{12,30},{14,28},{16,2},... | collective-permute-start | bytes 307208 | tf_op jit(solution)/shard_map/ppermute | solution.py:284
  28.2 0.8 %collective-permute-start.3 = (bf16[400,128]{1,0:T(8,128)(2,1)S(1)}, bf16[400,128]{1,0:T(8,128)(2,1)S(1)}, u32[]{:S(2)}, u32[]{:S(2)}) collective-permute-start(bf16[400,128]{1,0:T(8,128)(2,1)S(1)} %get-tuple-element.40), channel_id=1, source_target_pairs={{0,4},{2,6},{4,0},{6,2},{8,12},{10,14},{12,8},{14,10},{16,20},{18,... | collective-permute-start | bytes 307208 | tf_op jit(solution)/shard_map/ppermute | solution.py:284
  29.0 1.6 %collective-permute-start.4 = (bf16[400,128]{1,0:T(8,128)(2,1)S(1)}, bf16[400,128]{1,0:T(8,128)(2,1)S(1)}, u32[]{:S(2)}, u32[]{:S(2)}) collective-permute-start(bf16[400,128]{1,0:T(8,128)(2,1)S(1)} %get-tuple-element.41), channel_id=1, source_target_pairs={{0,20},{2,22},{4,16},{6,18},{8,28},{10,30},{12,24},{14,26},{16,4},... | collective-permute-start | bytes 307208 | tf_op jit(solution)/shard_map/ppermute | solution.py:284
  30.6 1.0 %collective-permute-done.refs_1_ = bf16[400,128]{1,0:T(8,128)(2,1)S(1)} collective-permute-done((bf16[400,128]{1,0:T(8,128)(2,1)S(1)}, bf16[400,128]{1,0:T(8,128)(2,1)S(1)}, u32[]{:S(2)}, u32[]{:S(2)}) %collective-permute-start) | collective-permute-done | bytes 102432 | tf_op jit(solution)/shard_map/ppermute | solution.py:284
  31.6 1.5 %collective-permute-start.5 = (bf16[400,128]{1,0:T(8,128)(2,1)S(1)}, bf16[400,128]{1,0:T(8,128)(2,1)S(1)}, u32[]{:S(2)}, u32[]{:S(2)}) collective-permute-start(bf16[400,128]{1,0:T(8,128)(2,1)S(1)} %get-tuple-element.42), channel_id=1, source_target_pairs={{0,6},{2,4},{4,2},{6,0},{8,14},{10,12},{12,10},{14,8},{16,22},{18,... | collective-permute-start | bytes 307208 | tf_op jit(solution)/shard_map/ppermute | solution.py:284
  33.1 1.6 %collective-permute-done.1.refs_2_ = bf16[400,128]{1,0:T(8,128)(2,1)S(1)} collective-permute-done((bf16[400,128]{1,0:T(8,128)(2,1)S(1)}, bf16[400,128]{1,0:T(8,128)(2,1)S(1)}, u32[]{:S(2)}, u32[]{:S(2)}) %collective-permute-start.1) | collective-permute-done | bytes 102432 | tf_op jit(solution)/shard_map/ppermute | solution.py:284
  34.7 6.5 %collective-permute-start.6 = (bf16[400,128]{1,0:T(8,128)(2,1)S(1)}, bf16[400,128]{1,0:T(8,128)(2,1)S(1)}, u32[]{:S(2)}, u32[]{:S(2)}) collective-permute-start(bf16[400,128]{1,0:T(8,128)(2,1)S(1)} %get-tuple-element.43), channel_id=1, source_target_pairs={{0,22},{2,20},{4,18},{6,16},{8,30},{10,28},{12,26},{14,24},{16,6},... | collective-permute-start | bytes 307208 | tf_op jit(solution)/shard_map/ppermute | solution.py:284
  42.3 1.6 %collective-permute-done.6.refs_7_ = bf16[400,128]{1,0:T(8,128)(2,1)S(1)} collective-permute-done((bf16[400,128]{1,0:T(8,128)(2,1)S(1)}, bf16[400,128]{1,0:T(8,128)(2,1)S(1)}, u32[]{:S(2)}, u32[]{:S(2)}) %collective-permute-start.6) | collective-permute-done | bytes 102432 | tf_op jit(solution)/shard_map/ppermute | solution.py:284
  44.2 0.8 %shard_map.43 = (f32[8,512]{1,0:T(8,128)S(1)}, f32[8,512]{1,0:T(8,128)S(1)}) custom-call(bf16[512,896]{1,0:T(8,128)(2,1)S(1)} %get-tuple-element.54.refs_0_.refs_5_, f32[8,512]{1,0:T(8,128)S(1)} %get-tuple-element.55.refs_1_.refs_2_, bf16[512,896]{1,0:T(8,128)(2,1)S(1)} %collective-permute-done.16.refs_2_.refs_6_), custom_call_target="tpu_custom_call" | custom-call | flops 1 | bytes 1 | tf_op jit(solution)/shard_map/pallas_call | solution.py:199
  45.5 1.5 %shard_map.44 = (f32[8,512]{1,0:T(8,128)S(1)}, f32[8,512]{1,0:T(8,128)S(1)}) custom-call(bf16[512,896]{1,0:T(8,128)(2,1)S(1)} %get-tuple-element.54.refs_0_.refs_5_, bf16[512,896]{1,0:T(8,128)(2,1)S(1)} %get-tuple-element.52.refs_0_.refs_2_.refs_1_.refs_4_, f32[8,512]{1,0:T(8,128)S(1)} %get-tuple-element.55.refs_1_.refs_2_, ...), custom_call_target="tpu_custom_call" | custom-call | flops 1 | bytes 1 | tf_op jit(solution)/shard_map/pallas_call | solution.py:199
  47.1 0.6 %shard_map.45.first_ref = f32[8,512]{1,0:T(8,128)S(1)} custom-call(bf16[512,896]{1,0:T(8,128)(2,1)S(1)} %get-tuple-element.54.refs_0_.refs_5_, f32[8,512]{1,0:T(8,128)S(1)} %get-tuple-element.55.refs_1_.refs_2_, bf16[512,896]{1,0:T(8,128)(2,1)S(1)} %collective-permute-done.15.refs_2_, f32[8,512]{1,0:T(8,128)S(1)} %get-tuple-element.57.refs_3_), custom_call_target="tpu_custom_call" | custom-call | flops 1 | bytes 1 | tf_op jit(solution)/shard_map/pallas_call | solution.py:199
  47.8 9.5 %all_to_all.5.back_ref = f32[16,1,128]{2,1,0:T(1,128)S(1)} all-to-all(f32[16,1,128]{2,1,0:T(1,128)S(1)} %shard_map.46), channel_id=1, replica_groups={{30,28,26,24,22,20,18,16,14,12,10,8,6,4,2,0},{31,29,27,25,23,21,19,17,1..., dimensions={0} | all-to-all | bytes 16384 | tf_op jit(solution)/shard_map/all_to_all | solution.py:312
  57.3 0.7 %shard_map.47 = f32[1,512]{1,0:T(1,128)} custom-call(f32[16,1,128]{2,1,0:T(1,128)S(1)} %all_to_all.5.back_ref, s32[1,512]{1,0:T(1,128)S(1)} %bitcast.5, s32[1,512]{1,0:T(1,128)S(1)} %get-tuple-element.60.pos_ref), custom_call_target="tpu_custom_call" | custom-call | tf_op jit(solution)/shard_map/pallas_call | solution.py:320
  (30 shorter events, 2.5 us)
Async XLA Ops:
  0.0 0.7 %copy-start.2 = (s32[512]{0:T(512)S(1)}, s32[512]{0:T(512)}, u32[]{:S(2)}) copy-start(s32[512]{0:T(512)} %param.5) | copy-start | bytes 6148
  0.0 0.7 %copy-start = (s32[512]{0:T(512)S(1)}, s32[512]{0:T(512)}, u32[]{:S(2)}) copy-start(s32[512]{0:T(512)} %param.4) | copy-start | bytes 6148
  0.0 1.2 %copy-start.1 = (bf16[512,768]{1,0:T(8,128)(2,1)S(1)}, bf16[512,768]{1,0:T(8,128)(2,1)}, u32[]{:S(2)}) copy-start(bf16[512,768]{1,0:T(8,128)(2,1)} %rows_ref.1) | copy-start | bytes 2359300
  2.1 11.0 %collective-permute-start.10 = (bf16[400,128]{1,0:T(8,128)(2,1)S(1)}, bf16[400,128]{1,0:T(8,128)(2,1)S(1)}, u32[]{:S(2)}, u32[]{:S(2)}) collective-permute-start(bf16[400,128]{1,0:T(8,128)(2,1)S(1)} %get-tuple-element.47), channel_id=1, source_target_pairs={{0,16},{2,18},{4,20},{6,22},{8,24},{10,26},{12,28},{14,30},{16,0},... | collective-permute-start | bytes 307208 | tf_op jit(solution)/shard_map/ppermute | solution.py:284
  6.2 9.1 %collective-permute-start.11 = (bf16[400,128]{1,0:T(8,128)(2,1)S(1)}, bf16[400,128]{1,0:T(8,128)(2,1)S(1)}, u32[]{:S(2)}, u32[]{:S(2)}) collective-permute-start(bf16[400,128]{1,0:T(8,128)(2,1)S(1)} %get-tuple-element.48), channel_id=1, source_target_pairs={{0,2},{2,0},{4,6},{6,4},{8,10},{10,8},{12,14},{14,12},{16,18},{18,... | collective-permute-start | bytes 307208 | tf_op jit(solution)/shard_map/ppermute | solution.py:284
  7.7 11.9 %collective-permute-start.12 = (bf16[400,128]{1,0:T(8,128)(2,1)S(1)}, bf16[400,128]{1,0:T(8,128)(2,1)S(1)}, u32[]{:S(2)}, u32[]{:S(2)}) collective-permute-start(bf16[400,128]{1,0:T(8,128)(2,1)S(1)} %get-tuple-element.49), channel_id=1, source_target_pairs={{0,30},{2,28},{4,26},{6,24},{8,22},{10,20},{12,18},{14,16},{16,14}... | collective-permute-start | bytes 307208 | tf_op jit(solution)/shard_map/ppermute | solution.py:284
  9.9 12.1 %collective-permute-start.13 = (bf16[400,128]{1,0:T(8,128)(2,1)S(1)}, bf16[400,128]{1,0:T(8,128)(2,1)S(1)}, u32[]{:S(2)}, u32[]{:S(2)}) collective-permute-start(bf16[400,128]{1,0:T(8,128)(2,1)S(1)} %get-tuple-element.50), channel_id=1, source_target_pairs={{0,8},{2,10},{4,12},{6,14},{8,0},{10,2},{12,4},{14,6},{16,24},{18,... | collective-permute-start | bytes 307208 | tf_op jit(solution)/shard_map/ppermute | solution.py:284
  9.9 15.9 %collective-permute-start.14 = (bf16[400,128]{1,0:T(8,128)(2,1)S(1)}, bf16[400,128]{1,0:T(8,128)(2,1)S(1)}, u32[]{:S(2)}, u32[]{:S(2)}) collective-permute-start(bf16[400,128]{1,0:T(8,128)(2,1)S(1)} %get-tuple-element.51), channel_id=1, source_target_pairs={{0,24},{2,26},{4,28},{6,30},{8,16},{10,18},{12,20},{14,22},{16,8},... | collective-permute-start | bytes 307208 | tf_op jit(solution)/shard_map/ppermute | solution.py:284
  13.1 12.7 %collective-permute-start.7 = (bf16[400,128]{1,0:T(8,128)(2,1)S(1)}, bf16[400,128]{1,0:T(8,128)(2,1)S(1)}, u32[]{:S(2)}, u32[]{:S(2)}) collective-permute-start(bf16[400,128]{1,0:T(8,128)(2,1)S(1)} %get-tuple-element.44), channel_id=1, source_target_pairs={{0,10},{2,8},{4,14},{6,12},{8,2},{10,0},{12,6},{14,4},{16,26},{18,... | collective-permute-start | bytes 307208 | tf_op jit(solution)/shard_map/ppermute | solution.py:284
  15.2 13.0 %collective-permute-start.8 = (bf16[400,128]{1,0:T(8,128)(2,1)S(1)}, bf16[400,128]{1,0:T(8,128)(2,1)S(1)}, u32[]{:S(2)}, u32[]{:S(2)}) collective-permute-start(bf16[400,128]{1,0:T(8,128)(2,1)S(1)} %get-tuple-element.45), channel_id=1, source_target_pairs={{0,26},{2,24},{4,30},{6,28},{8,18},{10,16},{12,22},{14,20},{16,10}... | collective-permute-start | bytes 307208 | tf_op jit(solution)/shard_map/ppermute | solution.py:284
  19.6 9.4 %collective-permute-start.9 = (bf16[400,128]{1,0:T(8,128)(2,1)S(1)}, bf16[400,128]{1,0:T(8,128)(2,1)S(1)}, u32[]{:S(2)}, u32[]{:S(2)}) collective-permute-start(bf16[400,128]{1,0:T(8,128)(2,1)S(1)} %get-tuple-element.46), channel_id=1, source_target_pairs={{0,12},{2,14},{4,8},{6,10},{8,4},{10,6},{12,0},{14,2},{16,28},{18,... | collective-permute-start | bytes 307208 | tf_op jit(solution)/shard_map/ppermute | solution.py:284
  22.0 9.5 %collective-permute-start = (bf16[400,128]{1,0:T(8,128)(2,1)S(1)}, bf16[400,128]{1,0:T(8,128)(2,1)S(1)}, u32[]{:S(2)}, u32[]{:S(2)}) collective-permute-start(bf16[400,128]{1,0:T(8,128)(2,1)S(1)} %get-tuple-element.37), channel_id=1, source_target_pairs={{0,28},{2,30},{4,24},{6,26},{8,20},{10,22},{12,16},{14,18},{16,12}... | collective-permute-start | bytes 307208 | tf_op jit(solution)/shard_map/ppermute | solution.py:284
  25.8 8.9 %collective-permute-start.1 = (bf16[400,128]{1,0:T(8,128)(2,1)S(1)}, bf16[400,128]{1,0:T(8,128)(2,1)S(1)}, u32[]{:S(2)}, u32[]{:S(2)}) collective-permute-start(bf16[400,128]{1,0:T(8,128)(2,1)S(1)} %get-tuple-element.38), channel_id=1, source_target_pairs={{0,14},{2,12},{4,10},{6,8},{8,6},{10,4},{12,2},{14,0},{16,30},{18,... | collective-permute-start | bytes 307208 | tf_op jit(solution)/shard_map/ppermute | solution.py:284
  25.8 15.6 %collective-permute-start.2 = (bf16[400,128]{1,0:T(8,128)(2,1)S(1)}, bf16[400,128]{1,0:T(8,128)(2,1)S(1)}, u32[]{:S(2)}, u32[]{:S(2)}) collective-permute-start(bf16[400,128]{1,0:T(8,128)(2,1)S(1)} %get-tuple-element.39), channel_id=1, source_target_pairs={{0,18},{2,16},{4,22},{6,20},{8,26},{10,24},{12,30},{14,28},{16,2},... | collective-permute-start | bytes 307208 | tf_op jit(solution)/shard_map/ppermute | solution.py:284
  28.2 13.9 %collective-permute-start.3 = (bf16[400,128]{1,0:T(8,128)(2,1)S(1)}, bf16[400,128]{1,0:T(8,128)(2,1)S(1)}, u32[]{:S(2)}, u32[]{:S(2)}) collective-permute-start(bf16[400,128]{1,0:T(8,128)(2,1)S(1)} %get-tuple-element.40), channel_id=1, source_target_pairs={{0,4},{2,6},{4,0},{6,2},{8,12},{10,14},{12,8},{14,10},{16,20},{18,... | collective-permute-start | bytes 307208 | tf_op jit(solution)/shard_map/ppermute | solution.py:284
  29.0 13.3 %collective-permute-start.4 = (bf16[400,128]{1,0:T(8,128)(2,1)S(1)}, bf16[400,128]{1,0:T(8,128)(2,1)S(1)}, u32[]{:S(2)}, u32[]{:S(2)}) collective-permute-start(bf16[400,128]{1,0:T(8,128)(2,1)S(1)} %get-tuple-element.41), channel_id=1, source_target_pairs={{0,20},{2,22},{4,16},{6,18},{8,28},{10,30},{12,24},{14,26},{16,4},... | collective-permute-start | bytes 307208 | tf_op jit(solution)/shard_map/ppermute | solution.py:284
  31.6 10.7 %collective-permute-start.5 = (bf16[400,128]{1,0:T(8,128)(2,1)S(1)}, bf16[400,128]{1,0:T(8,128)(2,1)S(1)}, u32[]{:S(2)}, u32[]{:S(2)}) collective-permute-start(bf16[400,128]{1,0:T(8,128)(2,1)S(1)} %get-tuple-element.42), channel_id=1, source_target_pairs={{0,6},{2,4},{4,2},{6,0},{8,14},{10,12},{12,10},{14,8},{16,22},{18,... | collective-permute-start | bytes 307208 | tf_op jit(solution)/shard_map/ppermute | solution.py:284
  34.7 9.2 %collective-permute-start.6 = (bf16[400,128]{1,0:T(8,128)(2,1)S(1)}, bf16[400,128]{1,0:T(8,128)(2,1)S(1)}, u32[]{:S(2)}, u32[]{:S(2)}) collective-permute-start(bf16[400,128]{1,0:T(8,128)(2,1)S(1)} %get-tuple-element.43), channel_id=1, source_target_pairs={{0,22},{2,20},{4,18},{6,16},{8,30},{10,28},{12,26},{14,24},{16,6},... | collective-permute-start | bytes 307208 | tf_op jit(solution)/shard_map/ppermute | solution.py:284
  41.4 2.8 %collective-permute-start.16 = (bf16[512,896]{1,0:T(8,128)(2,1)S(1)}, bf16[512,896]{1,0:T(8,128)(2,1)S(1)}, u32[]{:S(2)}, u32[]{:S(2)}) collective-permute-start(bf16[512,896]{1,0:T(8,128)(2,1)S(1)} %get-tuple-element.52.refs_0_.refs_2_.refs_1_.refs_4_), channel_id=1, source_target_pairs={{0,1},{1,0},{2,3},{3,2},{4,5},{5,4},{6,7},{7,6},{8,9},{9,8},{10,11... | collective-permute-start | bytes 2752520 | tf_op jit(solution)/shard_map/ppermute | solution.py:287
  44.1 2.9 %collective-permute-start.15 = (bf16[512,896]{1,0:T(8,128)(2,1)S(1)}, bf16[512,896]{1,0:T(8,128)(2,1)S(1)}, u32[]{:S(2)}, u32[]{:S(2)}) collective-permute-start(bf16[512,896]{1,0:T(8,128)(2,1)S(1)} %get-tuple-element.54.refs_0_.refs_5_), channel_id=1, source_target_pairs={{0,1},{1,0},{2,3},{3,2},{4,5},{5,4},{6,7},{7,6},{8,9},{9,8},{10,11... | collective-permute-start | bytes 2752520 | tf_op jit(solution)/shard_map/ppermute | solution.py:287
  45.0 2.7 %collective-permute-start.17 = (f32[8,512]{1,0:T(8,128)S(1)}, f32[8,512]{1,0:T(8,128)S(1)}, u32[]{:S(2)}, u32[]{:S(2)}) collective-permute-start(f32[8,512]{1,0:T(8,128)S(1)} %get-tuple-element.59), channel_id=1, source_target_pairs={{0,1},{1,0},{2,3},{3,2},{4,5},{5,4},{6,7},{7,6},{8,9},{9,8},{10,11... | collective-permute-start | bytes 49160 | tf_op jit(solution)/shard_map/ppermute | solution.py:287
